TPU v7x, 32 devices: a whole 2x2x4 slice. The times are simulated.
32 devices in a mesh: wide: 8 (over y, x, core), narrow: 4 (over z).
Axes of the slice: x: 2, y: 2, z: 4, core: 2. Of those that a mesh axis runs over, the one named last changes fastest.
Arguments:
- tokens: bfloat16 [4, 2048, 2048], P('narrow', 'wide'), may hold values from -6 to 6
- doc_starts: int32 [4, 4], replicated, may hold values from 1 to 2047, as said below
- query_weight: bfloat16 [2048, 2048], P(('wide', 'narrow')), may hold values from -0.125 to 0.125
- key_weight: bfloat16 [2048, 2048], P(('wide', 'narrow')), may hold values from -0.125 to 0.125
- value_weight: bfloat16 [2048, 2048], P(('wide', 'narrow')), may hold values from -0.125 to 0.125
- gate_weight: bfloat16 [2048, 2048], P(('wide', 'narrow')), may hold values from -0.125 to 0.125
- out_weight: bfloat16 [2048, 2048], P(('wide', 'narrow')), may hold values from -0.125 to 0.125
- ffn_value_weight: bfloat16 [2048, 5632], P(('wide', 'narrow')), may hold values from -0.125 to 0.125
- ffn_gate_weight: bfloat16 [2048, 5632], P(('wide', 'narrow')), may hold values from -0.125 to 0.125
- ffn_out_weight: bfloat16 [5632, 2048], P(('wide', 'narrow')), may hold values from -0.078125 to 0.078125
- cotangent: bfloat16 [4, 2048, 2048], P('narrow', 'wide'), may hold values from -6 to 6
Outputs:
- output: bfloat16 [4, 2048, 2048], P('narrow', 'wide')
- input_grad: float32 [4, 2048, 2048], P('narrow', 'wide')
- query_grad: float32 [2048, 2048], P(('wide', 'narrow'))
- key_grad: float32 [2048, 2048], P(('wide', 'narrow'))
- value_grad: float32 [2048, 2048], P(('wide', 'narrow'))
- gate_grad: float32 [2048, 2048], P(('wide', 'narrow'))
- out_grad: float32 [2048, 2048], P(('wide', 'narrow'))
- ffn_value_grad: float32 [2048, 5632], P(('wide', 'narrow'))
- ffn_gate_grad: float32 [2048, 5632], P(('wide', 'narrow'))
- ffn_out_grad: float32 [5632, 2048], P(('wide', 'narrow'))
Inputs may be any that keep to these rules, and one draw needn't show every extreme that they name: Each row of doc_starts is ascending and may repeat entries; position 0 also starts a document; in one sequence, chosen by the seed, the entries lie in the first 256 or the last 256 positions, with 1 and 2047 among them.
All inputs are finite; a program needn't handle non-finite values.
Results may differ from a plain program's by a relative error of at most 0.014.
Values may be sent and summed in bfloat16 or wider, within the bound.
A program may use at most 448 MiB of HBM per device.

v0:
```python
import jax
import jax.numpy as jnp
from jax import lax
from jax.sharding import PartitionSpec as P

HEADS = 16
HEAD = 128
BLOCK = 256
LAYERS = 16
LAYER = 12


EPS = 1e-06
HIGH = lax.Precision.HIGHEST


def entering(value, axis, combine, identity, reverse):
    peers, index = (lax.axis_size(axis), lax.axis_index(axis))
    everything = jax.tree.map(lambda part: lax.all_gather(part, axis), value)
    start = jax.tree.map(
        lambda part, zero: jnp.broadcast_to(jnp.asarray(zero, part.dtype), part.shape),
        value,
        identity,
    )

    def lap(k, before):
        at = peers - 1 - k if reverse else k
        reached = at > index if reverse else at < index
        new = combine(before, jax.tree.map(lambda part: part[at], everything))
        return jax.tree.map(lambda a, b: jnp.where(reached, a, b), new, before)

    return lax.fori_loop(0, peers, lap, start)


def normalize(values):
    scale = lax.rsqrt(jnp.mean(values * values, axis=-1, keepdims=True) + EPS)
    return (values * scale, scale)


def normalize_back(normed, scale, grad):
    return scale * (grad - normed * jnp.mean(grad * normed, axis=-1, keepdims=True))


def silu_slope(values):
    sigma = jax.nn.sigmoid(values)
    return sigma * (1.0 + values * (1.0 - sigma))


def matmul(left, right):
    return jnp.dot(left, right, preferred_element_type=jnp.float32)


def matmul_right_t(left, right):
    return lax.dot_general(
        left, right, (((1,), (1,)), ((), ())), preferred_element_type=jnp.float32
    )


def weight_grad(left, right):
    return lax.dot_general(
        left, right, (((0,), (0,)), ((), ())), preferred_element_type=jnp.float32
    )


def head_slopes():
    order = jnp.arange(HEADS, dtype=jnp.float32)
    return jnp.exp2(-8.0 * (order + 1.0) / HEADS) * (1.0 - LAYER / (LAYERS - 1) + 1e-05)


def combine_states(earlier, later):
    return (earlier[0] * later[0], later[0][..., None, None] * earlier[1] + later[1])


def local(
    tokens,
    doc_starts,
    query_weight,
    key_weight,
    value_weight,
    gate_weight,
    out_weight,
    ffn_value_weight,
    ffn_gate_weight,
    ffn_out_weight,
    cotangent,
):
    tok_rows = tokens.shape[1]
    blocks = tok_rows // BLOCK
    wide_place = lax.axis_index("wide")
    heads_here = HEADS
    starts = lax.dynamic_slice_in_dim(doc_starts, lax.axis_index("narrow"), 1, 0)
    w_query, w_key, w_value, w_gate, w_out, w_fval, w_fgate, w_fout = (
        lax.all_gather(query_weight, ("wide", "narrow"), axis=0, tiled=True),
        lax.all_gather(key_weight, ("wide", "narrow"), axis=0, tiled=True),
        lax.all_gather(value_weight, ("wide", "narrow"), axis=0, tiled=True),
        lax.all_gather(gate_weight, ("wide", "narrow"), axis=0, tiled=True),
        lax.all_gather(out_weight, ("wide", "narrow"), axis=0, tiled=True),
        lax.all_gather(ffn_value_weight, ("wide", "narrow"), axis=0, tiled=True),
        lax.all_gather(ffn_gate_weight, ("wide", "narrow"), axis=0, tiled=True),
        lax.all_gather(ffn_out_weight, ("wide", "narrow"), axis=0, tiled=True),
    )
    seq_count = starts.shape[0]
    first_row = wide_place * tok_rows
    positions = first_row + jnp.arange(tok_rows, dtype=jnp.int32)
    doc_ids = jnp.sum(
        (starts[:, None, :] <= positions[None, :, None]).astype(jnp.int32), axis=2
    ).reshape(seq_count, blocks, BLOCK)
    firsts = first_row + jnp.arange(blocks, dtype=jnp.int32) * BLOCK - 1
    prev_ids = jnp.sum((starts[:, None, :] <= firsts[None, :, None]).astype(jnp.int32), axis=2)
    slopes = head_slopes()
    offsets = jnp.arange(BLOCK, dtype=jnp.float32)
    lags = offsets[:, None] - offsets[None, :]
    decays = jnp.exp(-slopes[:, None, None] * jnp.maximum(lags, 0.0)[None])
    within = (doc_ids[..., :, None] == doc_ids[..., None, :]) & (lags >= 0.0)
    block_mask = jnp.where(within[:, :, None], decays[None, None], 0.0)
    continues = (doc_ids == prev_ids[:, :, None]).astype(jnp.float32)
    entry_scale = continues[..., None] * jnp.exp(-slopes[None, :] * (offsets[:, None] + 1.0))
    tail_scale = (doc_ids == doc_ids[:, :, -1:]).astype(jnp.float32)[..., None] * jnp.exp(
        -slopes[None, :] * (BLOCK - 1.0 - offsets)[:, None]
    )
    passing = continues[:, :, -1:] * jnp.exp(-slopes * BLOCK)
    dev_factor = jnp.prod(passing, axis=1)

    def split_heads(values):
        return values.reshape(seq_count, blocks, BLOCK, heads_here, HEAD)

    inputs = tokens[0].astype(jnp.float32)
    normed, in_scale = normalize(inputs)
    normed_bf = normed.astype(jnp.bfloat16)
    query_pre = matmul(normed_bf, w_query)
    key_pre = matmul(normed_bf, w_key)
    queries = split_heads(jax.nn.silu(query_pre).astype(jnp.bfloat16))
    keys_bf = split_heads(jax.nn.silu(key_pre).astype(jnp.bfloat16))
    values_bf = split_heads(matmul(normed_bf, w_value).astype(jnp.bfloat16))
    gate_cols = matmul(normed_bf, w_gate)
    query_f = queries.astype(jnp.float32)
    key_f = keys_bf.astype(jnp.float32)
    value_f = values_bf.astype(jnp.float32)
    scores = jnp.einsum("sbihe,sbjhe->sbhij", queries, keys_bf, preferred_element_type=jnp.float32)
    block_probs = (scores * block_mask).astype(jnp.bfloat16)
    inner_part = jnp.einsum(
        "sbhij,sbjhe->sbihe", block_probs, values_bf, preferred_element_type=jnp.float32
    )
    local_state = jnp.einsum(
        "sbjhe,sbjhf->sbhef", key_f * tail_scale[..., None], value_f, precision=HIGH
    )

    def advance(carry, item):
        state, factor = carry
        pass_b, local_b = item
        return ((pass_b[..., None, None] * state + local_b, pass_b * factor), (state, factor))

    zero_state = jnp.zeros((seq_count, heads_here, HEAD, HEAD), jnp.float32)
    ones_heads = jnp.ones((seq_count, heads_here), jnp.float32)
    (dev_state, unused_f), (zero_in, reach) = lax.scan(
        advance,
        (zero_state, ones_heads),
        (jnp.swapaxes(passing, 0, 1), jnp.swapaxes(local_state, 0, 1)),
    )
    zero_in = jnp.swapaxes(zero_in, 0, 1)
    reach = jnp.swapaxes(reach, 0, 1)
    incoming = entering(
        (dev_factor, dev_state), "wide", combine_states, (ones_heads, zero_state), False
    )[1]
    block_in = zero_in + reach[..., None, None] * incoming[:, None]
    across = entry_scale[..., None] * jnp.einsum(
        "sbihe,sbhef->sbihf", query_f, block_in, precision=HIGH
    )
    attention = (inner_part + across).reshape(query_pre.shape)
    stacked = jnp.stack([attention, gate_cols])
    attn_tok = stacked[0]
    gate_tok = stacked[1]
    attn_n, attn_scale = normalize(attn_tok)
    mixed_tok = (attn_n * gate_tok).astype(jnp.bfloat16)
    middle = inputs + matmul(mixed_tok, w_out)[None][0]
    middle_n, middle_scale = normalize(middle)
    middle_bf = middle_n.astype(jnp.bfloat16)
    ffn_val = matmul(middle_bf, w_fval)
    ffn_gat = matmul(middle_bf, w_fgate)
    ffn_mix = (ffn_val * ffn_gat).astype(jnp.bfloat16)
    result = middle + matmul(ffn_mix, w_fout)[None][0]
    upstream = cotangent[0]
    up_cols = upstream[None][0]
    grad_fout = weight_grad(ffn_mix, up_cols)
    d_mix = matmul_right_t(up_cols, w_fout)
    d_val = (d_mix * ffn_gat).astype(jnp.bfloat16)
    d_gat = (d_mix * ffn_val).astype(jnp.bfloat16)
    grad_fval = weight_grad(middle_bf, d_val)
    grad_fgate = weight_grad(middle_bf, d_gat)
    d_middle_n = matmul_right_t(d_val, w_fval) + matmul_right_t(d_gat, w_fgate)
    d_middle = upstream.astype(jnp.float32) + normalize_back(middle_n, middle_scale, d_middle_n)
    d_branch = d_middle.astype(jnp.bfloat16)
    branch_cols = d_branch[None][0]
    grad_out = weight_grad(mixed_tok, branch_cols)
    d_mixed = matmul_right_t(branch_cols, w_out)
    d_gate_tok = (d_mixed * attn_n).astype(jnp.bfloat16)
    d_attn_tok = normalize_back(attn_n, attn_scale, d_mixed * gate_tok).astype(jnp.bfloat16)
    moved = jnp.stack([d_attn_tok, d_gate_tok])
    d_attn = moved[0]
    d_gate = moved[1]
    d_heads = split_heads(d_attn)
    d_heads_f = d_heads.astype(jnp.float32)
    d_probs = jnp.einsum(
        "sbihe,sbjhe->sbhij", d_heads, values_bf, preferred_element_type=jnp.float32
    )
    d_scores = (d_probs * block_mask).astype(jnp.bfloat16)
    d_query = jnp.einsum(
        "sbhij,sbjhe->sbihe", d_scores, keys_bf, preferred_element_type=jnp.float32
    )
    d_key = jnp.einsum("sbhij,sbihe->sbjhe", d_scores, queries, preferred_element_type=jnp.float32)
    d_value = jnp.einsum(
        "sbhij,sbihe->sbjhe", block_probs, d_heads, preferred_element_type=jnp.float32
    )
    d_query = d_query + entry_scale[..., None] * jnp.einsum(
        "sbihf,sbhef->sbihe", d_heads_f, block_in, precision=HIGH
    )
    grad_in = jnp.einsum(
        "sbihe,sbihf->sbhef", query_f * entry_scale[..., None], d_heads_f, precision=HIGH
    )

    def retreat(carry, item):
        state, factor = carry
        pass_b, grad_b = item
        return ((grad_b + pass_b[..., None, None] * state, pass_b * factor), (state, factor))

    (dev_grad, unused_g), (later_zero, after) = lax.scan(
        retreat,
        (zero_state, ones_heads),
        (jnp.swapaxes(passing, 0, 1), jnp.swapaxes(grad_in, 0, 1)),
        reverse=True,
    )
    later_zero = jnp.swapaxes(later_zero, 0, 1)
    after = jnp.swapaxes(after, 0, 1)
    outgoing = entering(
        (dev_factor, dev_grad), "wide", combine_states, (ones_heads, zero_state), True
    )[1]
    block_out = later_zero + after[..., None, None] * outgoing[:, None]
    d_key = d_key + tail_scale[..., None] * jnp.einsum(
        "sbjhf,sbhef->sbjhe", value_f, block_out, precision=HIGH
    )
    d_value = d_value + jnp.einsum(
        "sbjhe,sbhef->sbjhf", key_f * tail_scale[..., None], block_out, precision=HIGH
    )
    dq_pre = (d_query.reshape(query_pre.shape) * silu_slope(query_pre)).astype(jnp.bfloat16)
    dk_pre = (d_key.reshape(key_pre.shape) * silu_slope(key_pre)).astype(jnp.bfloat16)
    dv_pre = d_value.reshape(query_pre.shape).astype(jnp.bfloat16)
    grad_query = weight_grad(normed_bf, dq_pre)
    grad_key = weight_grad(normed_bf, dk_pre)
    grad_value = weight_grad(normed_bf, dv_pre)
    grad_gate = weight_grad(normed_bf, d_gate)
    d_normed = (
        matmul_right_t(dq_pre, w_query)
        + matmul_right_t(dk_pre, w_key)
        + matmul_right_t(dv_pre, w_value)
        + matmul_right_t(d_gate, w_gate)
    )
    d_inputs = d_middle + normalize_back(normed, in_scale, d_normed)
    sums = (
        lax.psum_scatter(grad_query, ("wide", "narrow"), scatter_dimension=0, tiled=True),
        lax.psum_scatter(grad_key, ("wide", "narrow"), scatter_dimension=0, tiled=True),
        lax.psum_scatter(grad_value, ("wide", "narrow"), scatter_dimension=0, tiled=True),
        lax.psum_scatter(grad_gate, ("wide", "narrow"), scatter_dimension=0, tiled=True),
        lax.psum_scatter(grad_out, ("wide", "narrow"), scatter_dimension=0, tiled=True),
        lax.psum_scatter(grad_fval, ("wide", "narrow"), scatter_dimension=0, tiled=True),
        lax.psum_scatter(grad_fgate, ("wide", "narrow"), scatter_dimension=0, tiled=True),
        lax.psum_scatter(grad_fout, ("wide", "narrow"), scatter_dimension=0, tiled=True),
    )
    return (
        result.astype(jnp.bfloat16)[None],
        d_inputs[None],
        sums[0],
        sums[1],
        sums[2],
        sums[3],
        sums[4],
        sums[5],
        sums[6],
        sums[7],
    )


def solution(mesh):
    in_specs = (
        P("narrow", "wide", None),
        P(),
        P(("wide", "narrow"), None),
        P(("wide", "narrow"), None),
        P(("wide", "narrow"), None),
        P(("wide", "narrow"), None),
        P(("wide", "narrow"), None),
        P(("wide", "narrow"), None),
        P(("wide", "narrow"), None),
        P(("wide", "narrow"), None),
        P("narrow", "wide", None),
    )
    out_specs = (
        P("narrow", "wide", None),
        P("narrow", "wide", None),
        P(("wide", "narrow"), None),
        P(("wide", "narrow"), None),
        P(("wide", "narrow"), None),
        P(("wide", "narrow"), None),
        P(("wide", "narrow"), None),
        P(("wide", "narrow"), None),
        P(("wide", "narrow"), None),
        P(("wide", "narrow"), None),
    )
    return jax.shard_map(local, mesh=mesh, in_specs=in_specs, out_specs=out_specs, check_vma=False)
```

profile of v0, /device:TPU:0, one launch (start us, length us, event | category | flops | bytes accessed | tf_op | source)
XLA Modules:
  0.0 5774.8 jit_solution(9295305490185162897)
XLA Ops:
  15.7 75.3 %all-gather.17.cloned.1.call-done = bf16[2048,2048]{1,0:T(8,128)(2,1)} async-done(((bf16[64,2048]{1,0:T(8,128)(2,1)}), bf16[2048,2048]{1,0:T(8,128)(2,1)}) %all-gather.17.cloned.1.call-update) | async-done | bytes 8388624 | tf_op jit(solution)/shard_map/all_gather | solution.py:94
  91.1 6.1 fusion.81
  99.1 70.9 %all-gather.13.cloned.1.call-done = bf16[2048,2048]{1,0:T(8,128)(2,1)} async-done(((bf16[64,2048]{1,0:T(8,128)(2,1)}), bf16[2048,2048]{1,0:T(8,128)(2,1)}) %all-gather.13.cloned.1.call-update) | async-done | bytes 8388624 | tf_op jit(solution)/shard_map/all_gather | solution.py:95
  170.0 5.8 fusion.29
  176.8 3.5 fusion.25
  183.8 8.7 all_gather.45
  192.6 56.3 all-gather.15.cloned.1.call-done
  249.0 7.6 multiply_convert_fusion.11
  265.0 39.3 all-gather.29.cloned.1.call-done
  304.3 12.0 while.20
  316.3 4.2 multiply_reduce_fusion.3
  323.5 61.0 %all-gather.19.cloned.1.call-done = bf16[2048,2048]{1,0:T(8,128)(2,1)} async-done(((bf16[64,2048]{1,0:T(8,128)(2,1)}), bf16[2048,2048]{1,0:T(8,128)(2,1)}) %all-gather.19.cloned.1.call-update) | async-done | bytes 8388624 | tf_op jit(solution)/shard_map/all_gather | solution.py:96
  384.5 8.0 multiply_convert_fusion.9
  392.5 70.8 %all-gather.21.cloned.1.call-done = bf16[2048,2048]{1,0:T(8,128)(2,1)} async-done(((bf16[64,2048]{1,0:T(8,128)(2,1)}), bf16[2048,2048]{1,0:T(8,128)(2,1)}) %all-gather.21.cloned.1.call-update) | async-done | bytes 8388624 | tf_op jit(solution)/shard_map/all_gather | solution.py:97
  463.3 6.2 multiply_reduce_fusion.2
  471.9 137.4 %all-gather.23.cloned.1.call-done = bf16[2048,5632]{1,0:T(8,128)(2,1)} async-done(((bf16[64,5632]{1,0:T(8,128)(2,1)}), bf16[2048,5632]{1,0:T(8,128)(2,1)}) %all-gather.23.cloned.1.call-update) | async-done | bytes 23068688 | tf_op jit(solution)/shard_map/all_gather | solution.py:98
  609.4 12.6 fusion.86
  621.9 133.1 %all-gather.25.cloned.1.call-done = bf16[2048,5632]{1,0:T(8,128)(2,1)} async-done(((bf16[64,5632]{1,0:T(8,128)(2,1)}), bf16[2048,5632]{1,0:T(8,128)(2,1)}) %all-gather.25.cloned.1.call-update) | async-done | bytes 23068688 | tf_op jit(solution)/shard_map/all_gather | solution.py:99
  755.0 12.8 fusion.87
  767.9 132.8 %all-gather.27.cloned.1.call-done = bf16[5632,2048]{1,0:T(8,128)(2,1)} async-done(((bf16[176,2048]{1,0:T(8,128)(2,1)}), bf16[5632,2048]{1,0:T(8,128)(2,1)}) %all-gather.27.cloned.1.call-update) | async-done | bytes 23068688 | tf_op jit(solution)/shard_map/all_gather | solution.py:100
  900.7 17.5 multiply_convert_fusion
  918.2 12.5 fusion.88
  930.7 14.2 multiply_reduce_fusion.1
  948.7 7.2 multiply_reduce_fusion
  959.6 3.4 fusion.26
  975.9 8.3 fusion.77
  985.4 9.4 fusion.73
  996.4 9.4 fusion.64
  1010.5 5.3 all-gather.31.cloned.1.call-done
  1015.8 12.2 while.21
  1028.0 4.0 fusion.17
  1038.9 8.3 fusion.75
  1047.5 3.9 fusion.23
  1053.0 8.4 fusion.31
  1062.6 19.9 fusion.91
  1082.5 19.9 fusion.92
  1103.6 19.9 fusion.45
  1124.8 7.3 fusion.89
  1132.0 12.6 fusion.9
  1147.2 6.1 convolution_add_fusion.3
  1157.8 225.8 %reduce-scatter.9.cloned.1.call-done = f32[64,2048]{1,0:T(8,128)} async-done(((f32[2048,2048]{1,0:T(8,128)}), f32[64,2048]{1,0:T(8,128)}) %reduce-scatter.9.cloned.1.call-update) | async-done | bytes 524304 | tf_op jit(solution)/shard_map/reduce_scatter | solution.py:259
  1383.6 364.9 %reduce-scatter.15.cloned.1.call-done = f32[64,2048]{1,0:T(8,128)} async-done(((f32[2048,2048]{1,0:T(8,128)}), f32[64,2048]{1,0:T(8,128)}) %reduce-scatter.15.cloned.1.call-update) | async-done | bytes 524304 | tf_op jit(solution)/shard_map/reduce_scatter | solution.py:262
  1748.5 365.0 %reduce-scatter.17.cloned.1.call-done = f32[64,2048]{1,0:T(8,128)} async-done(((f32[2048,2048]{1,0:T(8,128)}), f32[64,2048]{1,0:T(8,128)}) %reduce-scatter.17.cloned.1.call-update) | async-done | bytes 524304 | tf_op jit(solution)/shard_map/reduce_scatter | solution.py:263
  2113.5 364.9 %reduce-scatter.11.cloned.1.call-done = f32[64,2048]{1,0:T(8,128)} async-done(((f32[2048,2048]{1,0:T(8,128)}), f32[64,2048]{1,0:T(8,128)}) %reduce-scatter.11.cloned.1.call-update) | async-done | bytes 524304 | tf_op jit(solution)/shard_map/reduce_scatter | solution.py:260
  2478.4 364.9 %reduce-scatter.13.cloned.1.call-done = f32[64,2048]{1,0:T(8,128)} async-done(((f32[2048,2048]{1,0:T(8,128)}), f32[64,2048]{1,0:T(8,128)}) %reduce-scatter.13.cloned.1.call-update) | async-done | bytes 524304 | tf_op jit(solution)/shard_map/reduce_scatter | solution.py:261
  2843.3 973.1 %reduce-scatter.19.cloned.1.call-done = f32[64,5632]{1,0:T(8,128)} async-done(((f32[2048,5632]{1,0:T(8,128)}), f32[64,5632]{1,0:T(8,128)}) %reduce-scatter.19.cloned.1.call-update) | async-done | bytes 1441808 | tf_op jit(solution)/shard_map/reduce_scatter | solution.py:264
  3816.4 975.5 %reduce-scatter.21.cloned.1.call-done = f32[64,5632]{1,0:T(8,128)} async-done(((f32[2048,5632]{1,0:T(8,128)}), f32[64,5632]{1,0:T(8,128)}) %reduce-scatter.21.cloned.1.call-update) | async-done | bytes 1441808 | tf_op jit(solution)/shard_map/reduce_scatter | solution.py:265
  4791.9 975.5 %reduce-scatter.23.cloned.1.call-done = f32[176,2048]{1,0:T(8,128)} async-done(((f32[5632,2048]{1,0:T(8,128)}), f32[176,2048]{1,0:T(8,128)}) %reduce-scatter.23.cloned.1.call-update) | async-done | bytes 1441808 | tf_op jit(solution)/shard_map/reduce_scatter | solution.py:266
  (190 shorter events, 98.1 us)
Async XLA Ops:
  7.2 83.9 %all-gather.17.cloned.1.call-start = ((), (), s32[]{:S(2)}) async-start(), calls=%async_computation.10 | async-start | bytes 8650752 | tf_op jit(solution)/shard_map/all_gather | solution.py:94
  7.9 162.1 %all-gather.13.cloned.1.call-start = ((), (), s32[]{:S(2)}) async-start(), calls=%async_computation.8 | async-start | bytes 8650752 | tf_op jit(solution)/shard_map/all_gather | solution.py:95
  8.7 240.3 %all-gather.15.cloned.1.call-start = ((), (), s32[]{:S(2)}) async-start(), calls=%async_computation.9 | async-start | bytes 8650752 | tf_op jit(solution)/shard_map/all_gather | solution.py:93
  9.4 294.9 %all-gather.29.cloned.1.call-start = ((), (), s32[]{:S(2)}) async-start(), calls=%async_computation.24 | async-start | bytes 9437184 | tf_op jit(solution)/shard_map/all_gather | solution.py:19
  15.7 160.1 %copy-start.32 = (f32[256,16]{0,1:T(8,128)}, f32[256,16]{0,1:T(8,128)S(1)}, u32[]{:S(2)}) copy-start(f32[256,16]{0,1:T(8,128)S(1)} %get-tuple-element.377) | copy-start | bytes 49156
  97.2 1.4 copy-start.16
  98.5 71.5 %copy-start = (bf16[1,256,2048]{2,1,0:T(8,128)(2,1)S(1)}, bf16[1,256,2048]{2,1,0:T(8,128)(2,1)}, u32[]{:S(2)}) copy-start(bf16[1,256,2048]{2,1,0:T(8,128)(2,1)} %param.15) | copy-start | bytes 3145732
  99.1 76.7 %copy-start.12 = (bf16[32,16,8,128]{3,2,1,0:T(8,128)(2,1)}, bf16[32,16,8,128]{3,2,1,0:T(8,128)(2,1)S(1)}, u32[]{:S(2)}) copy-start(bf16[32,16,8,128]{3,2,1,0:T(8,128)(2,1)S(1)} %fusion.55) | copy-start | bytes 3145732
  180.3 204.2 %all-gather.19.cloned.1.call-start = ((), (), s32[]{:S(2)}) async-start(), calls=%async_computation.11 | async-start | bytes 8650752 | tf_op jit(solution)/shard_map/all_gather | solution.py:96
  180.9 282.4 %all-gather.21.cloned.1.call-start = ((), (), s32[]{:S(2)}) async-start(), calls=%async_computation.12 | async-start | bytes 8650752 | tf_op jit(solution)/shard_map/all_gather | solution.py:97
  181.4 427.9 %all-gather.23.cloned.1.call-start = ((), (), s32[]{:S(2)}) async-start(), calls=%async_computation.13 | async-start | bytes 23789568 | tf_op jit(solution)/shard_map/all_gather | solution.py:98
  182.2 572.8 %all-gather.25.cloned.1.call-start = ((), (), s32[]{:S(2)}) async-start(), calls=%async_computation.14 | async-start | bytes 23789568 | tf_op jit(solution)/shard_map/all_gather | solution.py:99
  182.9 717.7 %all-gather.27.cloned.1.call-start = ((), (), s32[]{:S(2)}) async-start(), calls=%async_computation.15 | async-start | bytes 23789568 | tf_op jit(solution)/shard_map/all_gather | solution.py:100
  183.7 832.1 %all-gather.31.cloned.1.call-start = ((), (), s32[]{:S(2)}) async-start(), calls=%async_computation.25 | async-start | bytes 9437184 | tf_op jit(solution)/shard_map/all_gather | solution.py:19
  258.2 701.4 %copy-start.5 = (bf16[256,2048]{0,1:T(8,128)(2,1)}, bf16[256,2048]{0,1:T(8,128)(2,1)S(1)}, u32[]{:S(2)}) copy-start(bf16[256,2048]{0,1:T(8,128)(2,1)S(1)} %copy.95) | copy-start | bytes 3145732
  258.3 4.5 copy-start.27
  261.3 1.5 copy-start.14
  469.5 1.3 copy-start.18
  944.9 3.2 copy-start.4
  944.9 3.8 copy-start.31
  948.1 7.9 copy-start.1
  963.1 2.9 copy-start.13
  963.1 420.5 %reduce-scatter.9.cloned.1.call-start = ((), (), s32[]{:S(2)}) async-start(), calls=%async_computation.16 | async-start | bytes 17301504 | tf_op jit(solution)/shard_map/reduce_scatter | solution.py:259
  966.0 1.4 copy-start.17
  966.0 2.0 copy-start.7
  984.2 764.3 %reduce-scatter.15.cloned.1.call-start = ((), (), s32[]{:S(2)}) async-start(), calls=%async_computation.19 | async-start | bytes 17301504 | tf_op jit(solution)/shard_map/reduce_scatter | solution.py:262
  994.8 1.6 copy-start.2
  994.8 1118.7 %reduce-scatter.17.cloned.1.call-start = ((), (), s32[]{:S(2)}) async-start(), calls=%async_computation.20 | async-start | bytes 17301504 | tf_op jit(solution)/shard_map/reduce_scatter | solution.py:263
  1005.9 1472.6 %reduce-scatter.11.cloned.1.call-start = ((), (), s32[]{:S(2)}) async-start(), calls=%async_computation.17 | async-start | bytes 17301504 | tf_op jit(solution)/shard_map/reduce_scatter | solution.py:260
  1015.8 12.2 copy-start.28
  1015.8 12.2 copy-start.33
  1047.2 4.2 copy-start.8
  1047.2 1796.1 %reduce-scatter.13.cloned.1.call-start = ((), (), s32[]{:S(2)}) async-start(), calls=%async_computation.18 | async-start | bytes 17301504 | tf_op jit(solution)/shard_map/reduce_scatter | solution.py:261
  1047.5 4.0 copy-start.15
  1061.4 2755.0 %reduce-scatter.19.cloned.1.call-start = ((), (), s32[]{:S(2)}) async-start(), calls=%async_computation.21 | async-start | bytes 47579136 | tf_op jit(solution)/shard_map/reduce_scatter | solution.py:264
  1082.5 3709.5 %reduce-scatter.21.cloned.1.call-start = ((), (), s32[]{:S(2)}) async-start(), calls=%async_computation.22 | async-start | bytes 47579136 | tf_op jit(solution)/shard_map/reduce_scatter | solution.py:265
  1102.4 4665.1 %reduce-scatter.23.cloned.1.call-start = ((), (), s32[]{:S(2)}) async-start(), calls=%async_computation.23 | async-start | bytes 47579136 | tf_op jit(solution)/shard_map/reduce_scatter | solution.py:266
  1124.7 7.3 copy-start.10
  1124.8 7.3 copy-start.19
  1124.8 19.9 slice-start
  1132.0 12.7 copy-start.25
  1132.0 12.7 slice-start.1
  1132.0 12.7 copy-start.34
  1144.7 2.4 copy-start.30
  1144.7 8.5 slice-start.2
  1147.2 6.1 copy-start.21
  1147.2 6.1 slice-start.3
  1153.3 2.7 copy-start.3
  (9 other events, 10.1 us)
Sparse Core Ops, SparseCore 0:
  10.9 80.0 all-gather.16
  94.0 75.9 all-gather.12
  172.9 75.9 all-gather.14
  251.3 52.9 all-gather.28
  307.1 77.3 all-gather.18
  387.3 75.9 all-gather.20
  466.1 143.1 all-gather.22
  612.2 142.7 all-gather.24
  757.9 142.7 all-gather.26
  963.2 52.5 all-gather.30
  1018.6 364.9 reduce-scatter.8
  1386.3 362.1 reduce-scatter.14
  1751.4 362.1 reduce-scatter.16
  2116.3 362.1 reduce-scatter.10
  2481.2 362.1 reduce-scatter.12
  2846.1 970.2 reduce-scatter.18
  3819.1 972.7 reduce-scatter.20
  4794.7 972.7 reduce-scatter.22
where the time goes:
time: 5780 us; the launch traced here: 5770 us
  waiting for transfers between devices  5400 us (93%)
  matrix products  279 us (5%)
    reduce_scatter x1, waiting for transfers between devices, local(): lax.psum_scatter(grad_fout, ('wide', 'narrow'), scatter_dimension=0, tile...  976 us
    reduce_scatter x1, waiting for transfers between devices, local(): lax.psum_scatter(grad_fgate, ('wide', 'narrow'), scatter_dimension=0, til...  976 us
    reduce_scatter x1, waiting for transfers between devices, local(): lax.psum_scatter(grad_fval, ('wide', 'narrow'), scatter_dimension=0, tile...  973 us
    reduce_scatter x1, waiting for transfers between devices, local(): lax.psum_scatter(grad_out, ('wide', 'narrow'), scatter_dimension=0, tiled...  365 us
    reduce_scatter x1, waiting for transfers between devices, local(): lax.psum_scatter(grad_key, ('wide', 'narrow'), scatter_dimension=0, tiled...  365 us
    reduce_scatter x1, waiting for transfers between devices, local(): lax.psum_scatter(grad_gate, ('wide', 'narrow'), scatter_dimension=0, tile...  365 us
    reduce_scatter x1, waiting for transfers between devices, local(): lax.psum_scatter(grad_value, ('wide', 'narrow'), scatter_dimension=0, til...  365 us
    reduce_scatter x1, waiting for transfers between devices, local(): lax.psum_scatter(grad_query, ('wide', 'narrow'), scatter_dimension=0, til...  226 us
  transfers between devices with their start and end apart: 18, of which 18 were waited for; matrix products, arithmetic and copies ran while one was open for 5% of the time, Pallas kernels for 0%

commit v1 on v0

v1 whole, which is shorter than its diff:
```python
import jax
import jax.numpy as jnp
from jax import lax
from jax.sharding import PartitionSpec as P

HEADS = 16
HEAD = 128
BLOCK = 256
LAYERS = 16
LAYER = 12

EPS = 1e-06
BOTH = ("wide", "narrow")
BF = jnp.bfloat16
F32 = jnp.float32


def normalize(values):
    scale = lax.rsqrt(jnp.mean(values * values, axis=-1, keepdims=True) + EPS)
    return (values * scale, scale)


def normalize_back(normed, scale, grad):
    return scale * (grad - normed * jnp.mean(grad * normed, axis=-1, keepdims=True))


def silu_slope(values):
    sigma = jax.nn.sigmoid(values)
    return sigma * (1.0 + values * (1.0 - sigma))


def matmul(left, right):
    return jnp.dot(left, right, preferred_element_type=F32)


def matmul_right_t(left, right):
    return lax.dot_general(left, right, (((1,), (1,)), ((), ())), preferred_element_type=F32)


def weight_grad(left, right):
    return lax.dot_general(left, right, (((0,), (0,)), ((), ())), preferred_element_type=F32)


def ein(spec, left, right):
    return jnp.einsum(spec, left, right, preferred_element_type=F32)


def head_slopes():
    order = jnp.arange(HEADS, dtype=F32)
    return jnp.exp2(-8.0 * (order + 1.0) / HEADS) * (1.0 - LAYER / (LAYERS - 1) + 1e-05)


def local(
    tokens,
    doc_starts,
    query_weight,
    key_weight,
    value_weight,
    gate_weight,
    out_weight,
    ffn_value_weight,
    ffn_gate_weight,
    ffn_out_weight,
    cotangent,
):
    wide, narrow = lax.axis_size("wide"), lax.axis_size("narrow")
    rows_here, width = tokens.shape[1:]
    length = rows_here * wide
    blocks = length // BLOCK
    heads_here = HEADS // wide
    shard = query_weight.shape[0]

    def reorder(values):
        return values.reshape(-1, wide, narrow, shard).swapaxes(1, 2).reshape(-1, width)

    def restore(values):
        return values.reshape(-1, narrow, wide, shard).swapaxes(1, 2).reshape(-1, width)

    def columns(weight):
        part = lax.all_to_all(weight, "wide", split_axis=1, concat_axis=0, tiled=True)
        return lax.all_gather(part, "narrow", axis=0, tiled=True)

    def gather_rows(values):
        return lax.all_gather(values, "wide", axis=0, tiled=True)

    def scatter_rows(values):
        return lax.psum_scatter(
            values.astype(BF), "wide", scatter_dimension=0, tiled=True
        ).astype(F32)

    def to_tokens(values):
        return lax.all_to_all(values, "wide", split_axis=0, concat_axis=1, tiled=True)

    def to_heads(values):
        return lax.all_to_all(values, "wide", split_axis=1, concat_axis=0, tiled=True)

    def column_sums(grad):
        part = lax.psum_scatter(grad.astype(BF), "narrow", scatter_dimension=0, tiled=True)
        return lax.all_to_all(part, "wide", split_axis=0, concat_axis=1, tiled=True).astype(F32)

    w_query, w_key, w_value, w_gate = map(
        columns, (query_weight, key_weight, value_weight, gate_weight)
    )
    w_out = lax.all_gather(out_weight, BOTH, axis=0, tiled=True)
    w_fval, w_fgate = map(columns, (ffn_value_weight, ffn_gate_weight))
    w_fout = lax.all_gather(ffn_out_weight, "narrow", axis=0, tiled=True)

    starts = lax.dynamic_slice_in_dim(doc_starts, lax.axis_index("narrow"), 1, 0)[0]
    positions = jnp.arange(length, dtype=jnp.int32)
    doc_ids = jnp.sum((starts[None, :] <= positions[:, None]).astype(jnp.int32), axis=1)
    doc_ids = doc_ids.reshape(blocks, BLOCK)
    firsts = jnp.arange(blocks, dtype=jnp.int32) * BLOCK - 1
    prev_ids = jnp.sum((starts[None, :] <= firsts[:, None]).astype(jnp.int32), axis=1)
    slopes = lax.dynamic_slice_in_dim(
        head_slopes(), lax.axis_index("wide") * heads_here, heads_here, 0
    )
    offsets = jnp.arange(BLOCK, dtype=F32)
    lags = offsets[:, None] - offsets[None, :]
    decays = jnp.exp(-slopes[:, None, None] * jnp.maximum(lags, 0.0)[None])
    within = (doc_ids[:, :, None] == doc_ids[:, None, :]) & (lags >= 0.0)
    block_mask = jnp.where(within[:, None], decays[None], 0.0)
    continues = (doc_ids == prev_ids[:, None]).astype(F32)
    entry_scale = continues[..., None] * jnp.exp(-slopes[None, :] * (offsets[:, None] + 1.0))
    tail_scale = (doc_ids == doc_ids[:, -1:]).astype(F32)[..., None] * jnp.exp(
        -slopes[None, :] * (BLOCK - 1.0 - offsets)[:, None]
    )
    passing = continues[:, -1:] * jnp.exp(-slopes * BLOCK)

    def split_heads(values):
        return values.reshape(blocks, BLOCK, heads_here, HEAD)

    inputs = tokens[0].astype(F32)
    normed, in_scale = normalize(inputs)
    normed_bf = gather_rows(reorder(normed.astype(BF)))
    query_pre = matmul(normed_bf, w_query)
    key_pre = matmul(normed_bf, w_key)
    queries = split_heads(jax.nn.silu(query_pre).astype(BF))
    keys = split_heads(jax.nn.silu(key_pre).astype(BF))
    values = split_heads(matmul(normed_bf, w_value).astype(BF))
    gate = matmul(normed_bf, w_gate)
    scores = ein("bihe,bjhe->bhij", queries, keys)
    probs = (scores * block_mask).astype(BF)
    inner = ein("bhij,bjhe->bihe", probs, values)
    tail_keys = (keys.astype(F32) * tail_scale[..., None]).astype(BF)
    fresh = ein("bjhe,bjhf->bhef", tail_keys, values)
    state = jnp.zeros((heads_here, HEAD, HEAD), F32)
    entering = []
    for b in range(blocks):
        entering.append(state)
        state = passing[b][:, None, None] * state + fresh[b]
    block_in = jnp.stack(entering).astype(BF)
    across = entry_scale[..., None] * ein("bihe,bhef->bihf", queries, block_in)
    attention = (inner + across).reshape(query_pre.shape)

    attn_tok = to_tokens(attention)
    gate_tok = to_tokens(gate)
    attn_n, attn_scale = normalize(attn_tok)
    mixed = (attn_n * gate_tok).astype(BF)
    middle = inputs + matmul(mixed, w_out)
    middle_n, middle_scale = normalize(middle)
    middle_bf = gather_rows(reorder(middle_n.astype(BF)))
    ffn_val = matmul(middle_bf, w_fval)
    ffn_gat = matmul(middle_bf, w_fgate)
    ffn_mix = (ffn_val * ffn_gat).astype(BF)
    result = middle + scatter_rows(matmul(ffn_mix, w_fout))

    upstream = cotangent[0]
    up_all = gather_rows(upstream)
    grad_fout = weight_grad(ffn_mix, up_all)
    d_mix = matmul_right_t(up_all, w_fout)
    d_val = (d_mix * ffn_gat).astype(BF)
    d_gat = (d_mix * ffn_val).astype(BF)
    grad_fval = weight_grad(middle_bf, d_val)
    grad_fgate = weight_grad(middle_bf, d_gat)
    d_middle_n = restore(
        scatter_rows(matmul_right_t(d_val, w_fval) + matmul_right_t(d_gat, w_fgate))
    )
    d_middle = upstream.astype(F32) + normalize_back(middle_n, middle_scale, d_middle_n)
    d_branch = d_middle.astype(BF)
    grad_out = weight_grad(mixed, d_branch)
    d_mixed = matmul_right_t(d_branch, w_out)
    d_gate = to_heads((d_mixed * attn_n).astype(BF))
    d_attn = to_heads(normalize_back(attn_n, attn_scale, d_mixed * gate_tok).astype(BF))

    d_heads = split_heads(d_attn)
    d_probs = ein("bihe,bjhe->bhij", d_heads, values)
    d_scores = (d_probs * block_mask).astype(BF)
    d_query = ein("bhij,bjhe->bihe", d_scores, keys)
    d_key = ein("bhij,bihe->bjhe", d_scores, queries)
    d_value = ein("bhij,bihe->bjhe", probs, d_heads)
    d_query = d_query + entry_scale[..., None] * ein("bihf,bhef->bihe", d_heads, block_in)
    entry_queries = (queries.astype(F32) * entry_scale[..., None]).astype(BF)
    grad_in = ein("bihe,bihf->bhef", entry_queries, d_heads)
    state = jnp.zeros((heads_here, HEAD, HEAD), F32)
    leaving = [None] * blocks
    for b in reversed(range(blocks)):
        leaving[b] = state
        state = passing[b][:, None, None] * state + grad_in[b]
    block_out = jnp.stack(leaving).astype(BF)
    d_key = d_key + tail_scale[..., None] * ein("bjhf,bhef->bjhe", values, block_out)
    d_value = d_value + ein("bjhe,bhef->bjhf", tail_keys, block_out)
    dq_pre = (d_query.reshape(query_pre.shape) * silu_slope(query_pre)).astype(BF)
    dk_pre = (d_key.reshape(key_pre.shape) * silu_slope(key_pre)).astype(BF)
    dv_pre = d_value.reshape(query_pre.shape).astype(BF)
    grad_query = weight_grad(normed_bf, dq_pre)
    grad_key = weight_grad(normed_bf, dk_pre)
    grad_value = weight_grad(normed_bf, dv_pre)
    grad_gate = weight_grad(normed_bf, d_gate)
    d_normed = restore(
        scatter_rows(
            matmul_right_t(dq_pre, w_query)
            + matmul_right_t(dk_pre, w_key)
            + matmul_right_t(dv_pre, w_value)
            + matmul_right_t(d_gate, w_gate)
        )
    )
    d_inputs = d_middle + normalize_back(normed, in_scale, d_normed)
    return (
        result.astype(BF)[None],
        d_inputs[None],
        column_sums(grad_query),
        column_sums(grad_key),
        column_sums(grad_value),
        column_sums(grad_gate),
        lax.psum_scatter(grad_out.astype(BF), BOTH, scatter_dimension=0, tiled=True).astype(F32),
        column_sums(grad_fval),
        column_sums(grad_fgate),
        lax.psum_scatter(grad_fout.astype(BF), "narrow", scatter_dimension=0, tiled=True).astype(
            F32
        ),
    )


def solution(mesh):
    tok = P("narrow", "wide", None)
    row = P(BOTH, None)
    return jax.shard_map(
        local,
        mesh=mesh,
        in_specs=(tok, P()) + (row,) * 8 + (tok,),
        out_specs=(tok, tok) + (row,) * 8,
        check_vma=False,
    )
```

time: 5780 us -> 1350 us (0.23)
  waiting for transfers between devices: 5400 us -> 828 us
  blocking collectives: 8.72 us -> 94.6 us
    reduce_scatter x8 -> x11, waiting for transfers between devices: 4610 us -> 393 us  [the longest x1 175 us: local(): lax.psum_scatter(grad_out.astype(BF), BOTH, scatter_dimension=0, tiled=True)]
    all_gather x10 -> x11, waiting for transfers between devices: 782 us -> 367 us  [the longest x3 160 us: gather_rows(): return lax.all_gather(values, 'wide', axis=0, tiled=True)]
    all_to_all x0 -> x7, blocking collectives: none -> 94.6 us  [the longest x5 58 us: columns(): lax.all_to_all(weight, 'wide', split_axis=1, concat_axis=0, tiled=True)]
    all_to_all x0 -> x9, waiting for transfers between devices: none -> 64.7 us  [the longest x2 43.3 us: to_tokens(): lax.all_to_all(values, 'wide', split_axis=0, concat_axis=1, tiled=True)]
  transfers between devices with their start and end apart: 18 -> 31, of which waited for: 18 -> 23; matrix products, arithmetic and copies ran while one was open for 5% -> 23% of each run, Pallas kernels for 0% -> 0%
where the time goes in v1:
time: 1350 us; the launch traced here: 1340 us
  waiting for transfers between devices  828 us (61%)
  matrix products  246 us (18%)
  blocking collectives  94.6 us (7%)
  local copies, waits for them, and re-layouts  80.4 us (6%)
  other arithmetic  41.1 us (3%)
  starting transfers between devices  35.3 us (3%)
  between operations  15.8 us (1%)
    reduce_scatter x1, waiting for transfers between devices, local(): lax.psum_scatter(grad_out.astype(BF), BOTH, scatter_dimension=0, tiled=True)  175 us
    all_gather x3, waiting for transfers between devices, gather_rows(): return lax.all_gather(values, 'wide', axis=0, tiled=True)  160 us
    reduce_scatter x3, waiting for transfers between devices, scatter_rows(): lax.psum_scatter(values.astype(BF), 'wide', scatter_dimension=0, tiled=True)  151 us
    all_gather x6, waiting for transfers between devices, columns(): return lax.all_gather(part, 'narrow', axis=0, tiled=True)  149 us
    dot_general x8, matrix products, matmul_right_t(): lax.dot_general(left, right, (((1,), (1,)), ((), ())), preferred_element_...  90.5 us
    dot_general x8, matrix products, matmul(): return jnp.dot(left, right, preferred_element_type=F32)  69.8 us
    reduce_scatter x6, waiting for transfers between devices, column_sums(): lax.psum_scatter(grad.astype(BF), 'narrow', scatter_dimension=0, tiled=True)  67.5 us
    dot_general x8, matrix products, weight_grad(): lax.dot_general(left, right, (((0,), (0,)), ((), ())), preferred_element_...  67.3 us
  transfers between devices with their start and end apart: 31, of which 23 were waited for; matrix products, arithmetic and copies ran while one was open for 23% of the time, Pallas kernels for 0%

profile of v1, /device:TPU:0, one launch (start us, length us, event | category | flops | bytes accessed | tf_op | source)
XLA Modules:
  0.0 1340.7 jit_solution(4751897208687020586)
XLA Ops:
  8.2 12.1 all_to_all.265
  24.5 10.2 all_to_all.266
  34.7 10.0 all_to_all.267
  44.9 10.0 all_to_all.268
  65.9 48.3 %all-gather.13.cloned.1.call-done = bf16[2048,2048]{0,1:T(8,128)(2,1)} async-done(((bf16[256,2048]{0,1:T(8,128)(2,1)}), bf16[2048,2048]{0,1:T(8,128)(2,1)}) %all-gather.13.cloned.1.call-update) | async-done | bytes 8388624 | tf_op jit(solution)/shard_map/all_gather | solution.py:84
  120.7 23.0 %all-gather.19.cloned.1.call-done = bf16[2048,256]{1,0:T(8,128)(2,1)} async-done(((bf16[512,256]{1,0:T(8,128)(2,1)}), bf16[2048,256]{1,0:T(8,128)(2,1)}) %all-gather.19.cloned.1.call-update) | async-done | bytes 1048592 | tf_op jit(solution)/shard_map/all_gather | solution.py:81
  143.7 7.7 multiply_convert_fusion.8
  155.4 17.2 %all-gather.17.cloned.1.call-done = bf16[2048,256]{1,0:T(8,128)(2,1)} async-done(((bf16[512,256]{1,0:T(8,128)(2,1)}), bf16[2048,256]{1,0:T(8,128)(2,1)}) %all-gather.17.cloned.1.call-update) | async-done | bytes 1048592 | tf_op jit(solution)/shard_map/all_gather | solution.py:81
  172.6 7.9 multiply_convert_fusion.9
  180.6 20.9 %all-gather.21.cloned.1.call-done = bf16[2048,256]{1,0:T(8,128)(2,1)} async-done(((bf16[512,256]{1,0:T(8,128)(2,1)}), bf16[2048,256]{1,0:T(8,128)(2,1)}) %all-gather.21.cloned.1.call-update) | async-done | bytes 1048592 | tf_op jit(solution)/shard_map/all_gather | solution.py:81
  201.5 7.4 fusion.46
  230.0 10.9 all-to-all-done.5
  248.5 32.4 %all-to-all-done.3 = f32[8,256,256]{1,2,0:T(8,128)S(1)} async-done(((f32[8,256,256]{1,2,0:T(8,128)}), f32[8,256,256]{1,2,0:T(8,128)S(1)}, u32[]{:S(2)}, u32[]{:S(2)}) %all-to-all-start.3) | async-done | bytes 2097184 | tf_op jit(solution)/shard_map/all_to_all | solution.py:92
  288.7 9.9 all-gather.23.cloned.1.call-done
  310.8 15.6 %all_to_all.269 = bf16[64,8,704]{2,0,1:T(8,128)(2,1)} all-to-all(bf16[64,8,704]{2,0,1:T(8,128)(2,1)S(1)} %copy.210), channel_id=1, replica_groups=mesh['wide'=8,'narrow'=4] {'wide'}, dimensions={1} | all-to-all | bytes 1441792 | tf_op jit(solution)/shard_map/all_to_all | solution.py:80
  327.9 34.0 %all-gather.29.cloned.1.call-done = bf16[2048,704]{1,0:T(8,128)(2,1)} async-done(((bf16[512,704]{1,0:T(8,128)(2,1)}), bf16[2048,704]{1,0:T(8,128)(2,1)}) %all-gather.29.cloned.1.call-update) | async-done | bytes 2883600 | tf_op jit(solution)/shard_map/all_gather | solution.py:81
  361.9 57.1 %all-gather.25.cloned.1.call-done = bf16[2048,2048]{0,1:T(8,128)(2,1)} async-done(((bf16[256,2048]{0,1:T(8,128)(2,1)}), bf16[2048,2048]{0,1:T(8,128)(2,1)}) %all-gather.25.cloned.1.call-update) | async-done | bytes 8388624 | tf_op jit(solution)/shard_map/all_gather | solution.py:84
  419.0 11.6 fusion.48
  430.5 53.5 %all-gather.27.cloned.1.call-done = bf16[2048,704]{1,0:T(8,128)(2,1)} async-done(((bf16[512,704]{1,0:T(8,128)(2,1)}), bf16[2048,704]{1,0:T(8,128)(2,1)}) %all-gather.27.cloned.1.call-update) | async-done | bytes 2883600 | tf_op jit(solution)/shard_map/all_gather | solution.py:81
  484.1 11.2 fusion.47
  495.3 48.0 %all-gather.31.cloned.1.call-done = bf16[704,2048]{1,0:T(8,128)(2,1)} async-done(((bf16[176,2048]{1,0:T(8,128)(2,1)}), bf16[704,2048]{1,0:T(8,128)(2,1)}) %all-gather.31.cloned.1.call-update) | async-done | bytes 2883600 | tf_op jit(solution)/shard_map/all_gather | solution.py:106
  543.3 55.0 %all-gather.33.cloned.1.call-done = bf16[1,2048,2048]{2,1,0:T(8,128)(2,1)} async-done(((bf16[1,256,2048]{2,1,0:T(8,128)(2,1)}), bf16[1,2048,2048]{2,1,0:T(8,128)(2,1)}) %all-gather.33.cloned.1.call-update) | async-done | bytes 8388624 | tf_op jit(solution)/shard_map/all_gather | solution.py:84
  598.3 13.4 %multiply_convert_fusion = (bf16[2048,704]{0,1:T(8,128)(2,1)S(1)}, bf16[2048,704]{0,1:T(8,128)(2,1)}, bf16[2048,704]{0,1:T(8,128)(2,1)S(1)}) fusion(f32[2048,704]{0,1:T(8,128)} %fusion.47, f32[2048,704]{0,1:T(8,128)} %fusion.48, bf16[704,2048]{1,0:T(8,128)(2,1)} %all-gather.31.cloned.1.call-done, bf16[1,2048,2048]{2,1,0:T(8,128)(2,1)} %all-gather.33.cloned.1.call-done), kind=kOutput, calls=%fused_computation.10 | convolution fusion | flops 5914230784 | bytes 31457280 | tf_op jit(solution)/shard_map/dot_general | solution.py:37
  611.8 10.7 fusion.49
  622.5 12.6 add_convert_fusion.1
  635.2 11.5 convolution_convert_fusion.1
  646.8 12.1 convolution_convert_fusion.3
  659.0 11.3 convolution_convert_fusion.2
  670.4 10.9 fusion.6
  681.3 25.3 %reduce-scatter.14.cloned.1.call-done = bf16[256,2048]{1,0:T(8,128)(2,1)} async-done(((bf16[2048,2048]{1,0:T(8,128)(2,1)}), bf16[256,2048]{1,0:T(8,128)(2,1)}) %reduce-scatter.14.cloned.1.call-update) | async-done | bytes 1048592 | tf_op jit(solution)/shard_map/reduce_scatter | solution.py:87
  717.8 63.9 %reduce-scatter.12.cloned.1.call-done = bf16[256,2048]{1,0:T(8,128)(2,1)} async-done(((bf16[2048,2048]{1,0:T(8,128)(2,1)}), bf16[256,2048]{1,0:T(8,128)(2,1)}) %reduce-scatter.12.cloned.1.call-update) | async-done | bytes 1048592 | tf_op jit(solution)/shard_map/reduce_scatter | solution.py:87
  786.0 7.1 multiply_reduce_fusion
  796.9 18.8 %all_to_all.270 = bf16[256,8,256]{0,2,1:T(8,128)(2,1)S(1)} all-to-all(bf16[256,8,256]{0,2,1:T(8,128)(2,1)} %bitcast.272), channel_id=1, replica_groups=mesh['wide'=8,'narrow'=4] {'wide'}, dimensions={1} | all-to-all | bytes 2097152 | tf_op jit(solution)/shard_map/all_to_all | solution.py:95
  829.9 6.9 convolution_convert_fusion.6
  850.8 6.7 convolution_convert_fusion.7
  862.5 6.9 convolution_convert_fusion.5
  869.6 17.8 %all_to_all.271 = bf16[256,8,256]{2,0,1:T(8,128)(2,1)S(1)} all-to-all(bf16[256,8,256]{2,0,1:T(8,128)(2,1)S(1)} %bitcast.274), channel_id=1, replica_groups=mesh['wide'=8,'narrow'=4] {'wide'}, dimensions={1} | all-to-all | bytes 2097152 | tf_op jit(solution)/shard_map/all_to_all | solution.py:95
  888.3 6.8 convolution_convert_fusion.4
  895.4 9.9 fusion.55
  905.3 8.1 fusion.51
  913.5 8.2 fusion.53
  921.6 20.5 %add_convert_fusion = bf16[2048,2048]{1,0:T(8,128)(2,1)} fusion(f32[2048,2048]{1,0:T(8,128)} %fusion.55, f32[2048,2048]{1,0:T(8,128)} %fusion.51, f32[2048,2048]{1,0:T(8,128)} %fusion.53, bf16[2048,256]{1,0:T(8,128)(2,1)S(1)} %bitcast.276, bf16[2048,256]{1,0:T(8,128)(2,1)S(1)} %copy-done.40), kind=kOutput, calls=%fused_computation | convolution fusion | flops 2164260864 | bytes 60817408 | tf_op jit(solution)/shard_map/dot_general | solution.py:37
  957.2 10.2 all-to-all-done.14
  994.5 19.3 %reduce-scatter.18.cloned.1.call-done = bf16[512,256]{1,0:T(8,128)(2,1)} async-done(((bf16[2048,256]{1,0:T(8,128)(2,1)}), bf16[512,256]{1,0:T(8,128)(2,1)}) %reduce-scatter.18.cloned.1.call-update) | async-done | bytes 262160 | tf_op jit(solution)/shard_map/reduce_scatter | solution.py:98
  1018.3 23.6 %reduce-scatter.22.cloned.1.call-done = bf16[512,256]{1,0:T(8,128)(2,1)} async-done(((bf16[2048,256]{1,0:T(8,128)(2,1)}), bf16[512,256]{1,0:T(8,128)(2,1)}) %reduce-scatter.22.cloned.1.call-update) | async-done | bytes 262160 | tf_op jit(solution)/shard_map/reduce_scatter | solution.py:98
  1046.5 23.5 %reduce-scatter.24.cloned.1.call-done = bf16[512,256]{1,0:T(8,128)(2,1)} async-done(((bf16[2048,256]{1,0:T(8,128)(2,1)}), bf16[512,256]{1,0:T(8,128)(2,1)}) %reduce-scatter.24.cloned.1.call-update) | async-done | bytes 262160 | tf_op jit(solution)/shard_map/reduce_scatter | solution.py:98
  1081.5 61.9 %reduce-scatter.16.cloned.1.call-done = bf16[256,2048]{1,0:T(8,128)(2,1)} async-done(((bf16[2048,2048]{1,0:T(8,128)(2,1)}), bf16[256,2048]{1,0:T(8,128)(2,1)}) %reduce-scatter.16.cloned.1.call-update) | async-done | bytes 1048592 | tf_op jit(solution)/shard_map/reduce_scatter | solution.py:87
  1157.1 174.6 %reduce-scatter.26.cloned.1.call-done = bf16[64,2048]{1,0:T(8,128)(2,1)} async-done(((bf16[2048,2048]{1,0:T(8,128)(2,1)}), bf16[64,2048]{1,0:T(8,128)(2,1)}) %reduce-scatter.26.cloned.1.call-update) | async-done | bytes 262160 | tf_op jit(solution)/shard_map/reduce_scatter | solution.py:225
  (322 shorter events, 208.1 us)
Async XLA Ops:
  7.2 54.2 %copy-start = (s32[4,4]{1,0:T(4,128)S(1)}, s32[4,4]{1,0:T(4,128)}, u32[]{:S(2)}) copy-start(s32[4,4]{1,0:T(4,128)} %param.12) | copy-start | bytes 196
  7.2 58.7 %all-gather.15.cloned.1.call-start = ((), (), s32[]{:S(2)}) async-start(), calls=%async_computation.28 | async-start | bytes 1310720 | tf_op jit(solution)/shard_map/all_gather | solution.py:81
  20.4 93.8 %all-gather.13.cloned.1.call-start = ((), (), s32[]{:S(2)}) async-start(), calls=%async_computation.27 | async-start | bytes 9437184 | tf_op jit(solution)/shard_map/all_gather | solution.py:84
  24.4 119.4 %all-gather.19.cloned.1.call-start = ((), (), s32[]{:S(2)}) async-start(), calls=%async_computation.30 | async-start | bytes 1310720 | tf_op jit(solution)/shard_map/all_gather | solution.py:81
  24.4 31.0 %copy-start.41 = (bf16[64,5632]{1,0:T(8,128)(2,1)S(1)}, bf16[64,5632]{1,0:T(8,128)(2,1)}, u32[]{:S(2)}) copy-start(bf16[64,5632]{1,0:T(8,128)(2,1)} %param.19) | copy-start | bytes 2162692
  34.7 138.0 %all-gather.17.cloned.1.call-start = ((), (), s32[]{:S(2)}) async-start(), calls=%async_computation.29 | async-start | bytes 1310720 | tf_op jit(solution)/shard_map/all_gather | solution.py:81
  44.8 156.7 %all-gather.21.cloned.1.call-start = ((), (), s32[]{:S(2)}) async-start(), calls=%async_computation.31 | async-start | bytes 1310720 | tf_op jit(solution)/shard_map/all_gather | solution.py:81
  54.9 243.7 %all-gather.23.cloned.1.call-start = ((), (), s32[]{:S(2)}) async-start(), calls=%async_computation.32 | async-start | bytes 8650752 | tf_op jit(solution)/shard_map/all_gather | solution.py:104
  57.2 151.7 %all-to-all-start.7 = ((bf16[64,8,704]{2,0,1:T(8,128)(2,1)}), bf16[64,8,704]{2,0,1:T(8,128)(2,1)}, u32[]{:S(2)}, u32[]{:S(2)}) async-start(bf16[64,8,704]{2,0,1:T(8,128)(2,1)} %copy.211), calls=%async_computation.7 | async-start | bytes 1572864 | tf_op jit(solution)/shard_map/all_to_all | solution.py:80
  63.7 90.3 %copy-start.64 = (f32[2]{0:T(128)}, f32[2]{0:T(128)S(1)}, u32[]{:S(2)}) copy-start(f32[2]{0:T(128)S(1)} %get-tuple-element.38) | copy-start | bytes 28
  63.7 149.6 %copy-start.55 = (f32[2]{0:T(128)}, f32[2]{0:T(128)S(1)}, u32[]{:S(2)}) copy-start(f32[2]{0:T(128)S(1)} %get-tuple-element.36) | copy-start | bytes 28
  63.7 149.6 %copy-start.59 = (f32[2]{0:T(128)}, f32[2]{0:T(128)S(1)}, u32[]{:S(2)}) copy-start(f32[2]{0:T(128)S(1)} %get-tuple-element.37) | copy-start | bytes 28
  63.7 156.7 %copy-start.53 = (f32[2]{0:T(128)}, f32[2]{0:T(128)S(1)}, u32[]{:S(2)}) copy-start(f32[2]{0:T(128)S(1)} %get-tuple-element.34) | copy-start | bytes 28
  63.7 156.7 %copy-start.57 = (f32[2]{0:T(128)}, f32[2]{0:T(128)S(1)}, u32[]{:S(2)}) copy-start(f32[2]{0:T(128)S(1)} %get-tuple-element.35) | copy-start | bytes 28
  63.7 158.4 %copy-start.62 = (f32[2]{0:T(128)}, f32[2]{0:T(128)S(1)}, u32[]{:S(2)}) copy-start(f32[2]{0:T(128)S(1)} %get-tuple-element.33) | copy-start | bytes 28
  63.7 162.9 %copy-start.46 = (f32[8,256,2]{1,2,0:T(2,128)}, f32[8,256,2]{1,2,0:T(2,128)S(1)}, u32[]{:S(2)}) copy-start(f32[8,256,2]{1,2,0:T(2,128)S(1)} %broadcast_multiply_fusion.1) | copy-start | bytes 49156
  63.7 88.9 %copy-start.44 = (f32[8,256,2]{1,2,0:T(2,128)}, f32[8,256,2]{1,2,0:T(2,128)S(1)}, u32[]{:S(2)}) copy-start(f32[8,256,2]{1,2,0:T(2,128)S(1)} %broadcast_multiply_fusion) | copy-start | bytes 49156
  120.7 105.1 %copy-start.11 = (bf16[8,256,2,128]{3,2,1,0:T(2,128)(2,1)}, bf16[8,256,2,128]{3,2,1,0:T(2,128)(2,1)S(1)}, u32[]{:S(2)}) copy-start(bf16[8,256,2,128]{3,2,1,0:T(2,128)(2,1)S(1)} %reshape.344) | copy-start | bytes 3145732
  152.7 71.0 %copy-start.9 = (bf16[8,256,2,128]{1,3,2,0:T(8,128)(2,1)}, bf16[8,256,2,128]{1,3,2,0:T(8,128)(2,1)S(1)}, u32[]{:S(2)}) copy-start(bf16[8,256,2,128]{1,3,2,0:T(8,128)(2,1)S(1)} %copy.201) | copy-start | bytes 3145732
  153.1 60.2 %copy-start.24 = (f32[8,2,128,128]{3,2,1,0:T(8,128)}, f32[8,2,128,128]{3,2,1,0:T(8,128)S(1)}, u32[]{:S(2)}) copy-start(f32[8,2,128,128]{3,2,1,0:T(8,128)S(1)} %fusion.27) | copy-start | bytes 3145732
  208.9 32.0 %all-to-all-start.5 = ((f32[8,256,256]{2,1,0:T(8,128)}), f32[8,256,256]{2,1,0:T(8,128)}, u32[]{:S(2)}, u32[]{:S(2)}) async-start(f32[8,256,256]{2,1,0:T(8,128)} %bitcast.278), calls=%async_computation.5 | async-start | bytes 4194304 | tf_op jit(solution)/shard_map/all_to_all | solution.py:92
  240.9 40.0 %all-to-all-start.3 = ((f32[8,256,256]{1,2,0:T(8,128)}), f32[8,256,256]{1,2,0:T(8,128)S(1)}, u32[]{:S(2)}, u32[]{:S(2)}) async-start(f32[8,256,256]{1,2,0:T(8,128)} %bitcast.265), calls=%async_computation.3 | async-start | bytes 4194304 | tf_op jit(solution)/shard_map/all_to_all | solution.py:92
  244.5 117.3 %all-gather.29.cloned.1.call-start = ((), (), s32[]{:S(2)}) async-start(), calls=%async_computation.35 | async-start | bytes 3932160 | tf_op jit(solution)/shard_map/all_gather | solution.py:81
  245.3 173.7 %all-gather.25.cloned.1.call-start = ((), (), s32[]{:S(2)}) async-start(), calls=%async_computation.33 | async-start | bytes 9437184 | tf_op jit(solution)/shard_map/all_gather | solution.py:84
  304.8 410.7 %copy-start.6 = (f32[256,2048]{1,0:T(8,128)}, f32[256,2048]{1,0:T(8,128)S(1)}, u32[]{:S(2)}) copy-start(f32[256,2048]{1,0:T(8,128)S(1)} %get-tuple-element.47) | copy-start | bytes 6291460
  308.8 175.3 %all-gather.27.cloned.1.call-start = ((), (), s32[]{:S(2)}) async-start(), calls=%async_computation.34 | async-start | bytes 3932160 | tf_op jit(solution)/shard_map/all_gather | solution.py:81
  326.5 216.9 %all-gather.31.cloned.1.call-start = ((), (), s32[]{:S(2)}) async-start(), calls=%async_computation.36 | async-start | bytes 3604480 | tf_op jit(solution)/shard_map/all_gather | solution.py:106
  327.1 271.3 %all-gather.33.cloned.1.call-start = ((), (), s32[]{:S(2)}) async-start(), calls=%async_computation.48 | async-start | bytes 9437184 | tf_op jit(solution)/shard_map/all_gather | solution.py:84
  327.8 378.8 %reduce-scatter.14.cloned.1.call-start = ((), (), s32[]{:S(2)}) async-start(), calls=%async_computation.38 | async-start | bytes 9437184 | tf_op jit(solution)/shard_map/reduce_scatter | solution.py:87
  635.2 146.6 %reduce-scatter.12.cloned.1.call-start = ((), (), s32[]{:S(2)}) async-start(), calls=%async_computation.37 | async-start | bytes 9437184 | tf_op jit(solution)/shard_map/reduce_scatter | solution.py:87
  646.8 302.3 %reduce-scatter.28.cloned.1.call-start = ((), (), s32[]{:S(2)}) async-start(), calls=%async_computation.45 | async-start | bytes 3604480 | tf_op jit(solution)/shard_map/reduce_scatter | solution.py:98
  658.9 296.0 %reduce-scatter.30.cloned.1.call-start = ((), (), s32[]{:S(2)}) async-start(), calls=%async_computation.46 | async-start | bytes 3604480 | tf_op jit(solution)/shard_map/reduce_scatter | solution.py:98
  670.3 301.8 %reduce-scatter.32.cloned.1.call-start = ((), (), s32[]{:S(2)}) async-start(), calls=%async_computation.47 | async-start | bytes 3604480 | tf_op jit(solution)/shard_map/reduce_scatter | solution.py:228
  681.2 304.5 %reduce-scatter.20.cloned.1.call-start = ((), (), s32[]{:S(2)}) async-start(), calls=%async_computation.41 | async-start | bytes 1310720 | tf_op jit(solution)/shard_map/reduce_scatter | solution.py:98
  715.6 66.2 %copy-start.29 = (bf16[1,256,2048]{2,1,0:T(8,128)(2,1)S(1)}, bf16[1,256,2048]{2,1,0:T(8,128)(2,1)}, u32[]{:S(2)}) copy-start(bf16[1,256,2048]{2,1,0:T(8,128)(2,1)} %param.21) | copy-start | bytes 3145732
  794.5 21.2 %copy-start.47 = (f32[8,256,2]{1,2,0:T(2,128)S(1)}, f32[8,256,2]{1,2,0:T(2,128)}, u32[]{:S(2)}) copy-start(f32[8,256,2]{1,2,0:T(2,128)} %copy-done.46) | copy-start | bytes 49156
  836.8 177.0 %reduce-scatter.18.cloned.1.call-start = ((), (), s32[]{:S(2)}) async-start(), calls=%async_computation.40 | async-start | bytes 1310720 | tf_op jit(solution)/shard_map/reduce_scatter | solution.py:98
  857.6 184.3 %reduce-scatter.22.cloned.1.call-start = ((), (), s32[]{:S(2)}) async-start(), calls=%async_computation.42 | async-start | bytes 1310720 | tf_op jit(solution)/shard_map/reduce_scatter | solution.py:98
  869.5 200.6 %reduce-scatter.24.cloned.1.call-start = ((), (), s32[]{:S(2)}) async-start(), calls=%async_computation.43 | async-start | bytes 1310720 | tf_op jit(solution)/shard_map/reduce_scatter | solution.py:98
  895.2 248.2 %reduce-scatter.16.cloned.1.call-start = ((), (), s32[]{:S(2)}) async-start(), calls=%async_computation.39 | async-start | bytes 9437184 | tf_op jit(solution)/shard_map/reduce_scatter | solution.py:87
  942.1 389.5 %reduce-scatter.26.cloned.1.call-start = ((), (), s32[]{:S(2)}) async-start(), calls=%async_computation.44 | async-start | bytes 8650752 | tf_op jit(solution)/shard_map/reduce_scatter | solution.py:225
  951.4 16.1 %all-to-all-start.14 = ((bf16[8,64,704]{2,1,0:T(8,128)(2,1)}), bf16[8,64,704]{2,1,0:T(8,128)(2,1)S(1)}, u32[]{:S(2)}, u32[]{:S(2)}) async-start(bf16[8,64,704]{2,1,0:T(8,128)(2,1)} %bitcast.65), calls=%async_computation.23 | async-start | bytes 1572864 | tf_op jit(solution)/shard_map/all_to_all | solution.py:99
  968.3 16.3 %all-to-all-start.15 = ((bf16[8,64,704]{2,1,0:T(8,128)(2,1)}), bf16[8,64,704]{2,1,0:T(8,128)(2,1)S(1)}, u32[]{:S(2)}, u32[]{:S(2)}) async-start(bf16[8,64,704]{2,1,0:T(8,128)(2,1)} %bitcast.67), calls=%async_computation.25 | async-start | bytes 1572864 | tf_op jit(solution)/shard_map/all_to_all | solution.py:99
  985.7 28.1 %all-to-all-start.11 = ((bf16[8,64,256]{2,1,0:T(8,128)(2,1)}), bf16[8,64,256]{2,1,0:T(8,128)(2,1)S(1)}, u32[]{:S(2)}, u32[]{:S(2)}) async-start(bf16[8,64,256]{2,1,0:T(8,128)(2,1)} %bitcast.295), calls=%async_computation.16 | async-start | bytes 524288 | tf_op jit(solution)/shard_map/all_to_all | solution.py:99
  1013.8 28.1 %all-to-all-start.10 = ((bf16[8,64,256]{2,1,0:T(8,128)(2,1)}), bf16[8,64,256]{2,1,0:T(8,128)(2,1)S(1)}, u32[]{:S(2)}, u32[]{:S(2)}) async-start(bf16[8,64,256]{2,1,0:T(8,128)(2,1)} %bitcast.296), calls=%async_computation.14 | async-start | bytes 524288 | tf_op jit(solution)/shard_map/all_to_all | solution.py:99
  1041.9 28.1 %all-to-all-start.12 = ((bf16[8,64,256]{2,1,0:T(8,128)(2,1)}), bf16[8,64,256]{2,1,0:T(8,128)(2,1)S(1)}, u32[]{:S(2)}, u32[]{:S(2)}) async-start(bf16[8,64,256]{2,1,0:T(8,128)(2,1)} %bitcast.297), calls=%async_computation.18 | async-start | bytes 524288 | tf_op jit(solution)/shard_map/all_to_all | solution.py:99
  1070.0 10.6 all-to-all-start.13
  1155.2 178.2 %copy-start.1 = (s32[4,4]{1,0:T(4,128)S(1)}, s32[4,4]{1,0:T(4,128)}, u32[]{:S(2)}) copy-start(s32[4,4]{1,0:T(4,128)} %param.12) | copy-start | bytes 196
  (53 other events, 258.1 us)
Sparse Core Ops, SparseCore 0:
  20.5 27.2 all-gather.14
  50.3 63.8 all-gather.12
  115.8 27.9 all-gather.18
  145.2 27.4 all-gather.16
  174.0 27.4 all-gather.20
  204.3 94.2 all-gather.22
  300.2 61.6 all-gather.28
  364.3 54.5 all-gather.24
  420.5 63.4 all-gather.26
  485.5 57.8 all-gather.30
  545.2 53.0 all-gather.32
  635.3 71.2 reduce-scatter.13
  710.4 71.2 reduce-scatter.11
  783.9 56.1 reduce-scatter.27
  842.3 56.0 reduce-scatter.29
  900.5 56.0 reduce-scatter.31
  958.7 26.9 reduce-scatter.19
  988.0 25.7 reduce-scatter.17
  1016.1 25.7 reduce-scatter.21
  1044.2 25.8 reduce-scatter.23
  1073.5 69.8 reduce-scatter.15
  1145.8 185.7 reduce-scatter.25

commit v2 on v1

--- a/solution.py
+++ b/solution.py
@@ -1,6 +1,8 @@
 import jax
 import jax.numpy as jnp
 from jax import lax
+from jax.experimental import pallas as pl
+from jax.experimental.pallas import tpu as pltpu
 from jax.sharding import PartitionSpec as P
 
 HEADS = 16
@@ -231,11 +233,698 @@
     )
 
 
+MESH = pl.DeviceIdType.MESH
+ANY = pl.BlockSpec(memory_space=pl.ANY)
+VMEM = pl.BlockSpec(memory_space=pltpu.VMEM)
+WIDE, NARROW = 8, 4
+CHIPS = WIDE // 2
+
+
+def dot(left, right):
+    return jnp.dot(left, right, preferred_element_type=F32)
+
+
+def dot_rt(left, right):
+    return lax.dot_general(left, right, (((1,), (1,)), ((), ())), preferred_element_type=F32)
+
+
+def dot_lt(left, right):
+    return lax.dot_general(left, right, (((0,), (0,)), ((), ())), preferred_element_type=F32)
+
+
+def at(start, size):
+    return pl.ds(pl.multiple_of(start, size), size)
+
+
+class Links:
+    def __init__(self, send, recv, here):
+        self.send, self.recv, self.here = send, recv, here
+        self.count = 0
+        self.sent, self.kept = [], []
+        w = lax.axis_index("wide")
+        n = lax.axis_index("narrow")
+        self.w, self.n = w, n
+        self.core = lax.rem(w, 2)
+        self.chip = lax.div(w, 2)
+        x, y = lax.rem(self.chip, 2), lax.div(self.chip, 2)
+        self.wx = w + 2 - 4 * x
+        self.wy = w + 4 - 8 * y
+        self.wd = w + 6 - 4 * x - 8 * y
+        self.ws = w + 1 - 2 * self.core
+        self.px = self.chip + 1 - 2 * x
+        self.py = self.chip + 2 - 4 * y
+        self.pd = 3 - self.chip
+        self.mid = lax.rem(lax.div(n + 1, 2), 2)
+        self.pair = n + 1 - 2 * lax.rem(n, 2)
+        self.cross = 2 - lax.div(n, 2)
+        self.far = 3 - 3 * lax.div(n, 2)
+        self.end_to = 3 * lax.rem(n + 1, 2)
+        self.end_part = lax.rem(2 * n, 3) + 3 * lax.div(n, 3)
+
+    def greet(self):
+        barrier = pltpu.get_barrier_semaphore()
+        for d in range(1, WIDE):
+            pl.semaphore_signal(
+                barrier, inc=1, device_id=(lax.rem(self.w + d, WIDE), self.n), device_id_type=MESH
+            )
+        for d in range(1, NARROW):
+            pl.semaphore_signal(
+                barrier, inc=1, device_id=(self.w, lax.rem(self.n + d, NARROW)), device_id_type=MESH
+            )
+
+    def met(self):
+        pl.semaphore_wait(pltpu.get_barrier_semaphore(), WIDE + NARROW - 2)
+
+    def take(self, number):
+        base = self.count
+        self.count += number
+        return base
+
+    def remote(self, src, dst, send, recv, wide=None, narrow=None):
+        return pltpu.make_async_remote_copy(
+            src_ref=src,
+            dst_ref=dst,
+            send_sem=self.send.at[send],
+            recv_sem=self.recv.at[recv],
+            device_id=(self.w if wide is None else wide, self.n if narrow is None else narrow),
+            device_id_type=MESH,
+        )
+
+    def go(self, src, dst, send, recv, wide=None, narrow=None):
+        copy = self.remote(src, dst, send, recv, wide, narrow)
+        copy.start()
+        self.sent.append(copy)
+
+    def arrived(self, ref, recv):
+        self.remote(ref, ref, recv, recv, wide=self.ws).wait_recv()
+
+    def keep(self, src, dst):
+        copy = pltpu.make_async_copy(src, dst, self.here.at[len(self.kept)])
+        copy.start()
+        self.kept.append(copy)
+        return copy
+
+    def drain(self):
+        for copy in self.sent:
+            copy.wait_send()
+
+
+class Line:
+    def __init__(self, links, part):
+        self.links, self.part = links, part
+        self.base = links.take(4)
+
+    def start(self):
+        k, b, mine = self.links, self.base, self.part(self.links.n)
+        k.go(mine, mine, b, b + k.n, narrow=k.pair)
+        k.go(mine, mine, b + 1, b + k.n, narrow=k.cross)
+        last = self.part(k.end_part)
+        self.last = k.remote(last, last, b + 2, b + k.end_part, narrow=k.end_to)
+
+        @pl.when(k.mid == 0)
+        def _():
+            self.last.start()
+
+    def wait(self, index):
+        self.links.arrived(self.part(index), self.base + index)
+
+    def forward(self):
+        @pl.when(self.links.mid == 1)
+        def _():
+            self.wait(self.links.cross)
+            self.last.start()
+
+    def finish(self):
+        k = self.links
+        self.wait(k.pair)
+        self.wait(k.far)
+
+        @pl.when(k.mid == 0)
+        def _():
+            self.wait(k.cross)
+
+        k.sent.append(self.last)
+
+
+class Plane:
+    def __init__(self, links, slot):
+        self.links, self.slot = links, slot
+        self.base = links.take(6)
+
+    def start(self):
+        k, b, slot = self.links, self.base, self.slot
+        k.go(slot(k.w, 0), slot(k.w, 0), b, b, wide=k.wx)
+        k.go(slot(k.w, 1), slot(k.w, 1), b + 3, b + 3, wide=k.wy)
+        k.go(slot(k.w, 1), slot(k.w, 1), b + 1, b + 1, wide=k.wx)
+        k.go(slot(k.w, 0), slot(k.w, 0), b + 2, b + 2, wide=k.wy)
+
+    def forward(self):
+        k, b, slot = self.links, self.base, self.slot
+        k.arrived(slot(k.wx, 0), b)
+        k.go(slot(k.wx, 0), slot(k.wx, 0), b + 4, b + 4, wide=k.wy)
+        k.arrived(slot(k.wy, 1), b + 3)
+        k.go(slot(k.wy, 1), slot(k.wy, 1), b + 5, b + 5, wide=k.wx)
+
+    def finish_near(self):
+        k, b, slot = self.links, self.base, self.slot
+        k.arrived(slot(k.wx, 1), b + 1)
+        k.arrived(slot(k.wy, 0), b + 2)
+
+    def finish_far(self):
+        k, b, slot = self.links, self.base, self.slot
+        k.arrived(slot(k.wd, 0), b + 4)
+        k.arrived(slot(k.wd, 1), b + 5)
+
+
+class Sibling:
+    def __init__(self, links, block, number):
+        self.links, self.block = links, block
+        self.base = links.take(number)
+        self.out, self.come = 0, 0
+
+    def send(self, w):
+        b = self.block(w)
+        self.links.go(b, b, self.base + self.out, self.base + self.out, wide=self.links.ws)
+        self.out += 1
+
+    def wait(self, w):
+        self.links.arrived(self.block(w), self.base + self.come)
+        self.come += 1
+
+
+class Spread:
+    def __init__(self, links, src, dst, peers=WIDE):
+        self.links, self.src, self.dst = links, src, dst
+        self.step = 1 if peers == WIDE else 2
+        self.base = links.take(WIDE)
+
+    def distances(self):
+        return range(self.step, WIDE, self.step)
+
+    def start(self):
+        k = self.links
+        for d in self.distances():
+            to = lax.rem(k.w + d, WIDE)
+            k.go(self.src(to), self.dst(k.w), self.base + d, self.base + d, wide=to)
+
+    def wait(self, d):
+        self.links.arrived(self.dst(lax.rem(self.links.w + WIDE - d, WIDE)), self.base + d)
+
+    def finish(self):
+        for d in self.distances():
+            self.wait(d)
+
+
+def row_scale(values):
+    return lax.rsqrt(jnp.mean(values * values, axis=-1, keepdims=True) + EPS)
+
+
+def row_chunks(rows, body, size=32):
+    def step(r, carry):
+        body(at(r * size, size))
+        return carry
+
+    lax.fori_loop(0, rows // size, step, 0)
+
+
+def doc_mask(cols, rowdoc, decay, rows, block):
+    tokens = decay.shape[-1]
+    same = cols[rows, 0:1] == rowdoc[pl.ds(block, 1), :]
+    i = lax.broadcasted_iota(jnp.int32, (tokens, tokens), 0)
+    j = lax.broadcasted_iota(jnp.int32, (tokens, tokens), 1)
+    return same & (i >= j)
+
+
+def forward_kernel(
+    x_ref, wq, wk, wv, wg, wo, fv, fg, dy, cols, rowdoc, passing, decay,
+    xn_o, wqk_o, wvg_o, wo_o, fv_o, fg_o, dy_o, pre_o, qkv_o, sin_o, attn_o, gate_o, mixed_o,
+    x1_o, x1n_o,
+    xn, wqk, wvg, wout, pre, qkv, gates, sin, state, attn_s, attn, gate, mixed, x1, x1n,
+    send, recv, here,
+):
+    k = Links(send, recv, here)
+    w, n, core, chip = k.w, k.n, k.core, k.chip
+    head_cols = 2 * HEAD
+    tok = x_ref.shape[0]
+    ff = fv_o.shape[-1]
+
+    def wide_cols(index):
+        return at(index * head_cols, head_cols)
+
+    def chip_cols(index):
+        return pl.ds(pl.multiple_of(index * ff, 128), ff)
+
+    k.greet()
+    own = [k.keep(wo, wout.at[w, n])]
+    for m, (weight, to) in enumerate(((wq, wqk), (wk, wqk), (wv, wvg), (wg, wvg))):
+        own.append(
+            k.keep(weight.at[:, wide_cols(w)], to.at[w, n, :, pl.ds((m % 2) * head_cols, head_cols)])
+        )
+    own_ff = [
+        k.keep(fv.at[:, chip_cols(chip)], fv_o.at[chip, core, n]),
+        k.keep(fg.at[:, chip_cols(chip)], fg_o.at[chip, core, n]),
+        k.keep(dy, dy_o.at[chip]),
+    ]
+
+    def norm_in(rows):
+        v = x_ref[rows, :].astype(F32)
+        xn[w, rows, :] = (v * row_scale(v)).astype(BF)
+
+    row_chunks(tok, norm_in)
+    k.met()
+
+    line_out = Line(k, lambda i: wout.at[w, i])
+    line_qk = Line(k, lambda i: wqk.at[:, i])
+    line_vg = Line(k, lambda i: wvg.at[:, i])
+    line_fv = Line(k, lambda i: fv_o.at[:, core, i])
+    line_fg = Line(k, lambda i: fg_o.at[:, core, i])
+    spreads = []
+    for m, (weight, to) in enumerate(((wq, wqk), (wk, wqk), (wv, wvg), (wg, wvg))):
+        lanes = pl.ds((m % 2) * head_cols, head_cols)
+        spreads.append(
+            Spread(
+                k,
+                lambda t, weight=weight: weight.at[:, wide_cols(t)],
+                lambda s, to=to, lanes=lanes: to.at[s, n, :, lanes],
+            )
+        )
+    spread_ff = [
+        Spread(
+            k,
+            lambda t, weight=weight: weight.at[:, chip_cols(lax.div(t, 2))],
+            lambda s, to=to: to.at[lax.div(s, 2), core, n],
+            peers=CHIPS,
+        )
+        for weight, to in ((fv, fv_o), (fg, fg_o))
+    ]
+    half = tok // 2
+    plane_xn = Plane(k, lambda s, h: xn.at[s, pl.ds(h * half, half)])
+    plane_out = Plane(k, lambda s, h: wout.at[s, pl.ds(h * 2, 2)])
+    plane_dy = Plane(k, lambda s, h: dy_o.at[lax.div(s, 2), pl.ds(h * half, half)])
+    plane_x1n = Plane(k, lambda s, h: x1n_o.at[lax.div(s, 2), pl.ds(h * half, half)])
+    twin_xn = Sibling(k, lambda s: xn.at[s], 4)
+    twin_out = Sibling(k, lambda s: wout.at[s], 4)
+    twin_fv = Sibling(k, lambda s: fv_o.at[:, s], 1)
+    twin_fg = Sibling(k, lambda s: fg_o.at[:, s], 1)
+    other = 1 - core
+
+    for copy in own:
+        copy.wait()
+    line_out.start()
+    spreads[0].start()
+    spreads[1].start()
+    plane_xn.start()
+    spreads[2].start()
+    spreads[3].start()
+    twin_xn.send(w)
+    spreads[0].finish()
+    spreads[1].finish()
+    line_qk.start()
+    spreads[2].finish()
+    spreads[3].finish()
+    line_vg.start()
+    for copy in own_ff:
+        copy.wait()
+    spread_ff[0].start()
+    spread_ff[1].start()
+    plane_xn.forward()
+    plane_xn.finish_near()
+    twin_xn.send(k.wx)
+    twin_xn.send(k.wy)
+    line_out.forward()
+    line_out.finish()
+    plane_out.start()
+    twin_out.send(w)
+    line_qk.forward()
+    plane_xn.finish_far()
+    twin_xn.send(k.wd)
+    line_vg.forward()
+    plane_out.forward()
+    plane_out.finish_near()
+    twin_out.send(k.wx)
+    twin_out.send(k.wy)
+    plane_out.finish_far()
+    twin_out.send(k.wd)
+    plane_dy.start()
+    spread_ff[0].finish()
+    spread_ff[1].finish()
+    for s in (k.ws, k.wx + 1 - 2 * core, k.wy + 1 - 2 * core, k.wd + 1 - 2 * core):
+        twin_xn.wait(s)
+    keep_xn = k.keep(xn, xn_o)
+
+    line_qk.finish()
+    line_fv.start()
+
+    def project_qk(t, carry):
+        v = dot(xn[t], wqk[...].reshape(-1, 2 * head_cols))
+        rows = at(t * tok, tok)
+        pre[rows, :] = v
+        qkv[rows, 0 : 2 * head_cols] = (v * jax.nn.sigmoid(v)).astype(BF)
+        return carry
+
+    lax.fori_loop(0, WIDE, project_qk, 0)
+    keep_pre = k.keep(pre, pre_o)
+    keep_wqk = k.keep(wqk, wqk_o)
+    line_vg.finish()
+    line_fg.start()
+
+    def project_vg(t, carry):
+        v = dot(xn[t], wvg[...].reshape(-1, 2 * head_cols)).astype(BF)
+        qkv[at(t * tok, tok), 2 * head_cols : 3 * head_cols] = v[:, 0:head_cols]
+        gates[t] = v[:, head_cols:]
+        return carry
+
+    lax.fori_loop(0, WIDE, project_vg, 0)
+    keep_wvg = k.keep(wvg, wvg_o)
+    keep_qkv = k.keep(qkv, qkv_o)
+    spread_gate = Spread(k, lambda t: gates.at[t], lambda s: gate.at[:, wide_cols(s)])
+    spread_gate.start()
+    gate[:, wide_cols(w)] = gates[w]
+
+    plane_dy.forward()
+    state[...] = jnp.zeros_like(state)
+    spread_attn = Spread(k, lambda t: attn_s.at[t], lambda s: attn.at[:, wide_cols(s)])
+
+    def attend(b, carry):
+        rows = at(b * BLOCK, BLOCK)
+        mask = doc_mask(cols, rowdoc, decay, rows, b)
+        for h in range(2):
+            lanes = slice(h * HEAD, (h + 1) * HEAD)
+            q = qkv[rows, h * HEAD : (h + 1) * HEAD]
+            key = qkv[rows, head_cols + h * HEAD : head_cols + (h + 1) * HEAD]
+            v = qkv[rows, 2 * head_cols + h * HEAD : 2 * head_cols + (h + 1) * HEAD]
+            probs = jnp.where(mask, dot_rt(q, key) * decay[h], 0.0).astype(BF)
+            before = state[h]
+            before_bf = before.astype(BF)
+            sin[b, h] = before_bf
+            entry = cols[rows, 1 + h : 2 + h]
+            tail = cols[rows, 3 + h : 4 + h]
+            out = dot(probs, v) + entry * dot(q, before_bf)
+            attn_s[b, :, lanes] = out.astype(BF)
+            tailed = (key.astype(F32) * tail).astype(BF)
+            state[h] = passing[pl.ds(2 * b + h, 1), :] * before + dot_lt(tailed, v)
+
+        @pl.when(b != w)
+        def _():
+            d = lax.rem(b - w + WIDE, WIDE)
+            base = spread_attn.base
+            k.remote(attn_s.at[b], attn.at[:, wide_cols(w)], base + d, base + d, wide=b).start()
+
+        @pl.when(b == w)
+        def _():
+            attn[:, wide_cols(w)] = attn_s[b]
+
+        return carry
+
+    lax.fori_loop(0, WIDE, attend, 0)
+    for d in spread_attn.distances():
+        to = lax.rem(w + d, WIDE)
+        k.sent.append(
+            k.remote(
+                attn_s.at[to], attn.at[:, wide_cols(w)], spread_attn.base + d, spread_attn.base + d,
+                wide=to,
+            )
+        )
+    keep_sin = k.keep(sin, sin_o)
+    for s in (k.ws, k.wx + 1 - 2 * core, k.wy + 1 - 2 * core, k.wd + 1 - 2 * core):
+        twin_out.wait(s)
+    keep_wo = k.keep(wout, wo_o)
+    spread_gate.finish()
+    spread_attn.finish()
+    keep_attn = k.keep(attn, attn_o)
+    keep_gate = k.keep(gate, gate_o)
+
+    def mix(rows):
+        a = attn[rows, :].astype(F32)
+        mixed[rows, :] = (a * row_scale(a) * gate[rows, :].astype(F32)).astype(BF)
+
+    row_chunks(tok, mix)
+    keep_mixed = k.keep(mixed, mixed_o)
+
+    def project_out(j, carry):
+        lanes = at(j * 512, 512)
+        part = dot(mixed[...], wout[:, :, :, lanes].reshape(-1, 512))
+        x1[:, lanes] = x_ref[:, lanes].astype(F32) + part
+        return carry
+
+    lax.fori_loop(0, x1.shape[1] // 512, project_out, 0)
+    keep_x1 = k.keep(x1, x1_o)
+
+    def norm_mid(rows):
+        v = x1[rows, :]
+        x1n[rows, :] = (v * row_scale(v)).astype(BF)
+
+    row_chunks(tok, norm_mid)
+    k.keep(x1n, x1n_o.at[chip]).wait()
+    plane_x1n.start()
+    line_fv.forward()
+    line_fg.forward()
+    plane_x1n.forward()
+    plane_dy.finish_near()
+    plane_dy.finish_far()
+    line_fv.finish()
+    twin_fv.send(core)
+    line_fg.finish()
+    twin_fg.send(core)
+    plane_x1n.finish_near()
+    plane_x1n.finish_far()
+    twin_fv.wait(other)
+    twin_fg.wait(other)
+    for copy in (
+        keep_xn, keep_pre, keep_wqk, keep_wvg, keep_qkv, keep_sin, keep_wo, keep_attn, keep_gate,
+        keep_mixed, keep_x1,
+    ):
+        copy.wait()
+    k.drain()
+
+
+def forward(tokens, weights, dy, cols, rowdoc, passing, decay):
+    tok, width = tokens.shape
+    shard = weights[0].shape[0]
+    full = WIDE * tok
+    ff = weights[5].shape[1] // CHIPS
+    two = 2 * HEAD
+
+    def hbm(shape, dtype=BF):
+        return jax.ShapeDtypeStruct(shape, dtype)
+
+    out_shape = (
+        hbm((WIDE, tok, width)),
+        hbm((WIDE, NARROW, shard, 2 * two)),
+        hbm((WIDE, NARROW, shard, 2 * two)),
+        hbm((WIDE, NARROW, shard, width)),
+        hbm((CHIPS, 2, NARROW, shard, ff)),
+        hbm((CHIPS, 2, NARROW, shard, ff)),
+        hbm((CHIPS, tok, width)),
+        hbm((full, 2 * two), F32),
+        hbm((full, 3 * two)),
+        hbm((WIDE, 2, HEAD, HEAD)),
+        hbm((tok, width)),
+        hbm((tok, width)),
+        hbm((tok, width)),
+        hbm((tok, width), F32),
+        hbm((CHIPS, tok, width)),
+    )
+    scratch = [
+        pltpu.VMEM((WIDE, tok, width), BF),
+        pltpu.VMEM((WIDE, NARROW, shard, 2 * two), BF),
+        pltpu.VMEM((WIDE, NARROW, shard, 2 * two), BF),
+        pltpu.VMEM((WIDE, NARROW, shard, width), BF),
+        pltpu.VMEM((full, 2 * two), F32),
+        pltpu.VMEM((full, 3 * two), BF),
+        pltpu.VMEM((WIDE, tok, two), BF),
+        pltpu.VMEM((WIDE, 2, HEAD, HEAD), BF),
+        pltpu.VMEM((2, HEAD, HEAD), F32),
+        pltpu.VMEM((WIDE, tok, two), BF),
+        pltpu.VMEM((tok, width), BF),
+        pltpu.VMEM((tok, width), BF),
+        pltpu.VMEM((tok, width), BF),
+        pltpu.VMEM((tok, width), F32),
+        pltpu.VMEM((tok, width), BF),
+        pltpu.SemaphoreType.DMA((136,)),
+        pltpu.SemaphoreType.DMA((136,)),
+        pltpu.SemaphoreType.DMA((24,)),
+    ]
+    return pl.pallas_call(
+        forward_kernel,
+        out_shape=out_shape,
+        in_specs=[VMEM] + [ANY] * 8 + [VMEM] * 4,
+        out_specs=(ANY,) * len(out_shape),
+        scratch_shapes=scratch,
+        compiler_params=pltpu.CompilerParams(
+            collective_id=0, has_side_effects=True, vmem_limit_bytes=60 * 2**20
+        ),
+        cost_estimate=pl.CostEstimate(flops=2 * 10**10, bytes_accessed=10**8, transcendentals=0),
+    )(tokens, *weights, dy, cols, rowdoc, passing, decay)
+
+
+def prepare(doc_starts, length):
+    starts = lax.dynamic_slice_in_dim(doc_starts, lax.axis_index("narrow"), 1, 0)[0]
+    blocks = length // BLOCK
+    positions = jnp.arange(length, dtype=jnp.int32)
+    doc_ids = jnp.sum((starts[None, :] <= positions[:, None]).astype(jnp.int32), axis=1)
+    doc_ids = doc_ids.reshape(blocks, BLOCK).astype(F32)
+    firsts = jnp.arange(blocks, dtype=jnp.int32) * BLOCK - 1
+    prev_ids = jnp.sum((starts[None, :] <= firsts[:, None]).astype(jnp.int32), axis=1).astype(F32)
+    slopes = lax.dynamic_slice_in_dim(head_slopes(), lax.axis_index("wide") * 2, 2, 0)
+    offsets = jnp.arange(BLOCK, dtype=F32)
+    lags = offsets[:, None] - offsets[None, :]
+    decay = jnp.exp(-slopes[:, None, None] * jnp.maximum(lags, 0.0)[None])
+    continues = (doc_ids == prev_ids[:, None]).astype(F32)
+    entry = continues[..., None] * jnp.exp(-slopes[None, :] * (offsets[:, None] + 1.0))
+    tail = (doc_ids == doc_ids[:, -1:]).astype(F32)[..., None] * jnp.exp(
+        -slopes[None, :] * (BLOCK - 1.0 - offsets)[:, None]
+    )
+    passing = continues[:, -1:] * jnp.exp(-slopes * BLOCK)
+    cols = jnp.concatenate([doc_ids[..., None], entry, tail], axis=-1).reshape(length, 5)
+    cols = jnp.pad(cols, ((0, 0), (0, HEAD - 5)))
+    passing = jnp.broadcast_to(passing.reshape(-1, 1), (2 * blocks, HEAD))
+    return cols, doc_ids, passing, decay
+
+
+TWINS = [[2 * i, 2 * i + 1] for i in range(CHIPS)]
+SAME = [[2 * i + j for i in range(CHIPS)] for j in range(2)]
+
+
+def local_box(
+    tokens, doc_starts, wq, wk, wv, wg, wo, fv, fg, fo, cotangent,
+):
+    length = WIDE * tokens.shape[1]
+    cols, rowdoc, passing, decay = prepare(doc_starts, length)
+    (xn, wqk, wvg, w_out, fvw, fgw, dy, pre, qkv, sin, attn, gate, mixed, middle, x1n) = forward(
+        tokens[0], (wq, wk, wv, wg, wo, fv, fg), cotangent[0], cols, rowdoc, passing, decay
+    )
+    two = 2 * HEAD
+    blocks = WIDE
+
+    def split_heads(values):
+        return values.reshape(blocks, BLOCK, 2, HEAD)
+
+    def to_heads(values):
+        return lax.all_to_all(values, "wide", split_axis=1, concat_axis=0, tiled=True)
+
+    normed_bf = xn.reshape(length, -1)
+    wqk, wvg, w_out = (a.reshape(normed_bf.shape[1], -1) for a in (wqk, wvg, w_out))
+    fvw, fgw = (a.reshape(normed_bf.shape[1], -1) for a in (fvw, fgw))
+    inputs = tokens[0].astype(F32)
+    normed, in_scale = normalize(inputs)
+    middle_n, middle_scale = normalize(middle)
+    attn_n, attn_scale = normalize(attn.astype(F32))
+    upstream = cotangent[0]
+
+    fow = lax.all_gather(fo, "narrow", axis=0, tiled=True)
+    fow = lax.all_gather(fow, "wide", axis=0, tiled=True, axis_index_groups=TWINS)
+    x4 = x1n.reshape(-1, normed_bf.shape[1])
+    dy4 = dy.reshape(x4.shape)
+    ffn_val, ffn_gat = matmul(x4, fvw), matmul(x4, fgw)
+    ffn_mix = (ffn_val * ffn_gat).astype(BF)
+
+    def scatter4(v):
+        return lax.psum_scatter(
+            v.astype(BF), "wide", scatter_dimension=0, tiled=True, axis_index_groups=SAME
+        ).astype(F32)
+
+    result = middle + scatter4(matmul(ffn_mix, fow))
+    grad_fout = weight_grad(ffn_mix, dy4).astype(BF)
+    d_mix = matmul_right_t(dy4, fow)
+    d_val = (d_mix * ffn_gat).astype(BF)
+    d_gat = (d_mix * ffn_val).astype(BF)
+    d_middle_n = scatter4(matmul_right_t(d_val, fvw) + matmul_right_t(d_gat, fgw))
+    d_middle = upstream.astype(F32) + normalize_back(middle_n, middle_scale, d_middle_n)
+    d_branch = d_middle.astype(BF)
+    grad_out = weight_grad(mixed, d_branch)
+    d_mixed = matmul_right_t(d_branch, w_out)
+    d_gate = to_heads((d_mixed * attn_n).astype(BF))
+    d_attn = to_heads(
+        normalize_back(attn_n, attn_scale, d_mixed * gate.astype(F32)).astype(BF)
+    )
+
+    doc_ids = rowdoc
+    offsets = jnp.arange(BLOCK)
+    within = (doc_ids[:, :, None] == doc_ids[:, None, :]) & (offsets[:, None] >= offsets[None, :])
+    block_mask = jnp.where(within[:, None], decay[None], 0.0)
+    entry_scale = cols[:, 1:3].reshape(blocks, BLOCK, 2)
+    tail_scale = cols[:, 3:5].reshape(blocks, BLOCK, 2)
+    passing = passing[:, 0].reshape(blocks, 2)
+    queries, keys, values = (split_heads(qkv[:, i * two : (i + 1) * two]) for i in range(3))
+    query_pre, key_pre = pre[:, :two], pre[:, two:]
+    d_heads = split_heads(d_attn)
+    probs = (ein("bihe,bjhe->bhij", queries, keys) * block_mask).astype(BF)
+    tail_keys = (keys.astype(F32) * tail_scale[..., None]).astype(BF)
+    d_probs = ein("bihe,bjhe->bhij", d_heads, values)
+    d_scores = (d_probs * block_mask).astype(BF)
+    d_query = ein("bhij,bjhe->bihe", d_scores, keys)
+    d_key = ein("bhij,bihe->bjhe", d_scores, queries)
+    d_value = ein("bhij,bihe->bjhe", probs, d_heads)
+    d_query = d_query + entry_scale[..., None] * ein("bihf,bhef->bihe", d_heads, sin)
+    entry_queries = (queries.astype(F32) * entry_scale[..., None]).astype(BF)
+    grad_in = ein("bihe,bihf->bhef", entry_queries, d_heads)
+    state = jnp.zeros((2, HEAD, HEAD), F32)
+    leaving = [None] * blocks
+    for b in reversed(range(blocks)):
+        leaving[b] = state
+        state = passing[b][:, None, None] * state + grad_in[b]
+    block_out = jnp.stack(leaving).astype(BF)
+    d_key = d_key + tail_scale[..., None] * ein("bjhf,bhef->bjhe", values, block_out)
+    d_value = d_value + ein("bjhe,bhef->bjhf", tail_keys, block_out)
+    dq_pre = (d_query.reshape(query_pre.shape) * silu_slope(query_pre)).astype(BF)
+    dk_pre = (d_key.reshape(key_pre.shape) * silu_slope(key_pre)).astype(BF)
+    dv_pre = d_value.reshape(query_pre.shape).astype(BF)
+    d_qk = jnp.concatenate([dq_pre, dk_pre], axis=1)
+    d_vg = jnp.concatenate([dv_pre, d_gate], axis=1)
+    d_normed = lax.psum_scatter(
+        (matmul_right_t(d_qk, wqk) + matmul_right_t(d_vg, wvg)).astype(BF),
+        "wide", scatter_dimension=0, tiled=True,
+    ).astype(F32)
+    d_inputs = d_middle + normalize_back(normed, in_scale, d_normed)
+
+    def narrow_sum(v):
+        return lax.psum_scatter(v, "narrow", scatter_dimension=0, tiled=True)
+
+    def head_grads(left, right):
+        g = weight_grad(left, right).astype(BF).reshape(WIDE, NARROW, -1, right.shape[1])
+        g = narrow_sum(g.swapaxes(0, 1).reshape(-1, right.shape[1]))
+        g = lax.all_to_all(
+            g.reshape(WIDE, -1, 2, two), "wide", split_axis=0, concat_axis=0, tiled=True
+        ).reshape(WIDE, -1, 2, two)
+        g = g.transpose(2, 1, 0, 3).astype(F32)
+        return g[0].reshape(g.shape[1], -1), g[1].reshape(g.shape[1], -1)
+
+    def ff_grads(left, right):
+        g = weight_grad(left, right).astype(BF).reshape(CHIPS, 2, NARROW, -1, right.shape[1])
+        g = g.transpose(1, 2, 0, 3, 4).reshape(-1, right.shape[1])
+        g = lax.psum_scatter(g, "wide", scatter_dimension=0, tiled=True, axis_index_groups=TWINS)
+        g = narrow_sum(g)
+        return lax.all_to_all(
+            g, "wide", split_axis=0, concat_axis=1, tiled=True, axis_index_groups=SAME
+        ).astype(F32)
+
+    g_query, g_key = head_grads(normed_bf, d_qk)
+    g_value, g_gate = head_grads(normed_bf, d_vg)
+    return (
+        result.astype(BF)[None],
+        d_inputs[None],
+        g_query,
+        g_key,
+        g_value,
+        g_gate,
+        lax.psum_scatter(grad_out.astype(BF), BOTH, scatter_dimension=0, tiled=True).astype(F32),
+        ff_grads(x4, d_val),
+        ff_grads(x4, d_gat),
+        narrow_sum(
+            lax.psum_scatter(
+                grad_fout, "wide", scatter_dimension=0, tiled=True, axis_index_groups=TWINS
+            )
+        ).astype(F32),
+    )
+
+
 def solution(mesh):
+    box = (mesh.shape["wide"], mesh.shape["narrow"]) == (WIDE, NARROW)
     tok = P("narrow", "wide", None)
     row = P(BOTH, None)
     return jax.shard_map(
-        local,
+        local_box if box else local,
         mesh=mesh,
         in_specs=(tok, P()) + (row,) * 8 + (tok,),
         out_specs=(tok, tok) + (row,) * 8,

time: 1350 us -> 1080 us (0.80)
  waiting for transfers between devices: 828 us -> 527 us
  Pallas kernels: 0 us -> 226 us
  blocking collectives: 94.6 us -> 0 us
  matrix products: 246 us -> 175 us
  local copies, waits for them, and re-layouts: 80.4 us -> 62.6 us
    all_gather x11 -> x2, waiting for transfers between devices: 367 us -> 58.6 us  [the longest x1 58.6 us: local_box(): fow = lax.all_gather(fo, 'narrow', axis=0, tiled=True)]
    pallas_call x0 -> x1, Pallas kernels: none -> 226 us  [forward(): pl.pallas_call(forward_kernel, out_shape=out_shape, in_specs=[VMEM] + [AN...]
    all_to_all x7 -> x0, blocking collectives: 94.6 us -> none  [the longest x5 58 us: columns(): lax.all_to_all(weight, 'wide', split_axis=1, concat_axis=0, tiled=True)]
    reduce_scatter x11 -> x12, waiting for transfers between devices: 393 us -> 455 us  [the longest x1 184 us: local_box(): lax.psum_scatter(grad_out.astype(BF), BOTH, scatter_dimension=0, tiled=True)]
    all_to_all x9 -> x6, waiting for transfers between devices: 64.7 us -> 11.3 us  [the longest x2 7.35 us: head_grads(): lax.all_to_all(g.reshape(WIDE, -1, 2, two), 'wide', split_axis=0, concat_...]
    dot_general x8 -> x3, matrix products: 69.8 us -> 31.1 us  [matmul(): return jnp.dot(left, right, preferred_element_type=F32)]
    dot_general x8 -> x6, matrix products: 90.5 us -> 69.1 us  [matmul_right_t(): lax.dot_general(left, right, (((1,), (1,)), ((), ())), preferred_element_...]
    convert_element_type x11 -> x4, local copies, waits for them, and re-layouts: 16.8 us -> 3.02 us  [the longest x2 2.43 us: ff_grads(): return lax.all_to_all(g, 'wide', split_axis=0, concat_axis=1, tiled=True,...]
  transfers between devices with their start and end apart: 31 -> 20, of which waited for: 23 -> 11; matrix products, arithmetic and copies ran while one was open for 23% -> 22% of each run, Pallas kernels for 0% -> 21%
where the time goes in v2:
time: 1080 us; the launch traced here: 1070 us
  waiting for transfers between devices  527 us (49%)
  Pallas kernels  226 us (21%)
  matrix products  175 us (16%)
  local copies, waits for them, and re-layouts  62.6 us (6%)
  other arithmetic  35.2 us (3%)
  starting transfers between devices  26.4 us (2%)
  between operations  15 us (1%)
    pallas_call x1, Pallas kernels, forward(): pl.pallas_call(forward_kernel, out_shape=out_shape, in_specs=[VMEM] + [AN...  226 us
    reduce_scatter x1, waiting for transfers between devices, local_box(): lax.psum_scatter(grad_out.astype(BF), BOTH, scatter_dimension=0, tiled=True)  184 us
    reduce_scatter x5, waiting for transfers between devices, narrow_sum(): return lax.psum_scatter(v, 'narrow', scatter_dimension=0, tiled=True)  148 us
    dot_general x6, matrix products, matmul_right_t(): lax.dot_general(left, right, (((1,), (1,)), ((), ())), preferred_element_...  69.1 us
    reduce_scatter x1, waiting for transfers between devices, local_box(): lax.psum_scatter((matmul_right_t(d_qk, wqk) + matmul_right_t(d_vg, wvg))....  67.8 us
    all_gather x1, waiting for transfers between devices, local_box(): fow = lax.all_gather(fo, 'narrow', axis=0, tiled=True)  58.6 us
    reduce_scatter x2, waiting for transfers between devices, scatter4(): lax.psum_scatter(v.astype(BF), 'wide', scatter_dimension=0, tiled=True, a...  54.9 us
    dot_general x6, matrix products, weight_grad(): lax.dot_general(left, right, (((0,), (0,)), ((), ())), preferred_element_...  53.7 us
  transfers between devices with their start and end apart: 20, of which 11 were waited for; matrix products, arithmetic and copies ran while one was open for 22% of the time, Pallas kernels for 21%

profile of v2, /device:TPU:0, one launch (start us, length us, event | category | flops | bytes accessed | tf_op | source)
XLA Modules:
  0.0 1067.4 jit_solution(16060584242041238101)
XLA Ops:
  12.9 58.6 %all-gather.3.cloned.1.call-done = bf16[704,2048]{1,0:T(8,128)(2,1)} async-done(((bf16[176,2048]{1,0:T(8,128)(2,1)}), bf16[704,2048]{1,0:T(8,128)(2,1)}) %all-gather.3.cloned.1.call-update) | async-done | bytes 2883600 | tf_op jit(solution)/shard_map/all_gather | solution.py:815
  72.3 225.8 %shard_map.186 = (bf16[8,256,2048]{2,1,0:T(8,128)(2,1)}, bf16[8,4,64,512]{3,2,1,0:T(8,128)(2,1)}, bf16[8,4,64,512]{3,2,1,0:T(8,128)(2,1)}, bf16[8,4,64,2048]{3,2...) custom-call(bf16[256,2048]{1,0:T(8,128)(2,1)} %bitcast.166, ...), custom_call_target="tpu_custom_call" | custom-call | flops 20000000000 | bytes 100000000 | tf_op jit(solution)/shard_map/pallas_call | solution.py:748
  298.1 11.8 %fusion.49 = f32[1024,1408]{1,0:T(8,128)} fusion(bf16[1024,2048]{1,0:T(8,128)(2,1)} %bitcast.207, bf16[2048,1408]{1,0:T(8,128)(2,1)} %bitcast.201), kind=kOutput, calls=%fused_computation.144 | convolution fusion | flops 5905580032 | bytes 15728640 | tf_op jit(solution)/shard_map/dot_general | solution.py:35
  309.9 8.4 fusion.48
  318.3 14.0 %multiply_convert_fusion = (bf16[1024,1408]{1,0:T(8,128)(2,1)S(1)}, bf16[1024,1408]{1,0:T(8,128)(2,1)}, bf16[1024,1408]{1,0:T(8,128)(2,1)S(1)}) fusion(f32[1024,1408]{1,0:T(8,128)} %fusion.48, f32[1024,1408]{1,0:T(8,128)} %fusion.49, bf16[1024,2048]{1,0:T(8,128)(2,1)} %bitcast.205, bf16[1408,2048]{1,0:T(8,128)(2,1)} %all-gather.5.cloned.1.call-done), kind=kOutput, calls=%fused_computation.8 | convolution fusion | flops 5914230784 | bytes 30146560 | tf_op jit(solution)/shard_map/dot_general | solution.py:39
  332.3 10.8 %fusion.50 = f32[1024,2048]{1,0:T(8,128)S(1)} fusion(bf16[1024,1408]{1,0:T(8,128)(2,1)S(1)} %get-tuple-element.48, bf16[2048,1408]{1,0:T(8,128)(2,1)} %bitcast.203), kind=kOutput, calls=%fused_computation.145 | convolution fusion | flops 5905580032 | bytes 17039360 | tf_op jit(solution)/shard_map/dot_general | solution.py:39
  343.1 10.9 %add_convert_fusion.1 = bf16[1024,2048]{1,0:T(8,128)(2,1)} fusion(f32[1024,2048]{1,0:T(8,128)S(1)} %fusion.50, bf16[1024,1408]{1,0:T(8,128)(2,1)S(1)} %get-tuple-element.46, bf16[2048,1408]{1,0:T(8,128)(2,1)} %bitcast.202), kind=kOutput, calls=%fused_computation.1 | convolution fusion | flops 5909774336 | bytes 21233664 | tf_op jit(solution)/shard_map/dot_general | solution.py:39
  354.1 10.9 %convolution_convert_fusion.4 = bf16[1024,2048]{1,0:T(8,128)(2,1)} fusion(bf16[1024,1408]{1,0:T(8,128)(2,1)} %get-tuple-element.47, bf16[1408,2048]{1,0:T(8,128)(2,1)} %all-gather.5.cloned.1.call-done), kind=kOutput, calls=%fused_computation.13 | convolution fusion | flops 5907677184 | bytes 12845056 | tf_op jit(solution)/shard_map/dot_general | solution.py:35
  365.1 9.4 convolution_convert_fusion.2
  374.5 3.0 copy.146
  377.6 10.0 convolution_convert_fusion.1
  387.6 3.0 copy.148
  390.7 11.2 %convolution_convert_fusion = bf16[1408,2048]{1,0:T(8,128)(2,1)} fusion(bf16[1024,1408]{1,0:T(8,128)(2,1)} %get-tuple-element.47, bf16[1024,2048]{1,0:T(8,128)(2,1)} %bitcast.206), kind=kOutput, calls=%fused_computation.2 | convolution fusion | flops 5908463616 | bytes 12845056 | tf_op jit(solution)/shard_map/dot_general | solution.py:43
  409.0 54.1 %reduce-scatter.13.cloned.1.call-done = bf16[256,2048]{1,0:T(8,128)(2,1)} async-done(((bf16[1024,2048]{1,0:T(8,128)(2,1)}), bf16[256,2048]{1,0:T(8,128)(2,1)}) %reduce-scatter.13.cloned.1.call-update) | async-done | bytes 1048592 | tf_op jit(solution)/shard_map/reduce_scatter | solution.py:823
  463.1 4.0 fusion.8
  467.1 6.0 fusion.10
  476.1 4.4 all-to-all-start
  486.1 2.4 copy.127
  492.1 3.9 all-to-all-done
  496.0 4.2 all-to-all-start.1
  507.4 5.2 fusion.24
  512.6 2.7 fusion.25
  519.5 8.5 convolution_convert_fusion.5
  531.8 2.7 fusion
  536.5 2.9 fusion.22
  539.4 4.2 copy.131
  543.7 2.5 fusion.51
  546.2 3.0 fusion.23
  549.2 4.1 copy.126
  553.3 4.2 fusion.21
  557.5 9.0 convolution_convert_fusion.6
  570.2 12.2 %fusion.26 = f32[2048,2048]{1,0:T(8,128)} fusion(bf16[2048,512]{1,0:T(8,128)(2,1)} %bitcast.212, bf16[2048,256]{1,0:T(8,128)(2,1)} %copy-done.16, bf16[2048,256]{1,0:T(8,128)(2,1)S(1)} %get-tuple-element.49), kind=kOutput, calls=%fused_computation.63 | convolution fusion | flops 4299161600 | bytes 20971520 | tf_op jit(solution)/shard_map/dot_general | solution.py:39
  582.4 15.2 %add_convert_fusion = bf16[2048,2048]{1,0:T(8,128)(2,1)} fusion(f32[2048,2048]{1,0:T(8,128)} %fusion.26, bf16[2048,512]{1,0:T(8,128)(2,1)} %bitcast.211, bf16[2048,256]{0,1:T(8,128)(2,1)} %copy.139, bf16[2048,256]{0,1:T(8,128)(2,1)} %bitcast.186), kind=kOutput, calls=%fused_computation | convolution fusion | flops 4307550208 | bytes 29360128 | tf_op jit(solution)/shard_map/dot_general | solution.py:39
  598.8 5.7 convolution_convert_fusion.3
  606.6 4.1 all-to-all-start.3
  611.1 10.0 reduce-scatter.19.cloned.1.call-done
  623.0 4.4 all-to-all-start.2
  627.4 2.4 convert_bitcast_fusion.2
  629.8 7.3 all-to-all-done.2
  637.1 41.7 %reduce-scatter.27.cloned.1.call-done = bf16[256,1408]{1,0:T(8,128)(2,1)} async-done(((bf16[1024,1408]{1,0:T(8,128)(2,1)}), bf16[256,1408]{1,0:T(8,128)(2,1)}) %reduce-scatter.27.cloned.1.call-update) | async-done | bytes 720912 | tf_op jit(solution)/shard_map/reduce_scatter | solution.py:882
  678.8 4.2 all-to-all-start.4
  683.0 2.5 convert_bitcast_fusion.3
  687.5 49.8 %reduce-scatter.31.cloned.1.call-done = bf16[256,1408]{1,0:T(8,128)(2,1)} async-done(((bf16[1024,1408]{1,0:T(8,128)(2,1)}), bf16[256,1408]{1,0:T(8,128)(2,1)}) %reduce-scatter.31.cloned.1.call-update) | async-done | bytes 720912 | tf_op jit(solution)/shard_map/reduce_scatter | solution.py:882
  737.3 4.2 all-to-all-start.5
  741.5 2.6 fusion.47
  749.2 46.4 %reduce-scatter.35.cloned.1.call-done = bf16[176,2048]{1,0:T(8,128)(2,1)} async-done(((bf16[704,2048]{1,0:T(8,128)(2,1)}), bf16[176,2048]{1,0:T(8,128)(2,1)}) %reduce-scatter.35.cloned.1.call-update) | async-done | bytes 720912 | tf_op jit(solution)/shard_map/reduce_scatter | solution.py:882
  802.8 67.8 %reduce-scatter.17.cloned.1.call-done = bf16[256,2048]{1,0:T(8,128)(2,1)} async-done(((bf16[2048,2048]{1,0:T(8,128)(2,1)}), bf16[256,2048]{1,0:T(8,128)(2,1)}) %reduce-scatter.17.cloned.1.call-update) | async-done | bytes 1048592 | tf_op jit(solution)/shard_map/reduce_scatter | solution.py:875
  874.4 184.3 %reduce-scatter.23.cloned.1.call-done = bf16[64,2048]{1,0:T(8,128)(2,1)} async-done(((bf16[2048,2048]{1,0:T(8,128)(2,1)}), bf16[64,2048]{1,0:T(8,128)(2,1)}) %reduce-scatter.23.cloned.1.call-update) | async-done | bytes 262160 | tf_op jit(solution)/shard_map/reduce_scatter | solution.py:911
  (194 shorter events, 71.6 us)
Async XLA Ops:
  7.2 64.3 %all-gather.3.cloned.1.call-start = ((), (), s32[]{:S(2)}) async-start(), calls=%async_computation.18 | async-start | bytes 3604480 | tf_op jit(solution)/shard_map/all_gather | solution.py:815
  7.9 310.4 %all-gather.5.cloned.1.call-start = ((), (), s32[]{:S(2)}) async-start(), calls=%async_computation.19 | async-start | bytes 8650752 | tf_op jit(solution)/shard_map/all_gather | solution.py:816
  8.1 4.8 copy-start.19
  8.8 4.1 copy-start.26
  10.5 61.0 %copy-start.21 = (f32[8,256]{1,0:T(8,128)}, f32[8,256]{1,0:T(8,128)S(1)}, u32[]{:S(2)}) copy-start(f32[8,256]{1,0:T(8,128)S(1)} %get-tuple-element.63) | copy-start | bytes 24580
  10.7 60.8 %copy-start.23 = (f32[8,2]{1,0:T(8,128)}, f32[8,2]{1,0:T(8,128)S(1)}, u32[]{:S(2)}) copy-start(f32[8,2]{1,0:T(8,128)S(1)} %broadcast_multiply_fusion.4) | copy-start | bytes 196
  71.6 335.7 %reduce-scatter.15.cloned.1.call-start = ((), (), s32[]{:S(2)}) async-start(), calls=%async_computation.21 | async-start | bytes 5242880 | tf_op jit(solution)/shard_map/reduce_scatter | solution.py:823
  298.1 11.8 %copy-start.30 = (bf16[4,2,4,64,1408]{4,3,2,1,0:T(8,128)(2,1)S(1)}, bf16[4,2,4,64,1408]{4,3,2,1,0:T(8,128)(2,1)}, u32[]{:S(2)}) copy-start(bf16[4,2,4,64,1408]{4,3,2,1,0:T(8,128)(2,1)} %get-tuple-element.27) | copy-start | bytes 17301508
  298.1 11.8 %copy-start.31 = (bf16[4,256,2048]{2,1,0:T(8,128)(2,1)S(1)}, bf16[4,256,2048]{2,1,0:T(8,128)(2,1)}, u32[]{:S(2)}) copy-start(bf16[4,256,2048]{2,1,0:T(8,128)(2,1)} %get-tuple-element.26) | copy-start | bytes 12582916
  332.3 10.8 %copy-start.33 = (bf16[1024,1408]{1,0:T(8,128)(2,1)}, bf16[1024,1408]{1,0:T(8,128)(2,1)S(1)}, u32[]{:S(2)}) copy-start(bf16[1024,1408]{1,0:T(8,128)(2,1)S(1)} %get-tuple-element.48) | copy-start | bytes 8650756
  332.3 10.8 %copy-start.32 = (bf16[1024,1408]{1,0:T(8,128)(2,1)}, bf16[1024,1408]{1,0:T(8,128)(2,1)S(1)}, u32[]{:S(2)}) copy-start(bf16[1024,1408]{1,0:T(8,128)(2,1)S(1)} %get-tuple-element.46) | copy-start | bytes 8650756
  354.0 109.0 %reduce-scatter.13.cloned.1.call-start = ((), (), s32[]{:S(2)}) async-start(), calls=%async_computation.20 | async-start | bytes 5242880 | tf_op jit(solution)/shard_map/reduce_scatter | solution.py:823
  365.0 203.0 %reduce-scatter.25.cloned.1.call-start = ((), (), s32[]{:S(2)}) async-start(), calls=%async_computation.26 | async-start | bytes 8650752 | tf_op jit(solution)/shard_map/reduce_scatter | solution.py:896
  377.6 191.1 %reduce-scatter.29.cloned.1.call-start = ((), (), s32[]{:S(2)}) async-start(), calls=%async_computation.28 | async-start | bytes 8650752 | tf_op jit(solution)/shard_map/reduce_scatter | solution.py:896
  390.6 178.8 %reduce-scatter.33.cloned.1.call-start = ((), (), s32[]{:S(2)}) async-start(), calls=%async_computation.30 | async-start | bytes 8650752 | tf_op jit(solution)/shard_map/reduce_scatter | solution.py:915
  401.8 1.9 copy-start.2
  401.8 2.8 copy-start.12
  407.2 55.8 %copy-start.6 = (bf16[256,2048]{1,0:T(8,128)(2,1)S(1)}, bf16[256,2048]{1,0:T(8,128)(2,1)}, u32[]{:S(2)}) copy-start(bf16[256,2048]{1,0:T(8,128)(2,1)} %reduce-scatter.15.cloned.1.call-done) | copy-start | bytes 3145732
  463.1 4.0 copy-start.10
  463.1 4.0 copy-start.17
  476.1 19.9 %all-to-all-start = ((bf16[256,8,256]{0,2,1:T(8,128)(2,1)}), bf16[256,8,256]{0,2,1:T(8,128)(2,1)}, u32[]{:S(2)}, u32[]{:S(2)}) async-start(bf16[256,8,256]{0,2,1:T(8,128)(2,1)} %bitcast.12), calls=%async_computation.2 | async-start | bytes 2097152 | tf_op jit(solution)/shard_map/all_to_all | solution.py:804
  483.9 4.6 copy-start.24
  483.9 4.6 copy-start.22
  483.9 4.6 copy-start.29
  483.9 4.6 copy-start.25
  483.9 4.6 copy-start.27
  483.9 4.7 copy-start.20
  496.0 21.3 %all-to-all-start.1 = ((bf16[256,8,256]{2,0,1:T(8,128)(2,1)}), bf16[256,8,256]{2,0,1:T(8,128)(2,1)}, u32[]{:S(2)}, u32[]{:S(2)}) async-start(bf16[256,8,256]{2,0,1:T(8,128)(2,1)} %bitcast.173), calls=%async_computation.3 | async-start | bytes 2097152 | tf_op jit(solution)/shard_map/all_to_all | solution.py:804
  500.2 104.3 %reduce-scatter.21.cloned.1.call-start = ((), (), s32[]{:S(2)}) async-start(), calls=%async_computation.24 | async-start | bytes 2621440 | tf_op jit(solution)/shard_map/reduce_scatter | solution.py:882
  529.6 91.4 %reduce-scatter.19.cloned.1.call-start = ((), (), s32[]{:S(2)}) async-start(), calls=%async_computation.23 | async-start | bytes 2621440 | tf_op jit(solution)/shard_map/reduce_scatter | solution.py:882
  534.6 2.0 copy-start.11
  539.4 4.2 copy-start.4
  543.7 2.5 copy-start.18
  557.5 9.0 copy-start.16
  568.0 110.8 %reduce-scatter.27.cloned.1.call-start = ((), (), s32[]{:S(2)}) async-start(), calls=%async_computation.27 | async-start | bytes 3604480 | tf_op jit(solution)/shard_map/reduce_scatter | solution.py:882
  568.6 168.7 %reduce-scatter.31.cloned.1.call-start = ((), (), s32[]{:S(2)}) async-start(), calls=%async_computation.29 | async-start | bytes 3604480 | tf_op jit(solution)/shard_map/reduce_scatter | solution.py:882
  569.3 226.3 %reduce-scatter.35.cloned.1.call-start = ((), (), s32[]{:S(2)}) async-start(), calls=%async_computation.31 | async-start | bytes 3604480 | tf_op jit(solution)/shard_map/reduce_scatter | solution.py:882
  569.9 300.7 %reduce-scatter.17.cloned.1.call-start = ((), (), s32[]{:S(2)}) async-start(), calls=%async_computation.22 | async-start | bytes 9437184 | tf_op jit(solution)/shard_map/reduce_scatter | solution.py:875
  597.6 461.0 %reduce-scatter.23.cloned.1.call-start = ((), (), s32[]{:S(2)}) async-start(), calls=%async_computation.25 | async-start | bytes 8650752 | tf_op jit(solution)/shard_map/reduce_scatter | solution.py:911
  604.5 6.2 copy-start.3
  606.6 16.4 %all-to-all-start.3 = ((bf16[8,64,2,256]{3,2,1,0:T(2,128)(2,1)}), bf16[8,64,2,256]{3,2,1,0:T(2,128)(2,1)}, u32[]{:S(2)}, u32[]{:S(2)}) async-start(bf16[8,64,2,256]{3,2,1,0:T(2,128)(2,1)} %reshape.417), calls=%async_computation.8 | async-start | bytes 1048576 | tf_op jit(solution)/shard_map/all_to_all | solution.py:887
  623.0 14.2 %all-to-all-start.2 = ((bf16[8,64,2,256]{3,2,1,0:T(2,128)(2,1)}), bf16[8,64,2,256]{3,2,1,0:T(2,128)(2,1)}, u32[]{:S(2)}, u32[]{:S(2)}) async-start(bf16[8,64,2,256]{3,2,1,0:T(2,128)(2,1)} %reshape.414), calls=%async_computation.6 | async-start | bytes 1048576 | tf_op jit(solution)/shard_map/all_to_all | solution.py:887
  678.8 58.5 %all-to-all-start.4 = ((bf16[4,64,1408]{2,1,0:T(8,128)(2,1)}), bf16[4,64,1408]{2,1,0:T(8,128)(2,1)}, u32[]{:S(2)}, u32[]{:S(2)}) async-start(bf16[4,64,1408]{2,1,0:T(8,128)(2,1)} %bitcast.188), calls=%async_computation.12 | async-start | bytes 1441792 | tf_op jit(solution)/shard_map/all_to_all | solution.py:898
  683.0 2.5 copy-start.7
  737.3 63.1 %all-to-all-start.5 = ((bf16[4,64,1408]{2,1,0:T(8,128)(2,1)}), bf16[4,64,1408]{2,1,0:T(8,128)(2,1)}, u32[]{:S(2)}, u32[]{:S(2)}) async-start(bf16[4,64,1408]{2,1,0:T(8,128)(2,1)} %bitcast.187), calls=%async_computation.15 | async-start | bytes 1441792 | tf_op jit(solution)/shard_map/all_to_all | solution.py:898
  741.5 2.7 copy-start.14
  741.5 4.0 copy-start.13
  872.5 188.0 %copy-start.1 = (s32[4,4]{1,0:T(4,128)S(1)}, s32[4,4]{1,0:T(4,128)}, u32[]{:S(2)}) copy-start(s32[4,4]{1,0:T(4,128)} %param.12) | copy-start | bytes 196
  (6 other events, 7.0 us)
Sparse Core Ops, SparseCore 0:
  9.6 61.8 all-gather.2
  73.0 14.6 all-gather.4
  354.2 53.0 reduce-scatter.14
  410.3 52.6 reduce-scatter.12
  465.2 13.7 reduce-scatter.24
  481.3 15.0 reduce-scatter.28
  498.7 15.0 reduce-scatter.32
  529.7 45.1 reduce-scatter.20
  577.8 43.1 reduce-scatter.18
  623.3 55.4 reduce-scatter.26
  681.2 56.0 reduce-scatter.30
  739.5 56.0 reduce-scatter.34
  799.5 71.1 reduce-scatter.16
  872.8 185.8 reduce-scatter.22

commit v3 on v2

--- a/solution.py
+++ b/solution.py
@@ -310,10 +310,11 @@
             device_id_type=MESH,
         )
 
-    def go(self, src, dst, send, recv, wide=None, narrow=None):
+    def go(self, src, dst, send, recv, wide=None, narrow=None, record=True):
         copy = self.remote(src, dst, send, recv, wide, narrow)
         copy.start()
-        self.sent.append(copy)
+        if record:
+            self.sent.append(copy)
 
     def arrived(self, ref, recv):
         self.remote(ref, ref, recv, recv, wide=self.ws).wait_recv()
@@ -413,8 +414,8 @@
 
 
 class Spread:
-    def __init__(self, links, src, dst, peers=WIDE):
-        self.links, self.src, self.dst = links, src, dst
+    def __init__(self, links, src, dst, peers=WIDE, record=True):
+        self.links, self.src, self.dst, self.record = links, src, dst, record
         self.step = 1 if peers == WIDE else 2
         self.base = links.take(WIDE)
 
@@ -425,7 +426,13 @@
         k = self.links
         for d in self.distances():
             to = lax.rem(k.w + d, WIDE)
-            k.go(self.src(to), self.dst(k.w), self.base + d, self.base + d, wide=to)
+            k.go(self.src(to), self.dst(k.w), self.base + d, self.base + d, to, None, self.record)
+
+    def drain(self):
+        k = self.links
+        for d in self.distances():
+            to = lax.rem(k.w + d, WIDE)
+            k.remote(self.src(to), self.dst(k.w), self.base + d, self.base + d, to).wait_send()
 
     def wait(self, d):
         self.links.arrived(self.dst(lax.rem(self.links.w + WIDE - d, WIDE)), self.base + d)
@@ -456,10 +463,10 @@
 
 
 def forward_kernel(
-    x_ref, wq, wk, wv, wg, wo, fv, fg, dy, cols, rowdoc, passing, decay,
-    xn_o, wqk_o, wvg_o, wo_o, fv_o, fg_o, dy_o, pre_o, qkv_o, sin_o, attn_o, gate_o, mixed_o,
+    x_ref, wq, wk, wv, wg, wo, fv, fg, fo, dy, cols, rowdoc, passing, decay,
+    xn_o, wqk_o, wvg_o, wo_o, fv_o, fg_o, fo_o, dy_o, slope_o, qkv_o, sin_o, attn_o, gate_o, mixed_o,
     x1_o, x1n_o,
-    xn, wqk, wvg, wout, pre, qkv, gates, sin, state, attn_s, attn, gate, mixed, x1, x1n,
+    xn, wqk, wvg, wout, slope, qkv, gates, sin, state, attn_s, attn, gate, mixed, x1, x1n,
     send, recv, here,
 ):
     k = Links(send, recv, here)
@@ -483,6 +490,7 @@
     own_ff = [
         k.keep(fv.at[:, chip_cols(chip)], fv_o.at[chip, core, n]),
         k.keep(fg.at[:, chip_cols(chip)], fg_o.at[chip, core, n]),
+        k.keep(fo, fo_o.at[core, n]),
         k.keep(dy, dy_o.at[chip]),
     ]
 
@@ -498,6 +506,7 @@
     line_vg = Line(k, lambda i: wvg.at[:, i])
     line_fv = Line(k, lambda i: fv_o.at[:, core, i])
     line_fg = Line(k, lambda i: fg_o.at[:, core, i])
+    line_fo = Line(k, lambda i: fo_o.at[core, i])
     spreads = []
     for m, (weight, to) in enumerate(((wq, wqk), (wk, wqk), (wv, wvg), (wg, wvg))):
         lanes = pl.ds((m % 2) * head_cols, head_cols)
@@ -526,6 +535,7 @@
     twin_out = Sibling(k, lambda s: wout.at[s], 4)
     twin_fv = Sibling(k, lambda s: fv_o.at[:, s], 1)
     twin_fg = Sibling(k, lambda s: fg_o.at[:, s], 1)
+    twin_fo = Sibling(k, lambda s: fo_o.at[s], 1)
     other = 1 - core
 
     for copy in own:
@@ -578,15 +588,17 @@
     def project_qk(t, carry):
         v = dot(xn[t], wqk[...].reshape(-1, 2 * head_cols))
         rows = at(t * tok, tok)
-        pre[rows, :] = v
-        qkv[rows, 0 : 2 * head_cols] = (v * jax.nn.sigmoid(v)).astype(BF)
+        sigma = jax.nn.sigmoid(v)
+        slope[rows, :] = (sigma * (1.0 + v * (1.0 - sigma))).astype(BF)
+        qkv[rows, 0 : 2 * head_cols] = (v * sigma).astype(BF)
         return carry
 
     lax.fori_loop(0, WIDE, project_qk, 0)
-    keep_pre = k.keep(pre, pre_o)
+    keep_slope = k.keep(slope, slope_o)
     keep_wqk = k.keep(wqk, wqk_o)
     line_vg.finish()
     line_fg.start()
+    line_fo.start()
 
     def project_vg(t, carry):
         v = dot(xn[t], wvg[...].reshape(-1, 2 * head_cols)).astype(BF)
@@ -679,6 +691,7 @@
     plane_x1n.start()
     line_fv.forward()
     line_fg.forward()
+    line_fo.forward()
     plane_x1n.forward()
     plane_dy.finish_near()
     plane_dy.finish_far()
@@ -686,12 +699,15 @@
     twin_fv.send(core)
     line_fg.finish()
     twin_fg.send(core)
+    line_fo.finish()
+    twin_fo.send(core)
     plane_x1n.finish_near()
     plane_x1n.finish_far()
     twin_fv.wait(other)
     twin_fg.wait(other)
+    twin_fo.wait(other)
     for copy in (
-        keep_xn, keep_pre, keep_wqk, keep_wvg, keep_qkv, keep_sin, keep_wo, keep_attn, keep_gate,
+        keep_xn, keep_slope, keep_wqk, keep_wvg, keep_qkv, keep_sin, keep_wo, keep_attn, keep_gate,
         keep_mixed, keep_x1,
     ):
         copy.wait()
@@ -703,6 +719,7 @@
     shard = weights[0].shape[0]
     full = WIDE * tok
     ff = weights[5].shape[1] // CHIPS
+    fo_rows = weights[7].shape[0]
     two = 2 * HEAD
 
     def hbm(shape, dtype=BF):
@@ -715,8 +732,9 @@
         hbm((WIDE, NARROW, shard, width)),
         hbm((CHIPS, 2, NARROW, shard, ff)),
         hbm((CHIPS, 2, NARROW, shard, ff)),
+        hbm((2, NARROW, fo_rows, width)),
         hbm((CHIPS, tok, width)),
-        hbm((full, 2 * two), F32),
+        hbm((full, 2 * two)),
         hbm((full, 3 * two)),
         hbm((WIDE, 2, HEAD, HEAD)),
         hbm((tok, width)),
@@ -730,7 +748,7 @@
         pltpu.VMEM((WIDE, NARROW, shard, 2 * two), BF),
         pltpu.VMEM((WIDE, NARROW, shard, 2 * two), BF),
         pltpu.VMEM((WIDE, NARROW, shard, width), BF),
-        pltpu.VMEM((full, 2 * two), F32),
+        pltpu.VMEM((full, 2 * two), BF),
         pltpu.VMEM((full, 3 * two), BF),
         pltpu.VMEM((WIDE, tok, two), BF),
         pltpu.VMEM((WIDE, 2, HEAD, HEAD), BF),
@@ -748,7 +766,7 @@
     return pl.pallas_call(
         forward_kernel,
         out_shape=out_shape,
-        in_specs=[VMEM] + [ANY] * 8 + [VMEM] * 4,
+        in_specs=[VMEM] + [ANY] * 9 + [VMEM] * 4,
         out_specs=(ANY,) * len(out_shape),
         scratch_shapes=scratch,
         compiler_params=pltpu.CompilerParams(
@@ -756,6 +774,717 @@
         ),
         cost_estimate=pl.CostEstimate(flops=2 * 10**10, bytes_accessed=10**8, transcendentals=0),
     )(tokens, *weights, dy, cols, rowdoc, passing, decay)
+
+
+class LineSum:
+    def __init__(self, links, part, land):
+        self.links, self.part, self.land = links, part, land
+        self.base = links.take(3)
+        self.over = 1 + lax.rem(links.n, 2)
+
+    def relay(self, slot):
+        k, b = self.links, self.base
+        return k.remote(self.part(k.cross), self.land(slot), b, b + slot, narrow=self.over)
+
+    def near(self):
+        k, b = self.links, self.base
+        return k.remote(self.part(k.pair), self.land(0), b + 1, b, narrow=k.pair)
+
+    def distant(self):
+        k, b = self.links, self.base
+        slot = 2 - k.mid
+        return k.remote(self.part(k.far), self.land(slot), b + 2, b + slot, narrow=k.far)
+
+    def start(self):
+        @pl.when(self.links.mid == 0)
+        def _():
+            self.relay(1).start()
+
+        self.distant().start()
+        self.near().start()
+
+    def forward(self, add):
+        k = self.links
+
+        @pl.when(k.mid == 1)
+        def _():
+            k.arrived(self.land(1), self.base + 1)
+            add(self.part(k.cross), self.land(1))
+            self.relay(2).start()
+
+    def finish(self):
+        k = self.links
+        k.arrived(self.land(0), self.base)
+        k.arrived(self.land(2), self.base + 2)
+
+        @pl.when(k.mid == 0)
+        def _():
+            k.arrived(self.land(1), self.base + 1)
+
+    def drain(self):
+        self.relay(1).wait_send()
+        self.distant().wait_send()
+        self.near().wait_send()
+
+
+class PlaneSum:
+    def __init__(self, links, block, corner, near, half):
+        self.links, self.block, self.corner, self.near, self.half = links, block, corner, near, half
+        self.base = links.take(6)
+
+    def rows(self, h):
+        return pl.ds(h * self.half, self.half)
+
+    def copy(self, index):
+        k = self.links
+        chip, h, land, to = (
+            (k.pd, 0, self.corner.at[0], k.wx),
+            (k.pd, 1, self.corner.at[1], k.wy),
+            (k.px, 0, self.near.at[0, self.rows(0)], k.wx),
+            (k.py, 1, self.near.at[1, self.rows(1)], k.wy),
+            (k.px, 1, self.near.at[0, self.rows(1)], k.wx),
+            (k.py, 0, self.near.at[1, self.rows(0)], k.wy),
+        )[index]
+        sem = self.base + index
+        return k.remote(self.block(chip).at[self.rows(h)], land, sem, sem, wide=to)
+
+    def send_far(self):
+        self.copy(0).start()
+        self.copy(1).start()
+
+    def send_x(self):
+        self.copy(2).start()
+
+    def send_y(self):
+        self.copy(3).start()
+
+    def combine(self, add):
+        k = self.links
+        self.copy(1).wait_recv()
+        add(self.block(k.px).at[self.rows(1)], self.corner.at[1])
+        self.copy(4).start()
+        self.copy(0).wait_recv()
+        add(self.block(k.py).at[self.rows(0)], self.corner.at[0])
+        self.copy(5).start()
+
+    def finish(self):
+        for index in range(2, 6):
+            self.copy(index).wait_recv()
+
+    def drain(self):
+        for index in range(6):
+            self.copy(index).wait_send()
+
+
+def backward_kernel(
+    x_in, xn_in, wqk_in, wvg_in, wo_in, fv_in, fg_in, fo_in, dy_in, slope_in, qkv_in, sin_in,
+    attn_in, gate_in, mixed_in, x1_in, x1n_in, cols_in, decay_in, rowdoc, passing,
+    result_o, dx_o, gq_o, gk_o, gv_o, gg_o, go_o, gfv_o, gfg_o, gfo_o,
+    corner, near, twin_fo, twin_ff, twin_wo, twin_xn, land_fo, land_ff, land_wo, land_qk, turn_ff,
+    turn_qk, a_land, g_land,
+    g_fo, g_fv, g_fg, stage, acc, tmp, tmp_ff,
+    send, recv, here,
+):
+    k = Links(send, recv, here)
+    w, n, core, chip = k.w, k.n, k.core, k.chip
+    other = 1 - core
+    tok, width = acc.shape
+    ff = g_fv.shape[-1]
+    fo_rows = land_fo.shape[1]
+    half = tok // 2
+    two = 2 * HEAD
+    order = (k.pd, k.px, k.py, chip)
+
+    def nth(j):
+        flip_x, flip_y = 1 - lax.div(j, 2), 1 - lax.rem(j, 2)
+        return (
+            chip + flip_x * (1 - 2 * lax.rem(chip, 2)) + flip_y * (2 - 4 * lax.div(chip, 2))
+        )
+
+    def fetch(src, dst):
+        copy = pltpu.make_async_copy(src, dst, here.at[0])
+        copy.start()
+        copy.wait()
+
+    def adder(spot):
+        def add(to, land):
+            fetch(land, spot)
+            to[...] = (to[...].astype(F32) + spot[...].astype(F32)).astype(BF)
+
+        return add
+
+    add_half = adder(tmp.at[pl.ds(0, half)])
+    add_fo = adder(tmp.at[pl.ds(0, fo_rows)])
+    add_wo = adder(tmp.at[pl.ds(0, 64)])
+    add_ff = adder(tmp_ff)
+    k.kept.append(None)
+
+    def fo_part(owner, i):
+        return g_fo.at[pl.ds(pl.multiple_of((owner * NARROW + i) * fo_rows, 16), fo_rows)]
+
+    line_fo = LineSum(k, lambda i: fo_part(core, i), lambda s: land_fo.at[s])
+    line_ff = [
+        LineSum(k, lambda i, g=g: g.at[:, i], lambda s, m=m: land_ff.at[m, s])
+        for m, g in enumerate((g_fv, g_fg))
+    ]
+    planes = [
+        PlaneSum(k, lambda q: stage.at[q], corner.at[m], near.at[m], half) for m in range(4)
+    ]
+    plane_mid, plane_res, plane_out, plane_in = planes
+    twin_base = k.take(4 * 5)
+
+    def twin(m, j, src, dst):
+        sem = twin_base + 4 * m + j
+        return k.remote(src, dst, sem, sem, wide=k.ws)
+
+    k.greet()
+
+    def ffn(x1n, dy, fvw, fgw, fow, mix, val, gat, side):
+        loads = [
+            k.keep(x1n_in, x1n), k.keep(fv_in, fvw), k.keep(fg_in, fgw), k.keep(dy_in, dy),
+            k.keep(fo_in, fow),
+        ]
+        for copy in loads:
+            copy.wait()
+        k.met()
+
+        def up(j, carry):
+            v = dot(x1n[j], fvw[...].reshape(width, ff))
+            g = dot(x1n[j], fgw[...].reshape(width, ff))
+            mix[j] = (v * g).astype(BF)
+            val[j] = v.astype(BF)
+            gat[j] = g.astype(BF)
+            return carry
+
+        lax.fori_loop(0, CHIPS, up, 0)
+
+        def fo_grad(rows):
+            left = mix[:, :, rows].reshape(CHIPS * tok, -1)
+            for h in range(2):
+                lanes = slice(h * width // 2, (h + 1) * width // 2)
+                right = dy[:, :, lanes].reshape(CHIPS * tok, -1)
+                g_fo[rows, lanes] = dot_lt(left, right).astype(BF)
+
+        def fo_step(j, carry):
+            fo_grad(at(j * 256, 256))
+            return carry
+
+        lax.fori_loop(0, ff // 256, fo_step, 0)
+        if ff % 256:
+            fo_grad(pl.ds(ff - ff % 256, ff % 256))
+        for i in range(NARROW):
+            twin(0, i, fo_part(other, i), twin_fo.at[i]).start()
+        for i in range(NARROW):
+            copy = twin(0, i, fo_part(other, i), twin_fo.at[i])
+            copy.wait_recv()
+            add_fo(fo_part(core, i), twin_fo.at[i])
+            copy.wait_send()
+        line_fo.start()
+
+        def down(j, carry):
+            q = nth(j)
+            d_mix = dot_rt(dy[q], fow[...].reshape(ff, width))
+            d_val = (d_mix * gat[q].astype(F32)).astype(BF)
+            d_gat = (d_mix * val[q].astype(F32)).astype(BF)
+            val[q] = d_val
+            gat[q] = d_gat
+
+            def back(i, carry):
+                lanes = at(i * 512, 512)
+                d_x = dot_rt(val[q], fvw[i].reshape(512, ff)) + dot_rt(
+                    gat[q], fgw[i].reshape(512, ff)
+                )
+                stage[q, :, lanes] = d_x.astype(BF)
+
+                @pl.when(j == 3)
+                def _():
+                    acc[:, lanes] = d_x
+
+                return carry
+
+            lax.fori_loop(0, width // 512, back, 0)
+
+            for step, push in enumerate((plane_mid.send_far, plane_mid.send_x, plane_mid.send_y)):
+                pl.when(j == step)(push)
+
+            return carry
+
+        lax.fori_loop(0, CHIPS, down, 0)
+        plane_mid.combine(add_half)
+        line_fo.forward(add_fo)
+
+        for m, (d_ff, g_ff) in enumerate(((val, g_fv), (gat, g_fg))):
+
+            def ff_grad(owner):
+                left = x1n[:, :, at(owner * tok, tok)].reshape(CHIPS * tok, tok)
+                g = dot_lt(left, d_ff[...].reshape(CHIPS * tok, ff)).astype(BF)
+                return g.reshape(NARROW, -1, ff)
+
+            def side_step(q, carry):
+                slot = lax.rem(q, 2)
+
+                @pl.when(q >= 2)
+                def _():
+                    twin(1 + m, q - 2, side.at[slot], twin_ff.at[m, q]).wait_send()
+
+                side[slot] = ff_grad(2 * q + other)
+                twin(1 + m, q, side.at[slot], twin_ff.at[m, q]).start()
+                return carry
+
+            def own_step(q, carry):
+                g_ff[q] = ff_grad(2 * q + core)
+                return carry
+
+            lax.fori_loop(0, CHIPS, side_step, 0)
+            lax.fori_loop(0, CHIPS, own_step, 0)
+            for q in range(CHIPS):
+                copy = twin(1 + m, q, side.at[q % 2], twin_ff.at[m, q])
+                copy.wait_recv()
+                add_ff(g_ff.at[q], twin_ff.at[m, q])
+                if q >= 2:
+                    copy.wait_send()
+            line_ff[m].start()
+
+        plane_mid.drain()
+
+        def out_step(j, carry):
+            q = nth(j)
+            stage[q] = dot(mix[q], fow[...].reshape(ff, width)).astype(BF)
+            for step, push in enumerate((plane_res.send_far, plane_res.send_x, plane_res.send_y)):
+                pl.when(j == step)(push)
+            return carry
+
+        lax.fori_loop(0, CHIPS, out_step, 0)
+        plane_res.combine(add_half)
+
+    pl.run_scoped(
+        ffn,
+        pltpu.VMEM((CHIPS, tok, width), BF),
+        pltpu.VMEM((CHIPS, tok, width), BF),
+        pltpu.VMEM(fv_in.shape, BF),
+        pltpu.VMEM(fg_in.shape, BF),
+        pltpu.VMEM(fo_in.shape, BF),
+        pltpu.VMEM((CHIPS, tok, ff), BF),
+        pltpu.VMEM((CHIPS, tok, ff), BF),
+        pltpu.VMEM((CHIPS, tok, ff), BF),
+        pltpu.VMEM((2, *g_fv.shape[1:]), BF),
+    )
+
+    def rest(d_x1, d_branch, mixed, da_src, dg_src, side, g_wo, g_qk, g_vg):
+        line_wo = LineSum(k, lambda i: g_wo.at[i], lambda s: land_wo.at[s])
+        line_qk = [
+            LineSum(k, lambda i, g=g: g.at[:, i], lambda s, m=m: land_qk.at[m, s])
+            for m, g in enumerate((g_qk, g_vg))
+        ]
+        spread_a = Spread(
+            k, lambda t: da_src.at[:, at(t * two, two)], lambda s: a_land.at[s], record=False
+        )
+        spread_g = Spread(
+            k, lambda t: dg_src.at[:, at(t * two, two)], lambda s: g_land.at[s], record=False
+        )
+
+        def middle(wo, x1, attn, gate, dy, d_mixed, pair):
+            load_wo = k.keep(wo_in, wo)
+            load_mixed = k.keep(mixed_in, mixed)
+            loads = [
+                k.keep(x1_in, x1), k.keep(attn_in, attn), k.keep(gate_in, gate),
+                k.keep(dy_in.at[chip], dy),
+            ]
+            for copy in loads:
+                copy.wait()
+            plane_mid.finish()
+            fetch(near.at[0], pair)
+
+            def norm_back(rows):
+                g = acc[rows, :] + pair[0, rows, :].astype(F32) + pair[1, rows, :].astype(F32)
+                v = x1[rows, :]
+                r = row_scale(v)
+                u = v * r
+                d = dy[rows, :].astype(F32) + r * (g - u * jnp.mean(g * u, axis=-1, keepdims=True))
+                d_x1[rows, :] = d
+                d_branch[rows, :] = d.astype(BF)
+
+            row_chunks(tok, norm_back)
+            load_wo.wait()
+
+            def mixed_step(j, carry):
+                d_mixed[:, at(j * 512, 512)] = dot_rt(
+                    d_branch[...], wo[pl.ds(2 * j, 2)].reshape(512, width)
+                )
+                return carry
+
+            lax.fori_loop(0, width // 512, mixed_step, 0)
+
+            def attn_back(rows):
+                a = attn[rows, :].astype(F32)
+                s = row_scale(a)
+                u = a * s
+                d = d_mixed[rows, :]
+                dg_src[rows, :] = (d * u).astype(BF)
+                g = d * gate[rows, :].astype(F32)
+                da_src[rows, :] = (
+                    s * (g - u * jnp.mean(g * u, axis=-1, keepdims=True))
+                ).astype(BF)
+
+            row_chunks(tok, attn_back)
+            spread_a.start()
+            spread_g.start()
+            own = [
+                k.keep(da_src.at[:, at(w * two, two)], a_land.at[w]),
+                k.keep(dg_src.at[:, at(w * two, two)], g_land.at[w]),
+            ]
+
+            plane_res.finish()
+            fetch(near.at[1], pair)
+
+            def add_up(rows):
+                v = x1[rows, :] + stage[chip, rows, :].astype(F32)
+                v = v + pair[0, rows, :].astype(F32) + pair[1, rows, :].astype(F32)
+                dy[rows, :] = v.astype(BF)
+
+            row_chunks(tok, add_up)
+            store = k.keep(dy, result_o)
+            for copy in (load_mixed, store, *own):
+                copy.wait()
+
+        pl.run_scoped(
+            middle,
+            pltpu.VMEM((WIDE, tok, width), BF),
+            pltpu.VMEM((tok, width), F32),
+            pltpu.VMEM((tok, width), BF),
+            pltpu.VMEM((tok, width), BF),
+            pltpu.VMEM((tok, width), BF),
+            pltpu.VMEM((tok, width), F32),
+            pltpu.VMEM((2, tok, width), BF),
+        )
+        line_ff[0].forward(add_ff)
+        plane_res.drain()
+
+        def eight_way(plane, twin_index, landing, term):
+            def side_step(j, carry):
+                q = nth(j)
+                side[q] = term(2 * q + other).astype(BF)
+                twin(twin_index, j, side.at[q], landing.at[q]).start()
+                return carry
+
+            lax.fori_loop(0, CHIPS, side_step, 0)
+
+            def own_step(j, carry):
+                q = nth(j)
+                v = term(2 * q + core)
+                twin(twin_index, j, side.at[q], landing.at[q]).wait_recv()
+                fetch(landing.at[q], tmp)
+                v = v + tmp[...].astype(F32)
+
+                @pl.when(j < 3)
+                def _():
+                    stage[q] = v.astype(BF)
+
+                for step, push in enumerate((plane.send_far, plane.send_x, plane.send_y)):
+                    pl.when(j == step)(push)
+
+                @pl.when(j == 3)
+                def _():
+                    acc[...] = v
+
+                return carry
+
+            lax.fori_loop(0, CHIPS, own_step, 0)
+            plane.combine(add_half)
+            for j in range(CHIPS):
+                twin(twin_index, j, side.at[order[j]], landing.at[order[j]]).wait_send()
+
+        eight_way(
+            plane_out,
+            3,
+            twin_wo,
+            lambda owner: dot_lt(mixed[:, at(owner * tok, tok)], d_branch[...]),
+        )
+        line_ff[1].forward(add_ff)
+
+        def attention(xn, d_qk, d_vg, state):
+            load_xn = k.keep(xn_in, xn)
+            state[...] = jnp.zeros_like(state)
+
+            def heads(slope, qkv, sin, cols, decay, d_attn, d_gate):
+                loads = [
+                    k.keep(qkv_in, qkv), k.keep(sin_in, sin), k.keep(slope_in, slope),
+                    k.keep(cols_in, cols), k.keep(decay_in, decay),
+                ]
+                for copy in loads:
+                    copy.wait()
+                spread_a.finish()
+                spread_g.finish()
+                loads = [k.keep(a_land, d_attn), k.keep(g_land, d_gate)]
+                for copy in loads:
+                    copy.wait()
+
+                def step(i, carry):
+                    b = WIDE - 1 - i
+                    rows = at(b * BLOCK, BLOCK)
+                    mask = doc_mask(cols, rowdoc, decay, rows, b)
+                    for h in range(2):
+                        lanes = slice(h * HEAD, (h + 1) * HEAD)
+                        key_lanes = slice(two + h * HEAD, two + (h + 1) * HEAD)
+                        q = qkv[rows, lanes]
+                        key = qkv[rows, key_lanes]
+                        v = qkv[rows, 2 * two + h * HEAD : 2 * two + (h + 1) * HEAD]
+                        d_o = d_attn[b, :, lanes]
+                        factor = jnp.where(mask, decay[h], 0.0)
+                        probs = (dot_rt(q, key) * factor).astype(BF)
+                        d_probs = (dot_rt(d_o, v) * factor).astype(BF)
+                        entry = cols[rows, 1 + h : 2 + h]
+                        tail = cols[rows, 3 + h : 4 + h]
+                        before = sin[b, h]
+                        after = state[h]
+                        after_bf = after.astype(BF)
+                        tailed = (key.astype(F32) * tail).astype(BF)
+                        entered = (q.astype(F32) * entry).astype(BF)
+                        d_q = dot(d_probs, key) + entry * dot_rt(d_o, before)
+                        d_k = dot_lt(d_probs, q) + tail * dot_rt(v, after_bf)
+                        d_v = dot_lt(probs, d_o) + dot(tailed, after_bf)
+                        d_qk[rows, lanes] = (d_q * slope[rows, lanes].astype(F32)).astype(BF)
+                        d_qk[rows, key_lanes] = (d_k * slope[rows, key_lanes].astype(F32)).astype(BF)
+                        d_vg[rows, lanes] = d_v.astype(BF)
+                        state[h] = passing[pl.ds(2 * b + h, 1), :] * after + dot_lt(entered, d_o)
+                    d_vg[rows, two:] = d_gate[b]
+                    return carry
+
+                lax.fori_loop(0, WIDE, step, 0)
+
+            pl.run_scoped(
+                heads,
+                pltpu.VMEM(slope_in.shape, BF),
+                pltpu.VMEM(qkv_in.shape, BF),
+                pltpu.VMEM(sin_in.shape, BF),
+                pltpu.VMEM(cols_in.shape, F32),
+                pltpu.VMEM(decay_in.shape, F32),
+                pltpu.VMEM((WIDE, tok, two), BF),
+                pltpu.VMEM((WIDE, tok, two), BF),
+            )
+
+            plane_out.finish()
+            for side_index in range(2):
+                fetch(near.at[2, side_index], tmp)
+                acc[...] = acc[...] + tmp[...].astype(F32)
+            g_wo[...] = acc[...].astype(BF).reshape(g_wo.shape)
+            line_wo.start()
+            plane_out.drain()
+            load_xn.wait()
+
+            for m, (d_in, g_in) in enumerate(((d_qk, g_qk), (d_vg, g_vg))):
+
+                def in_grad(s, carry):
+                    left = xn[:, :, at(s * tok, tok)].reshape(WIDE * tok, tok)
+                    g_in[s] = dot_lt(left, d_in[...]).astype(BF).reshape(NARROW, -1, 2 * two)
+                    return carry
+
+                lax.fori_loop(0, WIDE, in_grad, 0)
+                line_qk[m].start()
+
+            def spread_in(wqk, wvg):
+                loads = [k.keep(wqk_in, wqk), k.keep(wvg_in, wvg)]
+                for copy in loads:
+                    copy.wait()
+
+                def term(owner):
+                    rows = at(owner * tok, tok)
+                    return dot_rt(d_qk[rows, :], wqk[...].reshape(width, 2 * two)) + dot_rt(
+                        d_vg[rows, :], wvg[...].reshape(width, 2 * two)
+                    )
+
+                eight_way(plane_in, 4, twin_xn, term)
+
+            pl.run_scoped(spread_in, pltpu.VMEM(wqk_in.shape, BF), pltpu.VMEM(wvg_in.shape, BF))
+
+        pl.run_scoped(
+            attention,
+            pltpu.VMEM((WIDE, tok, width), BF),
+            pltpu.VMEM((WIDE * tok, 2 * two), BF),
+            pltpu.VMEM((WIDE * tok, 2 * two), BF),
+            pltpu.VMEM((2, HEAD, HEAD), F32),
+        )
+
+        def last(x, pair, three, three_ff, three_qk, ff_src, qk_src, ff_all, qk_all, ff_f32, w_f32, tmp_qk):
+            add_qk = adder(tmp_qk)
+            load_x = k.keep(x_in, x)
+            line_wo.forward(add_wo)
+
+            def total(part, lands):
+                extra = jnp.where(k.mid == 0, lands[1].astype(F32), 0.0)
+                return part.astype(F32) + lands[0].astype(F32) + lands[2].astype(F32) + extra
+
+            turns = []
+            for m, g_ff in enumerate((g_fv, g_fg)):
+                line_ff[m].finish()
+                fetch(land_ff.at[m], three_ff)
+                for q in range(CHIPS):
+                    ff_src[m, q] = total(g_ff[q, n], [three_ff[s, q] for s in range(3)]).astype(BF)
+                turn = Spread(
+                    k,
+                    lambda t, m=m: ff_src.at[m, lax.div(t, 2)],
+                    lambda s, m=m: turn_ff.at[m, lax.div(s, 2)],
+                    peers=CHIPS,
+                    record=False,
+                )
+                turn.start()
+                turns.append(turn)
+            load_x.wait()
+            plane_in.finish()
+            fetch(near.at[3], pair)
+
+            def input_back(rows):
+                g = acc[rows, :] + pair[0, rows, :].astype(F32) + pair[1, rows, :].astype(F32)
+                v = x[rows, :].astype(F32)
+                r = row_scale(v)
+                u = v * r
+                d_x1[rows, :] = d_x1[rows, :] + r * (
+                    g - u * jnp.mean(g * u, axis=-1, keepdims=True)
+                )
+
+            row_chunks(tok, input_back)
+            stores = [k.keep(d_x1, dx_o)]
+            line_qk[0].forward(add_qk)
+            line_fo.finish()
+            fetch(land_fo, three.at[:, pl.ds(0, fo_rows)])
+            for r in range(0, fo_rows, 16):
+                rows = pl.ds(r, 16)
+                part = g_fo[pl.ds(pl.multiple_of((core * NARROW + n) * fo_rows + r, 16), 16), :]
+                acc[rows, :] = total(part, [three[s, rows, :] for s in range(3)])
+            store_fo = k.keep(acc.at[pl.ds(0, fo_rows)], gfo_o)
+            line_wo.finish()
+            fetch(land_wo, three.at[:, pl.ds(0, 64)])
+            w_f32[4] = total(g_wo[n], [three[s, 0:64, :] for s in range(3)])
+            stores.append(k.keep(w_f32.at[4], go_o))
+            for m, turn in enumerate(turns):
+                ff_all[chip] = ff_src[m, chip]
+                turn.finish()
+                for d in turn.distances():
+                    q = lax.rem(chip + CHIPS - d // 2, CHIPS)
+                    fetch(turn_ff.at[m, q], ff_all.at[q])
+                for q in range(CHIPS):
+                    ff_f32[m, :, q * ff : (q + 1) * ff] = ff_all[q].astype(F32)
+                stores.append(k.keep(ff_f32.at[m], (gfv_o, gfg_o)[m]))
+            line_qk[1].forward(add_qk)
+            ff_turns, turns = turns, []
+            for m, g_in in enumerate((g_qk, g_vg)):
+                line_qk[m].finish()
+                fetch(land_qk.at[m], three_qk)
+                for s in range(WIDE):
+                    qk_src[m, s] = total(g_in[s, n], [three_qk[i, s] for i in range(3)]).astype(BF)
+                turn = Spread(
+                    k,
+                    lambda t, m=m: qk_src.at[m, t],
+                    lambda s, m=m: turn_qk.at[m, s],
+                    record=False,
+                )
+                turn.start()
+                turns.append(turn)
+            for m, turn in enumerate(turns):
+                qk_all[m, w] = qk_src[m, w]
+                turn.finish()
+                for d in turn.distances():
+                    s = lax.rem(w + WIDE - d, WIDE)
+                    fetch(turn_qk.at[m, s], qk_all.at[m, s])
+                for s in range(WIDE):
+                    lanes = slice(s * two, (s + 1) * two)
+                    w_f32[2 * m, :, lanes] = qk_all[m, s, :, 0:two].astype(F32)
+                    w_f32[2 * m + 1, :, lanes] = qk_all[m, s, :, two:].astype(F32)
+                outs = ((gq_o, gk_o), (gv_o, gg_o))[m]
+                stores.append(k.keep(w_f32.at[2 * m], outs[0]))
+                stores.append(k.keep(w_f32.at[2 * m + 1], outs[1]))
+            for copy in stores + [store_fo]:
+                copy.wait()
+            plane_in.drain()
+            for sums in (line_fo, line_wo, *line_ff, *line_qk, spread_a, spread_g, *ff_turns, *turns):
+                sums.drain()
+
+        pl.run_scoped(
+            last,
+            pltpu.VMEM((tok, width), BF),
+            pltpu.VMEM((2, tok, width), BF),
+            pltpu.VMEM((3, tok, width), BF),
+            pltpu.VMEM(land_ff.shape[1:], BF),
+            pltpu.VMEM(land_qk.shape[1:], BF),
+            pltpu.VMEM((2, CHIPS, 64, ff), BF),
+            pltpu.VMEM((2, WIDE, 64, 2 * two), BF),
+            pltpu.VMEM((CHIPS, 64, ff), BF),
+            pltpu.VMEM((2, WIDE, 64, 2 * two), BF),
+            pltpu.VMEM((2, 64, CHIPS * ff), F32),
+            pltpu.VMEM((5, 64, width), F32),
+            pltpu.VMEM(g_qk.shape[:1] + g_qk.shape[2:], BF),
+        )
+
+    pl.run_scoped(
+        rest,
+        pltpu.VMEM((tok, width), F32),
+        pltpu.VMEM((tok, width), BF),
+        pltpu.VMEM((tok, width), BF),
+        pltpu.VMEM((tok, width), BF),
+        pltpu.VMEM((tok, width), BF),
+        pltpu.VMEM((CHIPS, tok, width), BF),
+        pltpu.VMEM((NARROW, 64, width), BF),
+        pltpu.VMEM((WIDE, NARROW, 64, 2 * two), BF),
+        pltpu.VMEM((WIDE, NARROW, 64, 2 * two), BF),
+    )
+
+
+def backward(tokens, kept, cols, rowdoc, passing, decay):
+    tok, width = tokens.shape
+    fv, fo = kept[4], kept[6]
+    shard, ff, fo_rows = fv.shape[3], fv.shape[4], fo.shape[2]
+    two = 2 * HEAD
+
+    def arr(*shape, dtype=BF):
+        return jax.ShapeDtypeStruct(shape, dtype)
+
+    square = [arr(shard, width, dtype=F32)] * 5
+    out_shape = (
+        arr(tok, width),
+        arr(tok, width, dtype=F32),
+        *square,
+        arr(shard, CHIPS * ff, dtype=F32),
+        arr(shard, CHIPS * ff, dtype=F32),
+        arr(fo_rows, width, dtype=F32),
+        arr(4, 2, tok // 2, width),
+        arr(4, 2, tok, width),
+        arr(NARROW, fo_rows, width),
+        arr(2, CHIPS, NARROW, shard, ff),
+        arr(CHIPS, tok, width),
+        arr(CHIPS, tok, width),
+        arr(3, fo_rows, width),
+        arr(2, 3, CHIPS, shard, ff),
+        arr(3, shard, width),
+        arr(2, 3, WIDE, shard, 2 * two),
+        arr(2, CHIPS, shard, ff),
+        arr(2, WIDE, shard, 2 * two),
+        arr(WIDE, tok, two),
+        arr(WIDE, tok, two),
+    )
+    scratch = [
+        pltpu.VMEM((CHIPS * ff // CHIPS, width), BF),
+        pltpu.VMEM((CHIPS, NARROW, shard, ff), BF),
+        pltpu.VMEM((CHIPS, NARROW, shard, ff), BF),
+        pltpu.VMEM((CHIPS, tok, width), BF),
+        pltpu.VMEM((tok, width), F32),
+        pltpu.VMEM((tok, width), BF),
+        pltpu.VMEM((CHIPS, shard, ff), BF),
+        pltpu.SemaphoreType.DMA((112,)),
+        pltpu.SemaphoreType.DMA((112,)),
+        pltpu.SemaphoreType.DMA((48,)),
+    ]
+    outs = pl.pallas_call(
+        backward_kernel,
+        out_shape=out_shape,
+        in_specs=[ANY] * 19 + [VMEM] * 2,
+        out_specs=(ANY,) * len(out_shape),
+        scratch_shapes=scratch,
+        compiler_params=pltpu.CompilerParams(
+            collective_id=1, has_side_effects=True, vmem_limit_bytes=63 * 2**20
+        ),
+        cost_estimate=pl.CostEstimate(flops=6 * 10**10, bytes_accessed=2 * 10**8, transcendentals=0),
+    )(tokens, *kept, cols, decay, rowdoc, passing)
+    return outs[:10]
 
 
 def prepare(doc_starts, length):
@@ -782,141 +1511,15 @@
     return cols, doc_ids, passing, decay
 
 
-TWINS = [[2 * i, 2 * i + 1] for i in range(CHIPS)]
-SAME = [[2 * i + j for i in range(CHIPS)] for j in range(2)]
-
-
-def local_box(
-    tokens, doc_starts, wq, wk, wv, wg, wo, fv, fg, fo, cotangent,
-):
-    length = WIDE * tokens.shape[1]
-    cols, rowdoc, passing, decay = prepare(doc_starts, length)
-    (xn, wqk, wvg, w_out, fvw, fgw, dy, pre, qkv, sin, attn, gate, mixed, middle, x1n) = forward(
-        tokens[0], (wq, wk, wv, wg, wo, fv, fg), cotangent[0], cols, rowdoc, passing, decay
+def local_box(tokens, doc_starts, wq, wk, wv, wg, wo, fv, fg, fo, cotangent):
+    tok, width = tokens.shape[1:]
+    tables = prepare(doc_starts, WIDE * tok)
+    kept = list(
+        forward(tokens[0], (wq, wk, wv, wg, wo, fv, fg, fo), cotangent[0], *tables)
     )
-    two = 2 * HEAD
-    blocks = WIDE
-
-    def split_heads(values):
-        return values.reshape(blocks, BLOCK, 2, HEAD)
-
-    def to_heads(values):
-        return lax.all_to_all(values, "wide", split_axis=1, concat_axis=0, tiled=True)
-
-    normed_bf = xn.reshape(length, -1)
-    wqk, wvg, w_out = (a.reshape(normed_bf.shape[1], -1) for a in (wqk, wvg, w_out))
-    fvw, fgw = (a.reshape(normed_bf.shape[1], -1) for a in (fvw, fgw))
-    inputs = tokens[0].astype(F32)
-    normed, in_scale = normalize(inputs)
-    middle_n, middle_scale = normalize(middle)
-    attn_n, attn_scale = normalize(attn.astype(F32))
-    upstream = cotangent[0]
-
-    fow = lax.all_gather(fo, "narrow", axis=0, tiled=True)
-    fow = lax.all_gather(fow, "wide", axis=0, tiled=True, axis_index_groups=TWINS)
-    x4 = x1n.reshape(-1, normed_bf.shape[1])
-    dy4 = dy.reshape(x4.shape)
-    ffn_val, ffn_gat = matmul(x4, fvw), matmul(x4, fgw)
-    ffn_mix = (ffn_val * ffn_gat).astype(BF)
-
-    def scatter4(v):
-        return lax.psum_scatter(
-            v.astype(BF), "wide", scatter_dimension=0, tiled=True, axis_index_groups=SAME
-        ).astype(F32)
-
-    result = middle + scatter4(matmul(ffn_mix, fow))
-    grad_fout = weight_grad(ffn_mix, dy4).astype(BF)
-    d_mix = matmul_right_t(dy4, fow)
-    d_val = (d_mix * ffn_gat).astype(BF)
-    d_gat = (d_mix * ffn_val).astype(BF)
-    d_middle_n = scatter4(matmul_right_t(d_val, fvw) + matmul_right_t(d_gat, fgw))
-    d_middle = upstream.astype(F32) + normalize_back(middle_n, middle_scale, d_middle_n)
-    d_branch = d_middle.astype(BF)
-    grad_out = weight_grad(mixed, d_branch)
-    d_mixed = matmul_right_t(d_branch, w_out)
-    d_gate = to_heads((d_mixed * attn_n).astype(BF))
-    d_attn = to_heads(
-        normalize_back(attn_n, attn_scale, d_mixed * gate.astype(F32)).astype(BF)
-    )
-
-    doc_ids = rowdoc
-    offsets = jnp.arange(BLOCK)
-    within = (doc_ids[:, :, None] == doc_ids[:, None, :]) & (offsets[:, None] >= offsets[None, :])
-    block_mask = jnp.where(within[:, None], decay[None], 0.0)
-    entry_scale = cols[:, 1:3].reshape(blocks, BLOCK, 2)
-    tail_scale = cols[:, 3:5].reshape(blocks, BLOCK, 2)
-    passing = passing[:, 0].reshape(blocks, 2)
-    queries, keys, values = (split_heads(qkv[:, i * two : (i + 1) * two]) for i in range(3))
-    query_pre, key_pre = pre[:, :two], pre[:, two:]
-    d_heads = split_heads(d_attn)
-    probs = (ein("bihe,bjhe->bhij", queries, keys) * block_mask).astype(BF)
-    tail_keys = (keys.astype(F32) * tail_scale[..., None]).astype(BF)
-    d_probs = ein("bihe,bjhe->bhij", d_heads, values)
-    d_scores = (d_probs * block_mask).astype(BF)
-    d_query = ein("bhij,bjhe->bihe", d_scores, keys)
-    d_key = ein("bhij,bihe->bjhe", d_scores, queries)
-    d_value = ein("bhij,bihe->bjhe", probs, d_heads)
-    d_query = d_query + entry_scale[..., None] * ein("bihf,bhef->bihe", d_heads, sin)
-    entry_queries = (queries.astype(F32) * entry_scale[..., None]).astype(BF)
-    grad_in = ein("bihe,bihf->bhef", entry_queries, d_heads)
-    state = jnp.zeros((2, HEAD, HEAD), F32)
-    leaving = [None] * blocks
-    for b in reversed(range(blocks)):
-        leaving[b] = state
-        state = passing[b][:, None, None] * state + grad_in[b]
-    block_out = jnp.stack(leaving).astype(BF)
-    d_key = d_key + tail_scale[..., None] * ein("bjhf,bhef->bjhe", values, block_out)
-    d_value = d_value + ein("bjhe,bhef->bjhf", tail_keys, block_out)
-    dq_pre = (d_query.reshape(query_pre.shape) * silu_slope(query_pre)).astype(BF)
-    dk_pre = (d_key.reshape(key_pre.shape) * silu_slope(key_pre)).astype(BF)
-    dv_pre = d_value.reshape(query_pre.shape).astype(BF)
-    d_qk = jnp.concatenate([dq_pre, dk_pre], axis=1)
-    d_vg = jnp.concatenate([dv_pre, d_gate], axis=1)
-    d_normed = lax.psum_scatter(
-        (matmul_right_t(d_qk, wqk) + matmul_right_t(d_vg, wvg)).astype(BF),
-        "wide", scatter_dimension=0, tiled=True,
-    ).astype(F32)
-    d_inputs = d_middle + normalize_back(normed, in_scale, d_normed)
-
-    def narrow_sum(v):
-        return lax.psum_scatter(v, "narrow", scatter_dimension=0, tiled=True)
-
-    def head_grads(left, right):
-        g = weight_grad(left, right).astype(BF).reshape(WIDE, NARROW, -1, right.shape[1])
-        g = narrow_sum(g.swapaxes(0, 1).reshape(-1, right.shape[1]))
-        g = lax.all_to_all(
-            g.reshape(WIDE, -1, 2, two), "wide", split_axis=0, concat_axis=0, tiled=True
-        ).reshape(WIDE, -1, 2, two)
-        g = g.transpose(2, 1, 0, 3).astype(F32)
-        return g[0].reshape(g.shape[1], -1), g[1].reshape(g.shape[1], -1)
-
-    def ff_grads(left, right):
-        g = weight_grad(left, right).astype(BF).reshape(CHIPS, 2, NARROW, -1, right.shape[1])
-        g = g.transpose(1, 2, 0, 3, 4).reshape(-1, right.shape[1])
-        g = lax.psum_scatter(g, "wide", scatter_dimension=0, tiled=True, axis_index_groups=TWINS)
-        g = narrow_sum(g)
-        return lax.all_to_all(
-            g, "wide", split_axis=0, concat_axis=1, tiled=True, axis_index_groups=SAME
-        ).astype(F32)
-
-    g_query, g_key = head_grads(normed_bf, d_qk)
-    g_value, g_gate = head_grads(normed_bf, d_vg)
-    return (
-        result.astype(BF)[None],
-        d_inputs[None],
-        g_query,
-        g_key,
-        g_value,
-        g_gate,
-        lax.psum_scatter(grad_out.astype(BF), BOTH, scatter_dimension=0, tiled=True).astype(F32),
-        ff_grads(x4, d_val),
-        ff_grads(x4, d_gat),
-        narrow_sum(
-            lax.psum_scatter(
-                grad_fout, "wide", scatter_dimension=0, tiled=True, axis_index_groups=TWINS
-            )
-        ).astype(F32),
-    )
+    kept[3] = kept[3].reshape(WIDE, tok, width)
+    outs = backward(tokens[0], kept, *tables)
+    return (outs[0][None], outs[1][None]) + tuple(outs[2:])
 
 
 def solution(mesh):

time: 1080 us -> 602 us (0.56)
  waiting for transfers between devices: 527 us -> 0 us
  Pallas kernels: 226 us -> 574 us
  matrix products: 175 us -> 0 us
  local copies, waits for them, and re-layouts: 62.6 us -> 14.1 us
  other arithmetic: 35.2 us -> 1.72 us
  starting transfers between devices: 26.4 us -> 0 us
  between operations: 15 us -> 0.82 us
    reduce_scatter x12 -> x0, waiting for transfers between devices: 455 us -> none  [the longest x1 184 us: local_box(): lax.psum_scatter(grad_out.astype(BF), BOTH, scatter_dimension=0, tiled=True)]
    pallas_call x0 -> x1, Pallas kernels: none -> 291 us  [backward(): pl.pallas_call(backward_kernel, out_shape=out_shape, in_specs=[ANY] * 19...]
    dot_general x23 -> x0, matrix products: 175 us -> none  [the longest x6 69.1 us: matmul_right_t(): lax.dot_general(left, right, (((1,), (1,)), ((), ())), preferred_element_...]
    all_gather x2 -> x0, waiting for transfers between devices: 58.6 us -> none  [the longest x1 58.6 us: local_box(): fow = lax.all_gather(fo, 'narrow', axis=0, tiled=True)]
    pallas_call x1, Pallas kernels: 226 us -> 283 us  [forward(): pl.pallas_call(forward_kernel, out_shape=out_shape, in_specs=[VMEM] + [AN...]
    all_to_all x6 -> x0, starting transfers between devices: 25.6 us -> none  [the longest x2 8.67 us: to_heads(): lax.all_to_all(values, 'wide', split_axis=1, concat_axis=0, tiled=True)]
    reshape x11 -> x0, local copies, waits for them, and re-layouts: 23 us -> none  [the longest x5 9.95 us: split_heads(): return values.reshape(blocks, BLOCK, 2, HEAD)]
    convert_element_type x7 -> x0, other arithmetic: 15.5 us -> none  [the longest x2 4.86 us: head_grads(): g = g.transpose(2, 1, 0, 3).astype(F32)]
  transfers between devices with their start and end apart: 20 -> 0, of which waited for: 11 -> 0; matrix products, arithmetic and copies ran while one was open for 22% -> 0% of each run, Pallas kernels for 21% -> 0%
where the time goes in v3:
time: 602 us; the launch traced here: 591 us
  Pallas kernels  574 us (95%)
  local copies, waits for them, and re-layouts  14.1 us (2%)
    pallas_call x1, Pallas kernels, backward(): pl.pallas_call(backward_kernel, out_shape=out_shape, in_specs=[ANY] * 19...  291 us
    pallas_call x1, Pallas kernels, forward(): pl.pallas_call(forward_kernel, out_shape=out_shape, in_specs=[VMEM] + [AN...  283 us

profile of v3, /device:TPU:0, one launch (start us, length us, event | category | flops | bytes accessed | tf_op | source)
XLA Modules:
  0.0 590.8 jit_solution(8761253643042313230)
XLA Ops:
  0.6 0.0 copy-start
  0.7 0.7 copy-done
  1.3 0.1 convert_reduce_fusion.2
  1.4 0.1 multiply_exponential_fusion.3
  1.6 0.1 multiply_exponential_fusion.2
  1.6 0.1 convert_reduce_fusion
  1.8 0.0 copy-start.11
  1.8 0.2 convert_reduce_fusion.1
  2.0 0.1 broadcast_multiply_fusion.2
  2.1 0.1 mul.141
  2.1 0.7 broadcast_in_dim.6.passing
  2.8 0.1 broadcast_bitcast_fusion.3
  2.9 0.1 broadcast_bitcast_fusion.2
  3.1 0.1 subtract_maximum_fusion
  3.2 0.9 multiply_exponential_fusion.decay.decay_in
  4.1 0.4 copy.23
  4.5 1.0 pad.4.cols.cols_in
  5.5 0.0 copy-done.11
  5.5 282.8 %shard_map.186 = (bf16[8,256,2048]{2,1,0:T(8,128)(2,1)}, bf16[8,4,64,512]{3,2,1,0:T(8,128)(2,1)}, bf16[8,4,64,512]{3,2,1,0:T(8,128)(2,1)}, bf16[8,4,64,2048]{3,2...) custom-call(bf16[256,2048]{1,0:T(8,128)(2,1)} %bitcast.32, ...), custom_call_target="tpu_custom_call" | custom-call | flops 20000000000 | bytes 100000000 | tf_op jit(solution)/shard_map/pallas_call | solution.py:766
  288.4 291.3 %shard_map.187 = (bf16[256,2048]{1,0:T(8,128)(2,1)}, f32[256,2048]{1,0:T(8,128)}, f32[64,2048]{1,0:T(8,128)}, f32[64,2048]{1,0:T(8,128)}, f32[64,2048]{1,0:T(8,1...) custom-call(bf16[256,2048]{1,0:T(8,128)(2,1)} %bitcast.33, ...), custom_call_target="tpu_custom_call" | custom-call | flops 60000002048 | bytes 200000000 | tf_op jit(solution)/shard_map/pallas_call | solution.py:1476
  579.7 0.0 copy-start.2
  579.7 0.0 copy-start.10
  579.7 2.5 copy.38
  582.2 0.0 copy-done.2
  582.2 0.0 copy-start.9
  582.2 0.0 copy-start.8
  582.2 0.0 copy-start.7
  582.2 1.3 copy.39
  583.5 0.0 copy-done.10
  583.5 0.0 copy-start.6
  583.5 0.0 copy-start.5
  583.5 0.8 copy.40
  584.3 0.0 copy-done.9
  584.3 0.8 copy.41
  585.1 0.0 copy-done.8
  585.1 0.0 copy-start.4
  585.1 0.8 copy.42
  585.9 0.0 copy-done.7
  585.9 0.8 copy.43
  586.7 0.0 copy-done.6
  586.7 0.8 copy.44
  587.5 0.0 copy-done.5
  587.5 1.1 copy.45
  588.6 0.0 copy-done.4
  588.6 1.1 copy.46
  589.7 0.0 copy-done.3
  589.7 1.1 copy.47
  590.8 0.0 copy-done.1
  (19 shorter events, 0.2 us)
Async XLA Ops:
  0.6 0.7 copy-start
  1.8 3.8 copy-start.11
  579.7 2.5 copy-start.2
  579.7 3.8 copy-start.10
  582.2 2.1 copy-start.9
  582.2 2.9 copy-start.8
  582.2 3.7 copy-start.7
  583.5 3.2 copy-start.6
  583.5 4.0 copy-start.5
  585.1 3.5 copy-start.4
  586.7 3.0 copy-start.3
  587.5 3.3 copy-start.1

commit v4 on v3

--- a/solution.py
+++ b/solution.py
@@ -337,8 +337,8 @@
 
     def start(self):
         k, b, mine = self.links, self.base, self.part(self.links.n)
+        k.go(mine, mine, b + 1, b + k.n, narrow=k.cross)
         k.go(mine, mine, b, b + k.n, narrow=k.pair)
-        k.go(mine, mine, b + 1, b + k.n, narrow=k.cross)
         last = self.part(k.end_part)
         self.last = k.remote(last, last, b + 2, b + k.end_part, narrow=k.end_to)
 
@@ -541,49 +541,42 @@
     for copy in own:
         copy.wait()
     line_out.start()
-    spreads[0].start()
-    spreads[1].start()
+    for spread in spreads:
+        spread.start()
     plane_xn.start()
-    spreads[2].start()
-    spreads[3].start()
     twin_xn.send(w)
+    for spread in spread_ff:
+        spread.start()
     spreads[0].finish()
     spreads[1].finish()
     line_qk.start()
     spreads[2].finish()
     spreads[3].finish()
     line_vg.start()
-    for copy in own_ff:
-        copy.wait()
-    spread_ff[0].start()
-    spread_ff[1].start()
+    line_out.forward()
     plane_xn.forward()
+    line_out.finish()
+    plane_out.start()
+    twin_out.send(w)
     plane_xn.finish_near()
     twin_xn.send(k.wx)
     twin_xn.send(k.wy)
-    line_out.forward()
-    line_out.finish()
-    plane_out.start()
-    twin_out.send(w)
     line_qk.forward()
     plane_xn.finish_far()
     twin_xn.send(k.wd)
+    spread_ff[0].finish()
+    spread_ff[1].finish()
+    for copy in own_ff:
+        copy.wait()
+    line_fv.start()
+    line_fg.start()
+    line_fo.start()
     line_vg.forward()
     plane_out.forward()
-    plane_out.finish_near()
-    twin_out.send(k.wx)
-    twin_out.send(k.wy)
-    plane_out.finish_far()
-    twin_out.send(k.wd)
-    plane_dy.start()
-    spread_ff[0].finish()
-    spread_ff[1].finish()
     for s in (k.ws, k.wx + 1 - 2 * core, k.wy + 1 - 2 * core, k.wd + 1 - 2 * core):
         twin_xn.wait(s)
     keep_xn = k.keep(xn, xn_o)
-
     line_qk.finish()
-    line_fv.start()
 
     def project_qk(t, carry):
         v = dot(xn[t], wqk[...].reshape(-1, 2 * head_cols))
@@ -596,9 +589,10 @@
     lax.fori_loop(0, WIDE, project_qk, 0)
     keep_slope = k.keep(slope, slope_o)
     keep_wqk = k.keep(wqk, wqk_o)
+    plane_out.finish_near()
+    twin_out.send(k.wx)
+    twin_out.send(k.wy)
     line_vg.finish()
-    line_fg.start()
-    line_fo.start()
 
     def project_vg(t, carry):
         v = dot(xn[t], wvg[...].reshape(-1, 2 * head_cols)).astype(BF)
@@ -613,7 +607,6 @@
     spread_gate.start()
     gate[:, wide_cols(w)] = gates[w]
 
-    plane_dy.forward()
     state[...] = jnp.zeros_like(state)
     spread_attn = Spread(k, lambda t: attn_s.at[t], lambda s: attn.at[:, wide_cols(s)])
 
@@ -658,6 +651,9 @@
             )
         )
     keep_sin = k.keep(sin, sin_o)
+    plane_out.finish_far()
+    twin_out.send(k.wd)
+    plane_dy.start()
     for s in (k.ws, k.wx + 1 - 2 * core, k.wy + 1 - 2 * core, k.wd + 1 - 2 * core):
         twin_out.wait(s)
     keep_wo = k.keep(wout, wo_o)
@@ -690,9 +686,10 @@
     k.keep(x1n, x1n_o.at[chip]).wait()
     plane_x1n.start()
     line_fv.forward()
+    plane_dy.forward()
+    plane_x1n.forward()
     line_fg.forward()
     line_fo.forward()
-    plane_x1n.forward()
     plane_dy.finish_near()
     plane_dy.finish_far()
     line_fv.finish()
@@ -927,10 +924,10 @@
         LineSum(k, lambda i, g=g: g.at[:, i], lambda s, m=m: land_ff.at[m, s])
         for m, g in enumerate((g_fv, g_fg))
     ]
-    planes = [
-        PlaneSum(k, lambda q: stage.at[q], corner.at[m], near.at[m], half) for m in range(4)
-    ]
-    plane_mid, plane_res, plane_out, plane_in = planes
+    def plane_sum(m, blocks):
+        return PlaneSum(k, lambda q: blocks.at[q], corner.at[m], near.at[m], half)
+
+    plane_mid, plane_res, plane_in = (plane_sum(m, stage) for m in (0, 1, 3))
     twin_base = k.take(4 * 5)
 
     def twin(m, j, src, dst):
@@ -944,7 +941,7 @@
             k.keep(x1n_in, x1n), k.keep(fv_in, fvw), k.keep(fg_in, fgw), k.keep(dy_in, dy),
             k.keep(fo_in, fow),
         ]
-        for copy in loads:
+        for copy in loads[:3]:
             copy.wait()
         k.met()
 
@@ -958,22 +955,24 @@
 
         lax.fori_loop(0, CHIPS, up, 0)
 
-        def fo_grad(rows):
-            left = mix[:, :, rows].reshape(CHIPS * tok, -1)
+        for copy in loads[3:]:
+            copy.wait()
+
+        def fo_grad(j, carry):
+            chunk = lax.rem(j + 2 * other, chunks)
+            rows = pl.ds(pl.multiple_of(jnp.minimum(chunk * 256, ff - 256), 128), 256)
+            left = mix[:, :, rows].reshape(CHIPS * tok, 256)
             for h in range(2):
                 lanes = slice(h * width // 2, (h + 1) * width // 2)
                 right = dy[:, :, lanes].reshape(CHIPS * tok, -1)
                 g_fo[rows, lanes] = dot_lt(left, right).astype(BF)
-
-        def fo_step(j, carry):
-            fo_grad(at(j * 256, 256))
             return carry
 
-        lax.fori_loop(0, ff // 256, fo_step, 0)
-        if ff % 256:
-            fo_grad(pl.ds(ff - ff % 256, ff % 256))
+        chunks = pl.cdiv(ff, 256)
+        lax.fori_loop(0, 4, fo_grad, 0)
         for i in range(NARROW):
             twin(0, i, fo_part(other, i), twin_fo.at[i]).start()
+        lax.fori_loop(4, chunks, fo_grad, 0)
         for i in range(NARROW):
             copy = twin(0, i, fo_part(other, i), twin_fo.at[i])
             copy.wait_recv()
@@ -1055,7 +1054,6 @@
             return carry
 
         lax.fori_loop(0, CHIPS, out_step, 0)
-        plane_res.combine(add_half)
 
     pl.run_scoped(
         ffn,
@@ -1070,7 +1068,9 @@
         pltpu.VMEM((2, *g_fv.shape[1:]), BF),
     )
 
-    def rest(d_x1, d_branch, mixed, da_src, dg_src, side, g_wo, g_qk, g_vg):
+    def rest(d_x1, d_branch, mixed, da_src, dg_src, side, stage_wo, own_res, g_wo, g_qk, g_vg):
+        plane_out = plane_sum(2, stage_wo)
+        own_res[...] = stage[chip]
         line_wo = LineSum(k, lambda i: g_wo.at[i], lambda s: land_wo.at[s])
         line_qk = [
             LineSum(k, lambda i, g=g: g.at[:, i], lambda s, m=m: land_qk.at[m, s])
@@ -1084,16 +1084,15 @@
         )
 
         def middle(wo, x1, attn, gate, dy, d_mixed, pair):
-            load_wo = k.keep(wo_in, wo)
-            load_mixed = k.keep(mixed_in, mixed)
-            loads = [
-                k.keep(x1_in, x1), k.keep(attn_in, attn), k.keep(gate_in, gate),
-                k.keep(dy_in.at[chip], dy),
+            loads = [k.keep(x1_in, x1), k.keep(dy_in.at[chip], dy)]
+            late = [
+                k.keep(attn_in, attn), k.keep(gate_in, gate), k.keep(wo_in, wo),
+                k.keep(mixed_in, mixed),
             ]
+            plane_mid.finish()
+            fetch(near.at[0], pair)
             for copy in loads:
                 copy.wait()
-            plane_mid.finish()
-            fetch(near.at[0], pair)
 
             def norm_back(rows):
                 g = acc[rows, :] + pair[0, rows, :].astype(F32) + pair[1, rows, :].astype(F32)
@@ -1105,7 +1104,8 @@
                 d_branch[rows, :] = d.astype(BF)
 
             row_chunks(tok, norm_back)
-            load_wo.wait()
+            for copy in late:
+                copy.wait()
 
             def mixed_step(j, carry):
                 d_mixed[:, at(j * 512, 512)] = dot_rt(
@@ -1134,17 +1134,7 @@
                 k.keep(dg_src.at[:, at(w * two, two)], g_land.at[w]),
             ]
 
-            plane_res.finish()
-            fetch(near.at[1], pair)
-
-            def add_up(rows):
-                v = x1[rows, :] + stage[chip, rows, :].astype(F32)
-                v = v + pair[0, rows, :].astype(F32) + pair[1, rows, :].astype(F32)
-                dy[rows, :] = v.astype(BF)
-
-            row_chunks(tok, add_up)
-            store = k.keep(dy, result_o)
-            for copy in (load_mixed, store, *own):
+            for copy in own:
                 copy.wait()
 
         pl.run_scoped(
@@ -1157,10 +1147,9 @@
             pltpu.VMEM((tok, width), F32),
             pltpu.VMEM((2, tok, width), BF),
         )
-        line_ff[0].forward(add_ff)
-        plane_res.drain()
-
-        def eight_way(plane, twin_index, landing, term):
+        plane_res.combine(add_half)
+
+        def eight_way(plane, twin_index, landing, blocks, term):
             def side_step(j, carry):
                 q = nth(j)
                 side[q] = term(2 * q + other).astype(BF)
@@ -1178,7 +1167,7 @@
 
                 @pl.when(j < 3)
                 def _():
-                    stage[q] = v.astype(BF)
+                    blocks[q] = v.astype(BF)
 
                 for step, push in enumerate((plane.send_far, plane.send_x, plane.send_y)):
                     pl.when(j == step)(push)
@@ -1190,7 +1179,6 @@
                 return carry
 
             lax.fori_loop(0, CHIPS, own_step, 0)
-            plane.combine(add_half)
             for j in range(CHIPS):
                 twin(twin_index, j, side.at[order[j]], landing.at[order[j]]).wait_send()
 
@@ -1198,12 +1186,12 @@
             plane_out,
             3,
             twin_wo,
+            stage_wo,
             lambda owner: dot_lt(mixed[:, at(owner * tok, tok)], d_branch[...]),
         )
-        line_ff[1].forward(add_ff)
+        line_ff[0].forward(add_ff)
 
         def attention(xn, d_qk, d_vg, state):
-            load_xn = k.keep(xn_in, xn)
             state[...] = jnp.zeros_like(state)
 
             def heads(slope, qkv, sin, cols, decay, d_attn, d_gate):
@@ -1211,6 +1199,7 @@
                     k.keep(qkv_in, qkv), k.keep(sin_in, sin), k.keep(slope_in, slope),
                     k.keep(cols_in, cols), k.keep(decay_in, decay),
                 ]
+                load_xn = k.keep(xn_in, xn)
                 for copy in loads:
                     copy.wait()
                 spread_a.finish()
@@ -1251,6 +1240,7 @@
                     return carry
 
                 lax.fori_loop(0, WIDE, step, 0)
+                load_xn.wait()
 
             pl.run_scoped(
                 heads,
@@ -1263,6 +1253,18 @@
                 pltpu.VMEM((WIDE, tok, two), BF),
             )
 
+            plane_out.combine(add_half)
+            for m, (d_in, g_in) in enumerate(((d_qk, g_qk), (d_vg, g_vg))):
+
+                def in_grad(s, carry):
+                    left = xn[:, :, at(s * tok, tok)].reshape(WIDE * tok, tok)
+                    g_in[s] = dot_lt(left, d_in[...]).astype(BF).reshape(NARROW, -1, 2 * two)
+                    return carry
+
+                lax.fori_loop(0, WIDE, in_grad, 0)
+                line_qk[m].start()
+
+            line_ff[1].forward(add_ff)
             plane_out.finish()
             for side_index in range(2):
                 fetch(near.at[2, side_index], tmp)
@@ -1270,17 +1272,7 @@
             g_wo[...] = acc[...].astype(BF).reshape(g_wo.shape)
             line_wo.start()
             plane_out.drain()
-            load_xn.wait()
-
-            for m, (d_in, g_in) in enumerate(((d_qk, g_qk), (d_vg, g_vg))):
-
-                def in_grad(s, carry):
-                    left = xn[:, :, at(s * tok, tok)].reshape(WIDE * tok, tok)
-                    g_in[s] = dot_lt(left, d_in[...]).astype(BF).reshape(NARROW, -1, 2 * two)
-                    return carry
-
-                lax.fori_loop(0, WIDE, in_grad, 0)
-                line_qk[m].start()
+            plane_res.drain()
 
             def spread_in(wqk, wvg):
                 loads = [k.keep(wqk_in, wqk), k.keep(wvg_in, wvg)]
@@ -1293,7 +1285,7 @@
                         d_vg[rows, :], wvg[...].reshape(width, 2 * two)
                     )
 
-                eight_way(plane_in, 4, twin_xn, term)
+                eight_way(plane_in, 4, twin_xn, stage, term)
 
             pl.run_scoped(spread_in, pltpu.VMEM(wqk_in.shape, BF), pltpu.VMEM(wvg_in.shape, BF))
 
@@ -1305,16 +1297,17 @@
             pltpu.VMEM((2, HEAD, HEAD), F32),
         )
 
-        def last(x, pair, three, three_ff, three_qk, ff_src, qk_src, ff_all, qk_all, ff_f32, w_f32, tmp_qk):
+        def last(
+            x, x1, pair, three, three_ff, three_qk, ff_src, qk_src, ff_all, qk_all, ff_f32, w_f32, w_fo, tmp_qk
+        ):
             add_qk = adder(tmp_qk)
-            load_x = k.keep(x_in, x)
-            line_wo.forward(add_wo)
+            load_x, load_x1 = k.keep(x_in, x), k.keep(x1_in, x1)
 
             def total(part, lands):
                 extra = jnp.where(k.mid == 0, lands[1].astype(F32), 0.0)
                 return part.astype(F32) + lands[0].astype(F32) + lands[2].astype(F32) + extra
 
-            turns = []
+            ff_turns = []
             for m, g_ff in enumerate((g_fv, g_fg)):
                 line_ff[m].finish()
                 fetch(land_ff.at[m], three_ff)
@@ -1328,7 +1321,28 @@
                     record=False,
                 )
                 turn.start()
-                turns.append(turn)
+                ff_turns.append((turn, k.keep(ff_src.at[m, chip], turn_ff.at[m, chip])))
+            plane_in.combine(add_half)
+            line_fo.finish()
+            fetch(land_fo, three.at[:, pl.ds(0, fo_rows)])
+            own = fo_part(core, n)
+            for r in range(0, fo_rows, 16):
+                rows = pl.ds(r, 16)
+                w_fo[rows, :] = total(own[rows, :], [three[s, rows, :] for s in range(3)])
+            stores = [k.keep(w_fo, gfo_o)]
+            line_qk[0].forward(add_qk)
+
+            plane_res.finish()
+            fetch(near.at[1], pair)
+            load_x1.wait()
+
+            def add_up(rows):
+                v = x1[rows, :] + own_res[rows, :].astype(F32)
+                v = v + pair[0, rows, :].astype(F32) + pair[1, rows, :].astype(F32)
+                own_res[rows, :] = v.astype(BF)
+
+            row_chunks(tok, add_up)
+            stores.append(k.keep(own_res, result_o))
             load_x.wait()
             plane_in.finish()
             fetch(near.at[3], pair)
@@ -1343,30 +1357,16 @@
                 )
 
             row_chunks(tok, input_back)
-            stores = [k.keep(d_x1, dx_o)]
-            line_qk[0].forward(add_qk)
-            line_fo.finish()
-            fetch(land_fo, three.at[:, pl.ds(0, fo_rows)])
-            for r in range(0, fo_rows, 16):
-                rows = pl.ds(r, 16)
-                part = g_fo[pl.ds(pl.multiple_of((core * NARROW + n) * fo_rows + r, 16), 16), :]
-                acc[rows, :] = total(part, [three[s, rows, :] for s in range(3)])
-            store_fo = k.keep(acc.at[pl.ds(0, fo_rows)], gfo_o)
-            line_wo.finish()
-            fetch(land_wo, three.at[:, pl.ds(0, 64)])
-            w_f32[4] = total(g_wo[n], [three[s, 0:64, :] for s in range(3)])
-            stores.append(k.keep(w_f32.at[4], go_o))
-            for m, turn in enumerate(turns):
-                ff_all[chip] = ff_src[m, chip]
+            stores.append(k.keep(d_x1, dx_o))
+            for m, (turn, copy) in enumerate(ff_turns):
                 turn.finish()
-                for d in turn.distances():
-                    q = lax.rem(chip + CHIPS - d // 2, CHIPS)
-                    fetch(turn_ff.at[m, q], ff_all.at[q])
+                copy.wait()
+                fetch(turn_ff.at[m], ff_all)
                 for q in range(CHIPS):
                     ff_f32[m, :, q * ff : (q + 1) * ff] = ff_all[q].astype(F32)
                 stores.append(k.keep(ff_f32.at[m], (gfv_o, gfg_o)[m]))
             line_qk[1].forward(add_qk)
-            ff_turns, turns = turns, []
+            qk_turns = []
             for m, g_in in enumerate((g_qk, g_vg)):
                 line_qk[m].finish()
                 fetch(land_qk.at[m], three_qk)
@@ -1379,29 +1379,35 @@
                     record=False,
                 )
                 turn.start()
-                turns.append(turn)
-            for m, turn in enumerate(turns):
-                qk_all[m, w] = qk_src[m, w]
+                qk_turns.append((turn, k.keep(qk_src.at[m, w], turn_qk.at[m, w])))
+                if m == 0:
+                    line_wo.forward(add_wo)
+            line_wo.finish()
+            fetch(land_wo, three.at[:, pl.ds(0, 64)])
+            w_f32[4] = total(g_wo[n], [three[s, 0:64, :] for s in range(3)])
+            stores.append(k.keep(w_f32.at[4], go_o))
+            for m, (turn, copy) in enumerate(qk_turns):
                 turn.finish()
-                for d in turn.distances():
-                    s = lax.rem(w + WIDE - d, WIDE)
-                    fetch(turn_qk.at[m, s], qk_all.at[m, s])
+                copy.wait()
+                fetch(turn_qk.at[m], qk_all)
                 for s in range(WIDE):
                     lanes = slice(s * two, (s + 1) * two)
-                    w_f32[2 * m, :, lanes] = qk_all[m, s, :, 0:two].astype(F32)
-                    w_f32[2 * m + 1, :, lanes] = qk_all[m, s, :, two:].astype(F32)
+                    w_f32[2 * m, :, lanes] = qk_all[s, :, 0:two].astype(F32)
+                    w_f32[2 * m + 1, :, lanes] = qk_all[s, :, two:].astype(F32)
                 outs = ((gq_o, gk_o), (gv_o, gg_o))[m]
                 stores.append(k.keep(w_f32.at[2 * m], outs[0]))
                 stores.append(k.keep(w_f32.at[2 * m + 1], outs[1]))
-            for copy in stores + [store_fo]:
+            for copy in stores:
                 copy.wait()
             plane_in.drain()
-            for sums in (line_fo, line_wo, *line_ff, *line_qk, spread_a, spread_g, *ff_turns, *turns):
+            turns = [turn for turn, copy in ff_turns + qk_turns]
+            for sums in (line_fo, line_wo, *line_ff, *line_qk, spread_a, spread_g, *turns):
                 sums.drain()
 
         pl.run_scoped(
             last,
             pltpu.VMEM((tok, width), BF),
+            pltpu.VMEM((tok, width), F32),
             pltpu.VMEM((2, tok, width), BF),
             pltpu.VMEM((3, tok, width), BF),
             pltpu.VMEM(land_ff.shape[1:], BF),
@@ -1409,10 +1415,11 @@
             pltpu.VMEM((2, CHIPS, 64, ff), BF),
             pltpu.VMEM((2, WIDE, 64, 2 * two), BF),
             pltpu.VMEM((CHIPS, 64, ff), BF),
-            pltpu.VMEM((2, WIDE, 64, 2 * two), BF),
+            pltpu.VMEM((WIDE, 64, 2 * two), BF),
             pltpu.VMEM((2, 64, CHIPS * ff), F32),
             pltpu.VMEM((5, 64, width), F32),
-            pltpu.VMEM(g_qk.shape[:1] + g_qk.shape[2:], BF),
+            pltpu.VMEM((fo_rows, width), F32),
+            pltpu.VMEM((WIDE, 64, 2 * two), BF),
         )
 
     pl.run_scoped(
@@ -1423,6 +1430,8 @@
         pltpu.VMEM((tok, width), BF),
         pltpu.VMEM((tok, width), BF),
         pltpu.VMEM((CHIPS, tok, width), BF),
+        pltpu.VMEM((CHIPS, tok, width), BF),
+        pltpu.VMEM((tok, width), BF),
         pltpu.VMEM((NARROW, 64, width), BF),
         pltpu.VMEM((WIDE, NARROW, 64, 2 * two), BF),
         pltpu.VMEM((WIDE, NARROW, 64, 2 * two), BF),

time: 602 us -> 557 us (0.925)
  Pallas kernels: 574 us -> 534 us
    pallas_call x1, Pallas kernels: 283 us -> 261 us  [forward(): pl.pallas_call(forward_kernel, out_shape=out_shape, in_specs=[VMEM] + [AN...]
    pallas_call x1, Pallas kernels: 291 us -> 272 us  [backward(): pl.pallas_call(backward_kernel, out_shape=out_shape, in_specs=[ANY] * 19...]
where the time goes in v4:
time: 557 us; the launch traced here: 550 us
  Pallas kernels  534 us (96%)
  local copies, waits for them, and re-layouts  14.1 us (3%)
    pallas_call x1, Pallas kernels, backward(): pl.pallas_call(backward_kernel, out_shape=out_shape, in_specs=[ANY] * 19...  272 us
    pallas_call x1, Pallas kernels, forward(): pl.pallas_call(forward_kernel, out_shape=out_shape, in_specs=[VMEM] + [AN...  261 us
    unnamed x41, local copies, waits for them, and re-layouts  11.9 us

profile of v4, /device:TPU:0, one launch (start us, length us, event | category | flops | bytes accessed | tf_op | source)
XLA Modules:
  0.0 550.2 jit_solution(13585135286718055789)
XLA Ops:
  0.6 0.0 copy-start
  0.7 0.7 copy-done
  1.3 0.1 convert_reduce_fusion.2
  1.4 0.1 multiply_exponential_fusion.3
  1.6 0.1 multiply_exponential_fusion.2
  1.6 0.1 convert_reduce_fusion
  1.8 0.0 copy-start.11
  1.8 0.2 convert_reduce_fusion.1
  2.0 0.1 broadcast_multiply_fusion.2
  2.1 0.1 mul.141
  2.1 0.7 broadcast_in_dim.6.passing
  2.8 0.1 broadcast_bitcast_fusion.3
  2.9 0.1 broadcast_bitcast_fusion.2
  3.1 0.1 subtract_maximum_fusion
  3.2 0.9 multiply_exponential_fusion.decay.decay_in
  4.1 0.4 copy.23
  4.5 1.0 pad.4.cols.cols_in
  5.5 0.0 copy-done.11
  5.5 261.3 %shard_map.186 = (bf16[8,256,2048]{2,1,0:T(8,128)(2,1)}, bf16[8,4,64,512]{3,2,1,0:T(8,128)(2,1)}, bf16[8,4,64,512]{3,2,1,0:T(8,128)(2,1)}, bf16[8,4,64,2048]{3,2...) custom-call(bf16[256,2048]{1,0:T(8,128)(2,1)} %bitcast.32, ...), custom_call_target="tpu_custom_call" | custom-call | flops 20000000000 | bytes 100000000 | tf_op jit(solution)/shard_map/pallas_call | solution.py:763
  266.8 272.2 %shard_map.187 = (bf16[256,2048]{1,0:T(8,128)(2,1)}, f32[256,2048]{1,0:T(8,128)}, f32[64,2048]{1,0:T(8,128)}, f32[64,2048]{1,0:T(8,128)}, f32[64,2048]{1,0:T(8,1...) custom-call(bf16[256,2048]{1,0:T(8,128)(2,1)} %bitcast.33, ...), custom_call_target="tpu_custom_call" | custom-call | flops 60000002048 | bytes 200000000 | tf_op jit(solution)/shard_map/pallas_call | solution.py:1485
  539.1 0.0 copy-start.2
  539.1 0.0 copy-start.10
  539.1 2.5 copy.38
  541.5 0.0 copy-done.2
  541.5 0.0 copy-start.9
  541.5 0.0 copy-start.8
  541.5 0.0 copy-start.7
  541.6 1.3 copy.39
  542.9 0.0 copy-done.10
  542.9 0.0 copy-start.6
  542.9 0.8 copy.40
  543.7 0.0 copy-done.9
  543.7 0.8 copy.41
  544.5 0.0 copy-done.8
  544.5 0.0 copy-start.4
  544.5 0.8 copy.42
  545.3 0.0 copy-done.7
  545.3 0.8 copy.43
  546.1 0.0 copy-done.6
  546.1 0.0 copy-start.3
  546.1 0.8 copy.44
  546.9 0.0 copy-done.5
  546.9 1.1 copy.45
  548.0 0.0 copy-done.4
  548.0 1.1 copy.46
  549.1 0.0 copy-done.3
  549.1 1.1 copy.47
  550.2 0.0 copy-done.1
  (19 shorter events, 0.2 us)
Async XLA Ops:
  0.6 0.7 copy-start
  1.8 3.8 copy-start.11
  539.1 2.5 copy-start.2
  539.1 3.8 copy-start.10
  541.5 2.1 copy-start.9
  541.5 2.9 copy-start.8
  541.5 3.7 copy-start.7
  542.9 3.2 copy-start.6
  542.9 4.0 copy-start.5
  544.5 3.5 copy-start.4
  546.1 3.0 copy-start.3
  546.9 3.3 copy-start.1

commit v5 on v4

--- a/solution.py
+++ b/solution.py
@@ -259,8 +259,7 @@
 class Links:
     def __init__(self, send, recv, here):
         self.send, self.recv, self.here = send, recv, here
-        self.count = 0
-        self.sent, self.kept = [], []
+        self.count, self.kept = 0, 1
         w = lax.axis_index("wide")
         n = lax.axis_index("narrow")
         self.w, self.n = w, n
@@ -310,41 +309,43 @@
             device_id_type=MESH,
         )
 
-    def go(self, src, dst, send, recv, wide=None, narrow=None, record=True):
-        copy = self.remote(src, dst, send, recv, wide, narrow)
-        copy.start()
-        if record:
-            self.sent.append(copy)
-
     def arrived(self, ref, recv):
         self.remote(ref, ref, recv, recv, wide=self.ws).wait_recv()
 
     def keep(self, src, dst):
-        copy = pltpu.make_async_copy(src, dst, self.here.at[len(self.kept)])
+        copy = pltpu.make_async_copy(src, dst, self.here.at[self.kept])
+        self.kept += 1
         copy.start()
-        self.kept.append(copy)
         return copy
-
-    def drain(self):
-        for copy in self.sent:
-            copy.wait_send()
 
 
 class Line:
     def __init__(self, links, part):
         self.links, self.part = links, part
-        self.base = links.take(4)
+        self.base = links.take(5)
+
+    def copy(self, index):
+        k, b = self.links, self.base
+        which, to = (
+            (k.n, k.pair),
+            (k.n, k.cross),
+            (k.pair, k.cross),
+            (k.cross, k.pair),
+            (k.far, k.pair),
+        )[index]
+        ref = self.part(which)
+        return k.remote(ref, ref, b + index, b + which, narrow=to)
 
     def start(self):
-        k, b, mine = self.links, self.base, self.part(self.links.n)
-        k.go(mine, mine, b + 1, b + k.n, narrow=k.cross)
-        k.go(mine, mine, b, b + k.n, narrow=k.pair)
-        last = self.part(k.end_part)
-        self.last = k.remote(last, last, b + 2, b + k.end_part, narrow=k.end_to)
-
-        @pl.when(k.mid == 0)
-        def _():
-            self.last.start()
+        self.start_away()
+        pl.when(self.links.mid == 1)(lambda: self.copy(0).start())
+
+    def start_away(self):
+        pl.when(self.links.mid == 1)(lambda: self.copy(1).start())
+        pl.when(self.links.mid == 0)(lambda: self.copy(0).start())
+
+    def start_home(self):
+        pl.when(self.links.mid == 1)(lambda: self.copy(0).start())
 
     def wait(self, index):
         self.links.arrived(self.part(index), self.base + index)
@@ -353,18 +354,30 @@
         @pl.when(self.links.mid == 1)
         def _():
             self.wait(self.links.cross)
-            self.last.start()
-
-    def finish(self):
+            self.copy(3).start()
+            self.wait(self.links.pair)
+            self.copy(2).start()
+
+    def forward_far(self):
+        @pl.when(self.links.mid == 1)
+        def _():
+            self.wait(self.links.far)
+            self.copy(4).start()
+
+    def finish(self, then=lambda place: None):
         k = self.links
-        self.wait(k.pair)
-        self.wait(k.far)
-
-        @pl.when(k.mid == 0)
+        then(0)
+        for place, index in enumerate((k.pair, k.cross, k.far)):
+            pl.when(k.mid == 0)(lambda index=index: self.wait(index))
+            then(place + 1)
+
+    def drain(self):
+        self.copy(0).wait_send()
+
+        @pl.when(self.links.mid == 1)
         def _():
-            self.wait(k.cross)
-
-        k.sent.append(self.last)
+            for index in range(1, 5):
+                self.copy(index).wait_send()
 
 
 class Plane:
@@ -372,74 +385,91 @@
         self.links, self.slot = links, slot
         self.base = links.take(6)
 
+    def copy(self, index):
+        k, b = self.links, self.base
+        owner, half, to = (
+            (k.w, 0, k.wx),
+            (k.w, 1, k.wy),
+            (k.w, 1, k.wx),
+            (k.w, 0, k.wy),
+            (k.wx, 0, k.wy),
+            (k.wy, 1, k.wx),
+        )[index]
+        ref = self.slot(owner, half)
+        return k.remote(ref, ref, b + index, b + index, wide=to)
+
     def start(self):
-        k, b, slot = self.links, self.base, self.slot
-        k.go(slot(k.w, 0), slot(k.w, 0), b, b, wide=k.wx)
-        k.go(slot(k.w, 1), slot(k.w, 1), b + 3, b + 3, wide=k.wy)
-        k.go(slot(k.w, 1), slot(k.w, 1), b + 1, b + 1, wide=k.wx)
-        k.go(slot(k.w, 0), slot(k.w, 0), b + 2, b + 2, wide=k.wy)
+        for index in range(4):
+            self.copy(index).start()
 
     def forward(self):
         k, b, slot = self.links, self.base, self.slot
         k.arrived(slot(k.wx, 0), b)
-        k.go(slot(k.wx, 0), slot(k.wx, 0), b + 4, b + 4, wide=k.wy)
-        k.arrived(slot(k.wy, 1), b + 3)
-        k.go(slot(k.wy, 1), slot(k.wy, 1), b + 5, b + 5, wide=k.wx)
+        self.copy(4).start()
+        k.arrived(slot(k.wy, 1), b + 1)
+        self.copy(5).start()
 
     def finish_near(self):
         k, b, slot = self.links, self.base, self.slot
-        k.arrived(slot(k.wx, 1), b + 1)
-        k.arrived(slot(k.wy, 0), b + 2)
+        k.arrived(slot(k.wx, 1), b + 2)
+        k.arrived(slot(k.wy, 0), b + 3)
 
     def finish_far(self):
         k, b, slot = self.links, self.base, self.slot
         k.arrived(slot(k.wd, 0), b + 4)
         k.arrived(slot(k.wd, 1), b + 5)
 
+    def drain(self):
+        for index in range(6):
+            self.copy(index).wait_send()
+
 
 class Sibling:
-    def __init__(self, links, block, number):
-        self.links, self.block = links, block
+    def __init__(self, links, block, twin, number):
+        self.links, self.block, self.twin, self.number = links, block, twin, number
         self.base = links.take(number)
-        self.out, self.come = 0, 0
-
-    def send(self, w):
-        b = self.block(w)
-        self.links.go(b, b, self.base + self.out, self.base + self.out, wide=self.links.ws)
-        self.out += 1
-
-    def wait(self, w):
-        self.links.arrived(self.block(w), self.base + self.come)
-        self.come += 1
+
+    def copy(self, index):
+        k, b = self.links, self.base + index
+        ref = self.block(index)
+        return k.remote(ref, ref, b, b, wide=k.ws)
+
+    def send(self, index):
+        self.copy(index).start()
+
+    def wait(self, index):
+        self.links.arrived(self.twin(index), self.base + index)
+
+    def drain(self):
+        for index in range(self.number):
+            self.copy(index).wait_send()
 
 
 class Spread:
-    def __init__(self, links, src, dst, peers=WIDE, record=True):
-        self.links, self.src, self.dst, self.record = links, src, dst, record
+    def __init__(self, links, src, dst, peers=WIDE):
+        self.links, self.src, self.dst = links, src, dst
         self.step = 1 if peers == WIDE else 2
         self.base = links.take(WIDE)
 
     def distances(self):
         return range(self.step, WIDE, self.step)
 
+    def copy(self, d, to):
+        k, b = self.links, self.base + d
+        return k.remote(self.src(to), self.dst(k.w), b, b, wide=to)
+
     def start(self):
+        for d in self.distances():
+            self.copy(d, lax.rem(self.links.w + d, WIDE)).start()
+
+    def finish(self):
         k = self.links
         for d in self.distances():
-            to = lax.rem(k.w + d, WIDE)
-            k.go(self.src(to), self.dst(k.w), self.base + d, self.base + d, to, None, self.record)
+            k.arrived(self.dst(lax.rem(k.w + WIDE - d, WIDE)), self.base + d)
 
     def drain(self):
-        k = self.links
         for d in self.distances():
-            to = lax.rem(k.w + d, WIDE)
-            k.remote(self.src(to), self.dst(k.w), self.base + d, self.base + d, to).wait_send()
-
-    def wait(self, d):
-        self.links.arrived(self.dst(lax.rem(self.links.w + WIDE - d, WIDE)), self.base + d)
-
-    def finish(self):
-        for d in self.distances():
-            self.wait(d)
+            self.copy(d, lax.rem(self.links.w + d, WIDE)).wait_send()
 
 
 def row_scale(values):
@@ -462,366 +492,70 @@
     return same & (i >= j)
 
 
-def forward_kernel(
-    x_ref, wq, wk, wv, wg, wo, fv, fg, fo, dy, cols, rowdoc, passing, decay,
-    xn_o, wqk_o, wvg_o, wo_o, fv_o, fg_o, fo_o, dy_o, slope_o, qkv_o, sin_o, attn_o, gate_o, mixed_o,
-    x1_o, x1n_o,
-    xn, wqk, wvg, wout, slope, qkv, gates, sin, state, attn_s, attn, gate, mixed, x1, x1n,
-    send, recv, here,
-):
-    k = Links(send, recv, here)
-    w, n, core, chip = k.w, k.n, k.core, k.chip
-    head_cols = 2 * HEAD
-    tok = x_ref.shape[0]
-    ff = fv_o.shape[-1]
-
-    def wide_cols(index):
-        return at(index * head_cols, head_cols)
-
-    def chip_cols(index):
-        return pl.ds(pl.multiple_of(index * ff, 128), ff)
-
-    k.greet()
-    own = [k.keep(wo, wout.at[w, n])]
-    for m, (weight, to) in enumerate(((wq, wqk), (wk, wqk), (wv, wvg), (wg, wvg))):
-        own.append(
-            k.keep(weight.at[:, wide_cols(w)], to.at[w, n, :, pl.ds((m % 2) * head_cols, head_cols)])
-        )
-    own_ff = [
-        k.keep(fv.at[:, chip_cols(chip)], fv_o.at[chip, core, n]),
-        k.keep(fg.at[:, chip_cols(chip)], fg_o.at[chip, core, n]),
-        k.keep(fo, fo_o.at[core, n]),
-        k.keep(dy, dy_o.at[chip]),
-    ]
-
-    def norm_in(rows):
-        v = x_ref[rows, :].astype(F32)
-        xn[w, rows, :] = (v * row_scale(v)).astype(BF)
-
-    row_chunks(tok, norm_in)
-    k.met()
-
-    line_out = Line(k, lambda i: wout.at[w, i])
-    line_qk = Line(k, lambda i: wqk.at[:, i])
-    line_vg = Line(k, lambda i: wvg.at[:, i])
-    line_fv = Line(k, lambda i: fv_o.at[:, core, i])
-    line_fg = Line(k, lambda i: fg_o.at[:, core, i])
-    line_fo = Line(k, lambda i: fo_o.at[core, i])
-    spreads = []
-    for m, (weight, to) in enumerate(((wq, wqk), (wk, wqk), (wv, wvg), (wg, wvg))):
-        lanes = pl.ds((m % 2) * head_cols, head_cols)
-        spreads.append(
-            Spread(
-                k,
-                lambda t, weight=weight: weight.at[:, wide_cols(t)],
-                lambda s, to=to, lanes=lanes: to.at[s, n, :, lanes],
-            )
-        )
-    spread_ff = [
-        Spread(
-            k,
-            lambda t, weight=weight: weight.at[:, chip_cols(lax.div(t, 2))],
-            lambda s, to=to: to.at[lax.div(s, 2), core, n],
-            peers=CHIPS,
-        )
-        for weight, to in ((fv, fv_o), (fg, fg_o))
-    ]
-    half = tok // 2
-    plane_xn = Plane(k, lambda s, h: xn.at[s, pl.ds(h * half, half)])
-    plane_out = Plane(k, lambda s, h: wout.at[s, pl.ds(h * 2, 2)])
-    plane_dy = Plane(k, lambda s, h: dy_o.at[lax.div(s, 2), pl.ds(h * half, half)])
-    plane_x1n = Plane(k, lambda s, h: x1n_o.at[lax.div(s, 2), pl.ds(h * half, half)])
-    twin_xn = Sibling(k, lambda s: xn.at[s], 4)
-    twin_out = Sibling(k, lambda s: wout.at[s], 4)
-    twin_fv = Sibling(k, lambda s: fv_o.at[:, s], 1)
-    twin_fg = Sibling(k, lambda s: fg_o.at[:, s], 1)
-    twin_fo = Sibling(k, lambda s: fo_o.at[s], 1)
-    other = 1 - core
-
-    for copy in own:
-        copy.wait()
-    line_out.start()
-    for spread in spreads:
-        spread.start()
-    plane_xn.start()
-    twin_xn.send(w)
-    for spread in spread_ff:
-        spread.start()
-    spreads[0].finish()
-    spreads[1].finish()
-    line_qk.start()
-    spreads[2].finish()
-    spreads[3].finish()
-    line_vg.start()
-    line_out.forward()
-    plane_xn.forward()
-    line_out.finish()
-    plane_out.start()
-    twin_out.send(w)
-    plane_xn.finish_near()
-    twin_xn.send(k.wx)
-    twin_xn.send(k.wy)
-    line_qk.forward()
-    plane_xn.finish_far()
-    twin_xn.send(k.wd)
-    spread_ff[0].finish()
-    spread_ff[1].finish()
-    for copy in own_ff:
-        copy.wait()
-    line_fv.start()
-    line_fg.start()
-    line_fo.start()
-    line_vg.forward()
-    plane_out.forward()
-    for s in (k.ws, k.wx + 1 - 2 * core, k.wy + 1 - 2 * core, k.wd + 1 - 2 * core):
-        twin_xn.wait(s)
-    keep_xn = k.keep(xn, xn_o)
-    line_qk.finish()
-
-    def project_qk(t, carry):
-        v = dot(xn[t], wqk[...].reshape(-1, 2 * head_cols))
-        rows = at(t * tok, tok)
-        sigma = jax.nn.sigmoid(v)
-        slope[rows, :] = (sigma * (1.0 + v * (1.0 - sigma))).astype(BF)
-        qkv[rows, 0 : 2 * head_cols] = (v * sigma).astype(BF)
-        return carry
-
-    lax.fori_loop(0, WIDE, project_qk, 0)
-    keep_slope = k.keep(slope, slope_o)
-    keep_wqk = k.keep(wqk, wqk_o)
-    plane_out.finish_near()
-    twin_out.send(k.wx)
-    twin_out.send(k.wy)
-    line_vg.finish()
-
-    def project_vg(t, carry):
-        v = dot(xn[t], wvg[...].reshape(-1, 2 * head_cols)).astype(BF)
-        qkv[at(t * tok, tok), 2 * head_cols : 3 * head_cols] = v[:, 0:head_cols]
-        gates[t] = v[:, head_cols:]
-        return carry
-
-    lax.fori_loop(0, WIDE, project_vg, 0)
-    keep_wvg = k.keep(wvg, wvg_o)
-    keep_qkv = k.keep(qkv, qkv_o)
-    spread_gate = Spread(k, lambda t: gates.at[t], lambda s: gate.at[:, wide_cols(s)])
-    spread_gate.start()
-    gate[:, wide_cols(w)] = gates[w]
-
-    state[...] = jnp.zeros_like(state)
-    spread_attn = Spread(k, lambda t: attn_s.at[t], lambda s: attn.at[:, wide_cols(s)])
-
-    def attend(b, carry):
-        rows = at(b * BLOCK, BLOCK)
-        mask = doc_mask(cols, rowdoc, decay, rows, b)
-        for h in range(2):
-            lanes = slice(h * HEAD, (h + 1) * HEAD)
-            q = qkv[rows, h * HEAD : (h + 1) * HEAD]
-            key = qkv[rows, head_cols + h * HEAD : head_cols + (h + 1) * HEAD]
-            v = qkv[rows, 2 * head_cols + h * HEAD : 2 * head_cols + (h + 1) * HEAD]
-            probs = jnp.where(mask, dot_rt(q, key) * decay[h], 0.0).astype(BF)
-            before = state[h]
-            before_bf = before.astype(BF)
-            sin[b, h] = before_bf
-            entry = cols[rows, 1 + h : 2 + h]
-            tail = cols[rows, 3 + h : 4 + h]
-            out = dot(probs, v) + entry * dot(q, before_bf)
-            attn_s[b, :, lanes] = out.astype(BF)
-            tailed = (key.astype(F32) * tail).astype(BF)
-            state[h] = passing[pl.ds(2 * b + h, 1), :] * before + dot_lt(tailed, v)
-
-        @pl.when(b != w)
-        def _():
-            d = lax.rem(b - w + WIDE, WIDE)
-            base = spread_attn.base
-            k.remote(attn_s.at[b], attn.at[:, wide_cols(w)], base + d, base + d, wide=b).start()
-
-        @pl.when(b == w)
-        def _():
-            attn[:, wide_cols(w)] = attn_s[b]
-
-        return carry
-
-    lax.fori_loop(0, WIDE, attend, 0)
-    for d in spread_attn.distances():
-        to = lax.rem(w + d, WIDE)
-        k.sent.append(
-            k.remote(
-                attn_s.at[to], attn.at[:, wide_cols(w)], spread_attn.base + d, spread_attn.base + d,
-                wide=to,
-            )
-        )
-    keep_sin = k.keep(sin, sin_o)
-    plane_out.finish_far()
-    twin_out.send(k.wd)
-    plane_dy.start()
-    for s in (k.ws, k.wx + 1 - 2 * core, k.wy + 1 - 2 * core, k.wd + 1 - 2 * core):
-        twin_out.wait(s)
-    keep_wo = k.keep(wout, wo_o)
-    spread_gate.finish()
-    spread_attn.finish()
-    keep_attn = k.keep(attn, attn_o)
-    keep_gate = k.keep(gate, gate_o)
-
-    def mix(rows):
-        a = attn[rows, :].astype(F32)
-        mixed[rows, :] = (a * row_scale(a) * gate[rows, :].astype(F32)).astype(BF)
-
-    row_chunks(tok, mix)
-    keep_mixed = k.keep(mixed, mixed_o)
-
-    def project_out(j, carry):
-        lanes = at(j * 512, 512)
-        part = dot(mixed[...], wout[:, :, :, lanes].reshape(-1, 512))
-        x1[:, lanes] = x_ref[:, lanes].astype(F32) + part
-        return carry
-
-    lax.fori_loop(0, x1.shape[1] // 512, project_out, 0)
-    keep_x1 = k.keep(x1, x1_o)
-
-    def norm_mid(rows):
-        v = x1[rows, :]
-        x1n[rows, :] = (v * row_scale(v)).astype(BF)
-
-    row_chunks(tok, norm_mid)
-    k.keep(x1n, x1n_o.at[chip]).wait()
-    plane_x1n.start()
-    line_fv.forward()
-    plane_dy.forward()
-    plane_x1n.forward()
-    line_fg.forward()
-    line_fo.forward()
-    plane_dy.finish_near()
-    plane_dy.finish_far()
-    line_fv.finish()
-    twin_fv.send(core)
-    line_fg.finish()
-    twin_fg.send(core)
-    line_fo.finish()
-    twin_fo.send(core)
-    plane_x1n.finish_near()
-    plane_x1n.finish_far()
-    twin_fv.wait(other)
-    twin_fg.wait(other)
-    twin_fo.wait(other)
-    for copy in (
-        keep_xn, keep_slope, keep_wqk, keep_wvg, keep_qkv, keep_sin, keep_wo, keep_attn, keep_gate,
-        keep_mixed, keep_x1,
-    ):
-        copy.wait()
-    k.drain()
-
-
-def forward(tokens, weights, dy, cols, rowdoc, passing, decay):
-    tok, width = tokens.shape
-    shard = weights[0].shape[0]
-    full = WIDE * tok
-    ff = weights[5].shape[1] // CHIPS
-    fo_rows = weights[7].shape[0]
-    two = 2 * HEAD
-
-    def hbm(shape, dtype=BF):
-        return jax.ShapeDtypeStruct(shape, dtype)
-
-    out_shape = (
-        hbm((WIDE, tok, width)),
-        hbm((WIDE, NARROW, shard, 2 * two)),
-        hbm((WIDE, NARROW, shard, 2 * two)),
-        hbm((WIDE, NARROW, shard, width)),
-        hbm((CHIPS, 2, NARROW, shard, ff)),
-        hbm((CHIPS, 2, NARROW, shard, ff)),
-        hbm((2, NARROW, fo_rows, width)),
-        hbm((CHIPS, tok, width)),
-        hbm((full, 2 * two)),
-        hbm((full, 3 * two)),
-        hbm((WIDE, 2, HEAD, HEAD)),
-        hbm((tok, width)),
-        hbm((tok, width)),
-        hbm((tok, width)),
-        hbm((tok, width), F32),
-        hbm((CHIPS, tok, width)),
-    )
-    scratch = [
-        pltpu.VMEM((WIDE, tok, width), BF),
-        pltpu.VMEM((WIDE, NARROW, shard, 2 * two), BF),
-        pltpu.VMEM((WIDE, NARROW, shard, 2 * two), BF),
-        pltpu.VMEM((WIDE, NARROW, shard, width), BF),
-        pltpu.VMEM((full, 2 * two), BF),
-        pltpu.VMEM((full, 3 * two), BF),
-        pltpu.VMEM((WIDE, tok, two), BF),
-        pltpu.VMEM((WIDE, 2, HEAD, HEAD), BF),
-        pltpu.VMEM((2, HEAD, HEAD), F32),
-        pltpu.VMEM((WIDE, tok, two), BF),
-        pltpu.VMEM((tok, width), BF),
-        pltpu.VMEM((tok, width), BF),
-        pltpu.VMEM((tok, width), BF),
-        pltpu.VMEM((tok, width), F32),
-        pltpu.VMEM((tok, width), BF),
-        pltpu.SemaphoreType.DMA((136,)),
-        pltpu.SemaphoreType.DMA((136,)),
-        pltpu.SemaphoreType.DMA((24,)),
-    ]
-    return pl.pallas_call(
-        forward_kernel,
-        out_shape=out_shape,
-        in_specs=[VMEM] + [ANY] * 9 + [VMEM] * 4,
-        out_specs=(ANY,) * len(out_shape),
-        scratch_shapes=scratch,
-        compiler_params=pltpu.CompilerParams(
-            collective_id=0, has_side_effects=True, vmem_limit_bytes=60 * 2**20
-        ),
-        cost_estimate=pl.CostEstimate(flops=2 * 10**10, bytes_accessed=10**8, transcendentals=0),
-    )(tokens, *weights, dy, cols, rowdoc, passing, decay)
-
-
 class LineSum:
     def __init__(self, links, part, land):
         self.links, self.part, self.land = links, part, land
-        self.base = links.take(3)
-        self.over = 1 + lax.rem(links.n, 2)
-
-    def relay(self, slot):
+        self.base = links.take(5)
+        self.onward = links.pair + links.mid * (links.cross - links.pair)
+
+    def copy(self, index):
         k, b = self.links, self.base
-        return k.remote(self.part(k.cross), self.land(slot), b, b + slot, narrow=self.over)
-
-    def near(self):
-        k, b = self.links, self.base
-        return k.remote(self.part(k.pair), self.land(0), b + 1, b, narrow=k.pair)
-
-    def distant(self):
-        k, b = self.links, self.base
-        slot = 2 - k.mid
-        return k.remote(self.part(k.far), self.land(slot), b + 2, b + slot, narrow=k.far)
+        which, slot, to = (
+            (k.far, 3 * k.mid, self.onward),
+            (k.cross, 1 + 3 * k.mid, self.onward),
+            (k.pair, 2 - 2 * k.mid, k.pair),
+        )[index]
+        return k.remote(self.part(which), self.land(slot), b + index, b + slot, narrow=to)
 
     def start(self):
         @pl.when(self.links.mid == 0)
         def _():
-            self.relay(1).start()
-
-        self.distant().start()
-        self.near().start()
+            for index in range(3):
+                self.copy(index).start()
+
+    def wait(self, slot):
+        self.links.arrived(self.land(slot), self.base + slot)
 
     def forward(self, add):
         k = self.links
 
         @pl.when(k.mid == 1)
         def _():
-            k.arrived(self.land(1), self.base + 1)
+            self.wait(0)
+            add(self.part(k.far), self.land(0))
+            self.copy(0).start()
+            self.wait(1)
             add(self.part(k.cross), self.land(1))
-            self.relay(2).start()
-
-    def finish(self):
+            self.copy(1).start()
+
+    def forward_near(self, add):
         k = self.links
-        k.arrived(self.land(0), self.base)
-        k.arrived(self.land(2), self.base + 2)
+
+        @pl.when(k.mid == 1)
+        def _():
+            self.wait(3)
+            add(self.part(k.pair), self.land(3))
+            self.copy(2).start()
+
+    def finish(self, fetch, spots):
+        k = self.links
+        pl.when(k.mid == 0)(lambda: self.wait(0))
+
+        @pl.when(k.mid == 1)
+        def _():
+            self.wait(2)
+            self.wait(4)
+            fetch(self.land(4), spots.at[1])
+
+        fetch(self.land(2 * k.mid), spots.at[0])
 
         @pl.when(k.mid == 0)
         def _():
-            k.arrived(self.land(1), self.base + 1)
+            spots[1] = jnp.zeros(spots.shape[1:], spots.dtype)
 
     def drain(self):
-        self.relay(1).wait_send()
-        self.distant().wait_send()
-        self.near().wait_send()
+        for index in range(3):
+            self.copy(index).wait_send()
 
 
 class PlaneSum:
@@ -873,12 +607,13 @@
             self.copy(index).wait_send()
 
 
-def backward_kernel(
-    x_in, xn_in, wqk_in, wvg_in, wo_in, fv_in, fg_in, fo_in, dy_in, slope_in, qkv_in, sin_in,
-    attn_in, gate_in, mixed_in, x1_in, x1n_in, cols_in, decay_in, rowdoc, passing,
+def layer_kernel(
+    x_in, wq, wk, wv, wg, wo, fv, fg, fo, dy_arg, cols_in, decay_in, rowdoc, passing,
     result_o, dx_o, gq_o, gk_o, gv_o, gg_o, go_o, gfv_o, gfg_o, gfo_o,
-    corner, near, twin_fo, twin_ff, twin_wo, twin_xn, land_fo, land_ff, land_wo, land_qk, turn_ff,
-    turn_qk, a_land, g_land,
+    xn_in, wqk_in, wvg_in, wo_in, fv_in, fg_in, fo_in, dy_in, slope_in, qkv_in, sin_in, attn_in,
+    gate_in, mixed_in, x1_in, x1n_in,
+    corner, near, twin_fo_land, twin_ff, twin_wo, twin_xn_land, land_fo, land_ff, land_wo, land_qk,
+    turn_ff, turn_qk, a_land, g_land,
     g_fo, g_fv, g_fg, stage, acc, tmp, tmp_ff,
     send, recv, here,
 ):
@@ -914,13 +649,11 @@
     add_fo = adder(tmp.at[pl.ds(0, fo_rows)])
     add_wo = adder(tmp.at[pl.ds(0, 64)])
     add_ff = adder(tmp_ff)
-    k.kept.append(None)
-
     def fo_part(owner, i):
         return g_fo.at[pl.ds(pl.multiple_of((owner * NARROW + i) * fo_rows, 16), fo_rows)]
 
-    line_fo = LineSum(k, lambda i: fo_part(core, i), lambda s: land_fo.at[s])
-    line_ff = [
+    sum_fo = LineSum(k, lambda i: fo_part(core, i), lambda s: land_fo.at[s])
+    sum_ff = [
         LineSum(k, lambda i, g=g: g.at[:, i], lambda s, m=m: land_ff.at[m, s])
         for m, g in enumerate((g_fv, g_fg))
     ]
@@ -934,16 +667,277 @@
         sem = twin_base + 4 * m + j
         return k.remote(src, dst, sem, sem, wide=k.ws)
 
+    def wide_cols(index):
+        return at(index * two, two)
+
+    def chip_cols(index):
+        return pl.ds(pl.multiple_of(index * ff, 128), ff)
+
+    projections = ((wq, wqk_in), (wk, wqk_in), (wv, wvg_in), (wg, wvg_in))
+    lines = line_out, line_qk, line_vg, line_fv, line_fg, line_fo = (
+        Line(k, lambda i: wo_in.at[w, i]),
+        Line(k, lambda i: wqk_in.at[:, i]),
+        Line(k, lambda i: wvg_in.at[:, i]),
+        Line(k, lambda i: fv_in.at[:, core, i]),
+        Line(k, lambda i: fg_in.at[:, core, i]),
+        Line(k, lambda i: fo_in.at[core, i]),
+    )
+    spreads = [
+        Spread(
+            k,
+            lambda t, weight=weight: weight.at[:, wide_cols(t)],
+            lambda s, m=m, to=to: to.at[s, n, :, pl.ds((m % 2) * two, two)],
+        )
+        for m, (weight, to) in enumerate(projections)
+    ]
+    spread_ff = [
+        Spread(
+            k,
+            lambda t, weight=weight: weight.at[:, chip_cols(lax.div(t, 2))],
+            lambda s, to=to: to.at[lax.div(s, 2), core, n],
+            peers=CHIPS,
+        )
+        for weight, to in ((fv, fv_in), (fg, fg_in))
+    ]
+    planes = plane_xn, plane_out, plane_dy, plane_x1n = (
+        Plane(k, lambda s, h: xn_in.at[s, pl.ds(h * half, half)]),
+        Plane(k, lambda s, h: wo_in.at[s, pl.ds(h * 2, 2)]),
+        Plane(k, lambda s, h: dy_in.at[lax.div(s, 2), pl.ds(h * half, half)]),
+        Plane(k, lambda s, h: x1n_in.at[lax.div(s, 2), pl.ds(h * half, half)]),
+    )
+    here4 = (w, k.wx, k.wy, k.wd)
+    there4 = tuple(s + 1 - 2 * core for s in here4)
+    near4 = (n, k.pair, k.cross, k.far)
+    twins = twin_xn, twin_out, twin_fv, twin_fg, twin_fo = (
+        Sibling(k, lambda i: xn_in.at[here4[i]], lambda i: xn_in.at[there4[i]], 4),
+        Sibling(k, lambda i: wo_in.at[here4[i]], lambda i: wo_in.at[there4[i]], 4),
+        Sibling(k, lambda i: fv_in.at[:, core, near4[i]], lambda i: fv_in.at[:, other, near4[i]], 4),
+        Sibling(k, lambda i: fg_in.at[:, core, near4[i]], lambda i: fg_in.at[:, other, near4[i]], 4),
+        Sibling(k, lambda i: fo_in.at[core, near4[i]], lambda i: fo_in.at[other, near4[i]], 4),
+    )
+
     k.greet()
+    own_out = k.keep(wo, wo_in.at[w, n])
+    own_in = [
+        k.keep(weight.at[:, wide_cols(w)], to.at[w, n, :, pl.ds((m % 2) * two, two)])
+        for m, (weight, to) in enumerate(projections)
+    ]
+    own_ff = [
+        k.keep(fv.at[:, chip_cols(chip)], fv_in.at[chip, core, n]),
+        k.keep(fg.at[:, chip_cols(chip)], fg_in.at[chip, core, n]),
+        k.keep(fo, fo_in.at[core, n]),
+        k.keep(dy_arg, dy_in.at[chip]),
+    ]
+
+    def before(
+        x, xn, wqk, wvg, wout, slope, qkv, gates, sin, state, attn_s, attn, gate, mixed, x1, x1n,
+        cols, decay,
+    ):
+        k.keep(x_in, x).wait()
+
+        def norm_in(rows):
+            v = x[rows, :].astype(F32)
+            x1n[rows, :] = (v * row_scale(v)).astype(BF)
+
+        row_chunks(tok, norm_in)
+        own_xn = k.keep(x1n, xn_in.at[w])
+        load_cols, load_decay = k.keep(cols_in, cols), k.keep(decay_in, decay)
+        k.met()
+        own_out.wait()
+        line_out.start()
+        for spread in spreads:
+            spread.start()
+        own_xn.wait()
+        plane_xn.start()
+        twin_xn.send(0)
+        for spread in spread_ff:
+            spread.start()
+        for copy in own_in:
+            copy.wait()
+        spreads[0].finish()
+        spreads[1].finish()
+        line_qk.start()
+        spreads[2].finish()
+        spreads[3].finish()
+        line_vg.start()
+        line_out.forward()
+        plane_xn.forward()
+        line_out.forward_far()
+        line_qk.forward()
+        plane_xn.finish_near()
+        twin_xn.send(1)
+        twin_xn.send(2)
+        line_vg.forward()
+        line_qk.forward_far()
+        line_out.finish()
+        plane_out.start()
+        twin_out.send(0)
+        plane_xn.finish_far()
+        twin_xn.send(3)
+        line_vg.forward_far()
+        spread_ff[0].finish()
+        spread_ff[1].finish()
+        for copy in own_ff:
+            copy.wait()
+        line_fv.start()
+        for i in range(4):
+            twin_xn.wait(i)
+        load_xn = k.keep(xn_in, xn)
+        plane_out.forward()
+        line_qk.finish()
+        load_qk = k.keep(wqk_in, wqk)
+        load_xn.wait()
+        load_qk.wait()
+
+        def project_qk(t, carry):
+            v = dot(xn[t], wqk[...].reshape(width, 2 * two))
+            rows = at(t * tok, tok)
+            sigma = jax.nn.sigmoid(v)
+            slope[rows, :] = (sigma * (1.0 + v * (1.0 - sigma))).astype(BF)
+            qkv[rows, 0 : 2 * two] = (v * sigma).astype(BF)
+            return carry
+
+        lax.fori_loop(0, WIDE, project_qk, 0)
+        stores = [k.keep(slope, slope_in)]
+        plane_out.finish_near()
+        twin_out.send(1)
+        twin_out.send(2)
+        line_vg.finish()
+        k.keep(wvg_in, wvg).wait()
+
+        def project_vg(t, carry):
+            v = dot(xn[t], wvg[...].reshape(width, 2 * two)).astype(BF)
+            qkv[at(t * tok, tok), 2 * two : 3 * two] = v[:, 0:two]
+            gates[t] = v[:, two:]
+            return carry
+
+        lax.fori_loop(0, WIDE, project_vg, 0)
+        line_fv.forward()
+        line_fg.start()
+        stores.append(k.keep(qkv, qkv_in))
+        spread_gate = Spread(k, lambda t: gates.at[t], lambda s: gate_in.at[:, wide_cols(s)])
+        spread_gate.start()
+        own = [k.keep(gates.at[w], gate_in.at[:, wide_cols(w)])]
+        load_cols.wait()
+        load_decay.wait()
+        state[...] = jnp.zeros_like(state)
+        spread_attn = Spread(k, lambda t: attn_s.at[t], lambda s: attn_in.at[:, wide_cols(s)])
+
+        def attend(b, carry):
+            rows = at(b * BLOCK, BLOCK)
+            mask = doc_mask(cols, rowdoc, decay, rows, b)
+            for h in range(2):
+                lanes = slice(h * HEAD, (h + 1) * HEAD)
+                q = qkv[rows, lanes]
+                key = qkv[rows, two + h * HEAD : two + (h + 1) * HEAD]
+                v = qkv[rows, 2 * two + h * HEAD : 2 * two + (h + 1) * HEAD]
+                probs = jnp.where(mask, dot_rt(q, key) * decay[h], 0.0).astype(BF)
+                old = state[h]
+                old_bf = old.astype(BF)
+                sin[b, h] = old_bf
+                entry = cols[rows, 1 + h : 2 + h]
+                tail = cols[rows, 3 + h : 4 + h]
+                out = dot(probs, v) + entry * dot(q, old_bf)
+                attn_s[b, :, lanes] = out.astype(BF)
+                tailed = (key.astype(F32) * tail).astype(BF)
+                state[h] = passing[pl.ds(2 * b + h, 1), :] * old + dot_lt(tailed, v)
+
+            @pl.when(b != w)
+            def _():
+                spread_attn.copy(lax.rem(b - w + WIDE, WIDE), b).start()
+
+            return carry
+
+        lax.fori_loop(0, WIDE, attend, 0)
+        stores.append(k.keep(sin, sin_in))
+        own.append(k.keep(attn_s.at[w], attn_in.at[:, wide_cols(w)]))
+        plane_out.finish_far()
+        twin_out.send(3)
+        for i in range(4):
+            twin_out.wait(i)
+        load_out = k.keep(wo_in, wout)
+        line_fv.forward_far()
+        spread_gate.finish()
+        spread_attn.finish()
+        for copy in own:
+            copy.wait()
+        loads = [k.keep(attn_in, attn), k.keep(gate_in, gate)]
+        for copy in loads:
+            copy.wait()
+
+        def mix(rows):
+            a = attn[rows, :].astype(F32)
+            mixed[rows, :] = (a * row_scale(a) * gate[rows, :].astype(F32)).astype(BF)
+
+        row_chunks(tok, mix)
+        stores.append(k.keep(mixed, mixed_in))
+        load_out.wait()
+
+        def project_out(j, carry):
+            lanes = at(j * 512, 512)
+            part = dot(mixed[...], wout[:, :, :, lanes].reshape(-1, 512))
+            x1[:, lanes] = x[:, lanes].astype(F32) + part
+            return carry
+
+        lax.fori_loop(0, width // 512, project_out, 0)
+        stores.append(k.keep(x1, x1_in))
+
+        def norm_mid(rows):
+            v = x1[rows, :]
+            x1n[rows, :] = (v * row_scale(v)).astype(BF)
+
+        row_chunks(tok, norm_mid)
+        k.keep(x1n, x1n_in.at[chip]).wait()
+        plane_x1n.start()
+        line_fg.forward()
+        line_fo.start_away()
+        plane_x1n.forward()
+        plane_dy.start()
+        line_fg.forward_far()
+        for copy in stores:
+            copy.wait()
+        spread_gate.drain()
+        spread_attn.drain()
+
+    pl.run_scoped(
+        before,
+        pltpu.VMEM((tok, width), BF),
+        pltpu.VMEM((WIDE, tok, width), BF),
+        pltpu.VMEM(wqk_in.shape, BF),
+        pltpu.VMEM(wvg_in.shape, BF),
+        pltpu.VMEM(wo_in.shape, BF),
+        pltpu.VMEM(slope_in.shape, BF),
+        pltpu.VMEM(qkv_in.shape, BF),
+        pltpu.VMEM((WIDE, tok, two), BF),
+        pltpu.VMEM(sin_in.shape, BF),
+        pltpu.VMEM((2, HEAD, HEAD), F32),
+        pltpu.VMEM((WIDE, tok, two), BF),
+        pltpu.VMEM((tok, width), BF),
+        pltpu.VMEM((tok, width), BF),
+        pltpu.VMEM((tok, width), BF),
+        pltpu.VMEM((tok, width), F32),
+        pltpu.VMEM((tok, width), BF),
+        pltpu.VMEM(cols_in.shape, F32),
+        pltpu.VMEM(decay_in.shape, F32),
+    )
 
     def ffn(x1n, dy, fvw, fgw, fow, mix, val, gat, side):
-        loads = [
-            k.keep(x1n_in, x1n), k.keep(fv_in, fvw), k.keep(fg_in, fgw), k.keep(dy_in, dy),
-            k.keep(fo_in, fow),
-        ]
-        for copy in loads[:3]:
+        line_fv.finish(twin_fv.send)
+        plane_x1n.finish_near()
+        plane_x1n.finish_far()
+        load_x1n = k.keep(x1n_in, x1n)
+        for i in range(4):
+            twin_fv.wait(i)
+        load_fv = k.keep(fv_in, fvw)
+        line_fo.forward()
+        line_fg.finish(twin_fg.send)
+        line_fo.start_home()
+        for i in range(4):
+            twin_fg.wait(i)
+        load_fg = k.keep(fg_in, fgw)
+        plane_dy.forward()
+        for copy in (load_x1n, load_fv, load_fg):
             copy.wait()
-        k.met()
 
         def up(j, carry):
             v = dot(x1n[j], fvw[...].reshape(width, ff))
@@ -953,10 +947,13 @@
             gat[j] = g.astype(BF)
             return carry
 
-        lax.fori_loop(0, CHIPS, up, 0)
-
-        for copy in loads[3:]:
-            copy.wait()
+        lax.fori_loop(0, CHIPS // 2, up, 0)
+        line_fo.forward_far()
+        plane_dy.finish_near()
+        plane_dy.finish_far()
+        load_dy = k.keep(dy_in, dy)
+        lax.fori_loop(CHIPS // 2, CHIPS, up, 0)
+        load_dy.wait()
 
         def fo_grad(j, carry):
             chunk = lax.rem(j + 2 * other, chunks)
@@ -971,24 +968,33 @@
         chunks = pl.cdiv(ff, 256)
         lax.fori_loop(0, 4, fo_grad, 0)
         for i in range(NARROW):
-            twin(0, i, fo_part(other, i), twin_fo.at[i]).start()
+            twin(0, i, fo_part(other, i), twin_fo_land.at[i]).start()
         lax.fori_loop(4, chunks, fo_grad, 0)
         for i in range(NARROW):
-            copy = twin(0, i, fo_part(other, i), twin_fo.at[i])
+            copy = twin(0, i, fo_part(other, i), twin_fo_land.at[i])
             copy.wait_recv()
-            add_fo(fo_part(core, i), twin_fo.at[i])
+            add_fo(fo_part(core, i), twin_fo_land.at[i])
             copy.wait_send()
-        line_fo.start()
-
-        def down(j, carry):
-            q = nth(j)
+        sum_fo.start()
+        line_fo.finish(twin_fo.send)
+        for i in range(4):
+            twin_fo.wait(i)
+        k.keep(fo_in, fow).wait()
+
+        def down(q, carry):
             d_mix = dot_rt(dy[q], fow[...].reshape(ff, width))
             d_val = (d_mix * gat[q].astype(F32)).astype(BF)
             d_gat = (d_mix * val[q].astype(F32)).astype(BF)
             val[q] = d_val
             gat[q] = d_gat
-
-            def back(i, carry):
+            return carry
+
+        lax.fori_loop(0, CHIPS, down, 0)
+
+        def back(j, carry):
+            q = nth(j)
+
+            def back_lanes(i, carry):
                 lanes = at(i * 512, 512)
                 d_x = dot_rt(val[q], fvw[i].reshape(512, ff)) + dot_rt(
                     gat[q], fgw[i].reshape(512, ff)
@@ -1001,16 +1007,10 @@
 
                 return carry
 
-            lax.fori_loop(0, width // 512, back, 0)
-
+            lax.fori_loop(0, width // 512, back_lanes, 0)
             for step, push in enumerate((plane_mid.send_far, plane_mid.send_x, plane_mid.send_y)):
                 pl.when(j == step)(push)
-
             return carry
-
-        lax.fori_loop(0, CHIPS, down, 0)
-        plane_mid.combine(add_half)
-        line_fo.forward(add_fo)
 
         for m, (d_ff, g_ff) in enumerate(((val, g_fv), (gat, g_fg))):
 
@@ -1042,15 +1042,18 @@
                 add_ff(g_ff.at[q], twin_ff.at[m, q])
                 if q >= 2:
                     copy.wait_send()
-            line_ff[m].start()
-
+            sum_ff[m].start()
+            if m == 0:
+                lax.fori_loop(0, CHIPS, back, 0)
+                plane_mid.combine(add_half)
+                sum_fo.forward(add_fo)
+
+        sum_fo.forward_near(add_fo)
         plane_mid.drain()
 
         def out_step(j, carry):
             q = nth(j)
             stage[q] = dot(mix[q], fow[...].reshape(ff, width)).astype(BF)
-            for step, push in enumerate((plane_res.send_far, plane_res.send_x, plane_res.send_y)):
-                pl.when(j == step)(push)
             return carry
 
         lax.fori_loop(0, CHIPS, out_step, 0)
@@ -1071,26 +1074,25 @@
     def rest(d_x1, d_branch, mixed, da_src, dg_src, side, stage_wo, own_res, g_wo, g_qk, g_vg):
         plane_out = plane_sum(2, stage_wo)
         own_res[...] = stage[chip]
-        line_wo = LineSum(k, lambda i: g_wo.at[i], lambda s: land_wo.at[s])
-        line_qk = [
+        sum_wo = LineSum(k, lambda i: g_wo.at[i], lambda s: land_wo.at[s])
+        sum_qk = [
             LineSum(k, lambda i, g=g: g.at[:, i], lambda s, m=m: land_qk.at[m, s])
             for m, g in enumerate((g_qk, g_vg))
         ]
         spread_a = Spread(
-            k, lambda t: da_src.at[:, at(t * two, two)], lambda s: a_land.at[s], record=False
+            k, lambda t: da_src.at[:, at(t * two, two)], lambda s: a_land.at[s]
         )
         spread_g = Spread(
-            k, lambda t: dg_src.at[:, at(t * two, two)], lambda s: g_land.at[s], record=False
+            k, lambda t: dg_src.at[:, at(t * two, two)], lambda s: g_land.at[at(s * tok, tok)]
         )
 
         def middle(wo, x1, attn, gate, dy, d_mixed, pair):
-            loads = [k.keep(x1_in, x1), k.keep(dy_in.at[chip], dy)]
+            plane_mid.finish()
+            loads = [k.keep(near.at[0], pair), k.keep(x1_in, x1), k.keep(dy_in.at[chip], dy)]
             late = [
-                k.keep(attn_in, attn), k.keep(gate_in, gate), k.keep(wo_in, wo),
+                k.keep(wo_in, wo), k.keep(attn_in, attn), k.keep(gate_in, gate),
                 k.keep(mixed_in, mixed),
             ]
-            plane_mid.finish()
-            fetch(near.at[0], pair)
             for copy in loads:
                 copy.wait()
 
@@ -1129,9 +1131,12 @@
             row_chunks(tok, attn_back)
             spread_a.start()
             spread_g.start()
+            plane_res.send_far()
+            plane_res.send_x()
+            plane_res.send_y()
             own = [
                 k.keep(da_src.at[:, at(w * two, two)], a_land.at[w]),
-                k.keep(dg_src.at[:, at(w * two, two)], g_land.at[w]),
+                k.keep(dg_src.at[:, at(w * two, two)], g_land.at[at(w * tok, tok)]),
             ]
 
             for copy in own:
@@ -1139,7 +1144,7 @@
 
         pl.run_scoped(
             middle,
-            pltpu.VMEM((WIDE, tok, width), BF),
+            pltpu.VMEM(wo_in.shape, BF),
             pltpu.VMEM((tok, width), F32),
             pltpu.VMEM((tok, width), BF),
             pltpu.VMEM((tok, width), BF),
@@ -1147,8 +1152,6 @@
             pltpu.VMEM((tok, width), F32),
             pltpu.VMEM((2, tok, width), BF),
         )
-        plane_res.combine(add_half)
-
         def eight_way(plane, twin_index, landing, blocks, term):
             def side_step(j, carry):
                 q = nth(j)
@@ -1189,12 +1192,12 @@
             stage_wo,
             lambda owner: dot_lt(mixed[:, at(owner * tok, tok)], d_branch[...]),
         )
-        line_ff[0].forward(add_ff)
+        sum_ff[0].forward(add_ff)
 
         def attention(xn, d_qk, d_vg, state):
             state[...] = jnp.zeros_like(state)
 
-            def heads(slope, qkv, sin, cols, decay, d_attn, d_gate):
+            def heads(slope, qkv, sin, cols, decay, d_attn):
                 loads = [
                     k.keep(qkv_in, qkv), k.keep(sin_in, sin), k.keep(slope_in, slope),
                     k.keep(cols_in, cols), k.keep(decay_in, decay),
@@ -1203,10 +1206,7 @@
                 for copy in loads:
                     copy.wait()
                 spread_a.finish()
-                spread_g.finish()
-                loads = [k.keep(a_land, d_attn), k.keep(g_land, d_gate)]
-                for copy in loads:
-                    copy.wait()
+                fetch(a_land, d_attn)
 
                 def step(i, carry):
                     b = WIDE - 1 - i
@@ -1236,10 +1236,13 @@
                         d_qk[rows, key_lanes] = (d_k * slope[rows, key_lanes].astype(F32)).astype(BF)
                         d_vg[rows, lanes] = d_v.astype(BF)
                         state[h] = passing[pl.ds(2 * b + h, 1), :] * after + dot_lt(entered, d_o)
-                    d_vg[rows, two:] = d_gate[b]
                     return carry
 
                 lax.fori_loop(0, WIDE, step, 0)
+                sum_ff[0].forward_near(add_ff)
+                spread_g.finish()
+                load_g = k.keep(g_land, d_vg.at[:, pl.ds(two, two)])
+                load_g.wait()
                 load_xn.wait()
 
             pl.run_scoped(
@@ -1250,10 +1253,8 @@
                 pltpu.VMEM(cols_in.shape, F32),
                 pltpu.VMEM(decay_in.shape, F32),
                 pltpu.VMEM((WIDE, tok, two), BF),
-                pltpu.VMEM((WIDE, tok, two), BF),
             )
 
-            plane_out.combine(add_half)
             for m, (d_in, g_in) in enumerate(((d_qk, g_qk), (d_vg, g_vg))):
 
                 def in_grad(s, carry):
@@ -1262,17 +1263,13 @@
                     return carry
 
                 lax.fori_loop(0, WIDE, in_grad, 0)
-                line_qk[m].start()
-
-            line_ff[1].forward(add_ff)
-            plane_out.finish()
-            for side_index in range(2):
-                fetch(near.at[2, side_index], tmp)
-                acc[...] = acc[...] + tmp[...].astype(F32)
+                sum_qk[m].start()
+
+            plane_res.combine(add_half)
+            plane_out.combine(add_half)
+            sum_ff[1].forward(add_ff)
+            plane_res.drain()
             g_wo[...] = acc[...].astype(BF).reshape(g_wo.shape)
-            line_wo.start()
-            plane_out.drain()
-            plane_res.drain()
 
             def spread_in(wqk, wvg):
                 loads = [k.keep(wqk_in, wqk), k.keep(wvg_in, wvg)]
@@ -1285,7 +1282,7 @@
                         d_vg[rows, :], wvg[...].reshape(width, 2 * two)
                     )
 
-                eight_way(plane_in, 4, twin_xn, stage, term)
+                eight_way(plane_in, 4, twin_xn_land, stage, term)
 
             pl.run_scoped(spread_in, pltpu.VMEM(wqk_in.shape, BF), pltpu.VMEM(wvg_in.shape, BF))
 
@@ -1302,35 +1299,39 @@
         ):
             add_qk = adder(tmp_qk)
             load_x, load_x1 = k.keep(x_in, x), k.keep(x1_in, x1)
+            plane_in.combine(add_half)
+            sum_ff[1].forward_near(add_ff)
+            plane_out.finish()
+            fetch(near.at[2], pair)
+            for i in range(NARROW):
+                rows = pl.ds(i * 64, 64)
+                v = g_wo[i].astype(F32) + pair[0, rows, :].astype(F32) + pair[1, rows, :].astype(F32)
+                g_wo[i] = v.astype(BF)
+            sum_wo.start()
 
             def total(part, lands):
-                extra = jnp.where(k.mid == 0, lands[1].astype(F32), 0.0)
-                return part.astype(F32) + lands[0].astype(F32) + lands[2].astype(F32) + extra
+                return part.astype(F32) + lands[0].astype(F32) + lands[1].astype(F32)
 
             ff_turns = []
             for m, g_ff in enumerate((g_fv, g_fg)):
-                line_ff[m].finish()
-                fetch(land_ff.at[m], three_ff)
+                sum_ff[m].finish(fetch, three_ff)
                 for q in range(CHIPS):
-                    ff_src[m, q] = total(g_ff[q, n], [three_ff[s, q] for s in range(3)]).astype(BF)
+                    ff_src[m, q] = total(g_ff[q, n], three_ff[:, q]).astype(BF)
                 turn = Spread(
                     k,
                     lambda t, m=m: ff_src.at[m, lax.div(t, 2)],
                     lambda s, m=m: turn_ff.at[m, lax.div(s, 2)],
                     peers=CHIPS,
-                    record=False,
                 )
                 turn.start()
                 ff_turns.append((turn, k.keep(ff_src.at[m, chip], turn_ff.at[m, chip])))
-            plane_in.combine(add_half)
-            line_fo.finish()
-            fetch(land_fo, three.at[:, pl.ds(0, fo_rows)])
+            sum_qk[0].forward(add_qk)
+            sum_fo.finish(fetch, three.at[:, pl.ds(0, fo_rows)])
             own = fo_part(core, n)
             for r in range(0, fo_rows, 16):
                 rows = pl.ds(r, 16)
-                w_fo[rows, :] = total(own[rows, :], [three[s, rows, :] for s in range(3)])
+                w_fo[rows, :] = total(own[rows, :], three[:, rows, :])
             stores = [k.keep(w_fo, gfo_o)]
-            line_qk[0].forward(add_qk)
 
             plane_res.finish()
             fetch(near.at[1], pair)
@@ -1343,6 +1344,8 @@
 
             row_chunks(tok, add_up)
             stores.append(k.keep(own_res, result_o))
+            sum_qk[1].forward(add_qk)
+            sum_qk[0].forward_near(add_qk)
             load_x.wait()
             plane_in.finish()
             fetch(near.at[3], pair)
@@ -1365,26 +1368,24 @@
                 for q in range(CHIPS):
                     ff_f32[m, :, q * ff : (q + 1) * ff] = ff_all[q].astype(F32)
                 stores.append(k.keep(ff_f32.at[m], (gfv_o, gfg_o)[m]))
-            line_qk[1].forward(add_qk)
+            sum_wo.forward(add_wo)
+            sum_qk[1].forward_near(add_qk)
             qk_turns = []
             for m, g_in in enumerate((g_qk, g_vg)):
-                line_qk[m].finish()
-                fetch(land_qk.at[m], three_qk)
+                sum_qk[m].finish(fetch, three_qk)
                 for s in range(WIDE):
-                    qk_src[m, s] = total(g_in[s, n], [three_qk[i, s] for i in range(3)]).astype(BF)
+                    qk_src[m, s] = total(g_in[s, n], three_qk[:, s]).astype(BF)
                 turn = Spread(
                     k,
                     lambda t, m=m: qk_src.at[m, t],
                     lambda s, m=m: turn_qk.at[m, s],
-                    record=False,
                 )
                 turn.start()
                 qk_turns.append((turn, k.keep(qk_src.at[m, w], turn_qk.at[m, w])))
                 if m == 0:
-                    line_wo.forward(add_wo)
-            line_wo.finish()
-            fetch(land_wo, three.at[:, pl.ds(0, 64)])
-            w_f32[4] = total(g_wo[n], [three[s, 0:64, :] for s in range(3)])
+                    sum_wo.forward_near(add_wo)
+            sum_wo.finish(fetch, three.at[:, pl.ds(0, 64)])
+            w_f32[4] = total(g_wo[n], three[:, 0:64, :])
             stores.append(k.keep(w_f32.at[4], go_o))
             for m, (turn, copy) in enumerate(qk_turns):
                 turn.finish()
@@ -1400,8 +1401,11 @@
             for copy in stores:
                 copy.wait()
             plane_in.drain()
+            plane_out.drain()
             turns = [turn for turn, copy in ff_turns + qk_turns]
-            for sums in (line_fo, line_wo, *line_ff, *line_qk, spread_a, spread_g, *turns):
+            for moved in (*lines, *planes, *twins, *spreads, *spread_ff):
+                moved.drain()
+            for sums in (sum_fo, sum_wo, *sum_ff, *sum_qk, spread_a, spread_g, *turns):
                 sums.drain()
 
         pl.run_scoped(
@@ -1409,9 +1413,9 @@
             pltpu.VMEM((tok, width), BF),
             pltpu.VMEM((tok, width), F32),
             pltpu.VMEM((2, tok, width), BF),
-            pltpu.VMEM((3, tok, width), BF),
-            pltpu.VMEM(land_ff.shape[1:], BF),
-            pltpu.VMEM(land_qk.shape[1:], BF),
+            pltpu.VMEM((2, tok, width), BF),
+            pltpu.VMEM((2, *land_ff.shape[2:]), BF),
+            pltpu.VMEM((2, *land_qk.shape[2:]), BF),
             pltpu.VMEM((2, CHIPS, 64, ff), BF),
             pltpu.VMEM((2, WIDE, 64, 2 * two), BF),
             pltpu.VMEM((CHIPS, 64, ff), BF),
@@ -1436,64 +1440,86 @@
         pltpu.VMEM((WIDE, NARROW, 64, 2 * two), BF),
         pltpu.VMEM((WIDE, NARROW, 64, 2 * two), BF),
     )
-
-
-def backward(tokens, kept, cols, rowdoc, passing, decay):
+    assert k.count <= send.shape[0] and k.kept <= here.shape[0], (k.count, k.kept)
+
+
+def layer(tokens, weights, dy, cols, rowdoc, passing, decay):
     tok, width = tokens.shape
-    fv, fo = kept[4], kept[6]
-    shard, ff, fo_rows = fv.shape[3], fv.shape[4], fo.shape[2]
+    shard = weights[0].shape[0]
+    ff = weights[5].shape[1] // CHIPS
+    fo_rows = weights[7].shape[0]
+    full = WIDE * tok
     two = 2 * HEAD
 
     def arr(*shape, dtype=BF):
         return jax.ShapeDtypeStruct(shape, dtype)
 
-    square = [arr(shard, width, dtype=F32)] * 5
-    out_shape = (
+    results = (
         arr(tok, width),
         arr(tok, width, dtype=F32),
-        *square,
+        *[arr(shard, width, dtype=F32)] * 5,
         arr(shard, CHIPS * ff, dtype=F32),
         arr(shard, CHIPS * ff, dtype=F32),
         arr(fo_rows, width, dtype=F32),
+    )
+    held = (
+        arr(WIDE, tok, width),
+        arr(WIDE, NARROW, shard, 2 * two),
+        arr(WIDE, NARROW, shard, 2 * two),
+        arr(WIDE, NARROW, shard, width),
+        arr(CHIPS, 2, NARROW, shard, ff),
+        arr(CHIPS, 2, NARROW, shard, ff),
+        arr(2, NARROW, fo_rows, width),
+        arr(CHIPS, tok, width),
+        arr(full, 2 * two),
+        arr(full, 3 * two),
+        arr(WIDE, 2, HEAD, HEAD),
+        arr(tok, width),
+        arr(tok, width),
+        arr(tok, width),
+        arr(tok, width, dtype=F32),
+        arr(CHIPS, tok, width),
+    )
+    landings = (
         arr(4, 2, tok // 2, width),
         arr(4, 2, tok, width),
         arr(NARROW, fo_rows, width),
         arr(2, CHIPS, NARROW, shard, ff),
         arr(CHIPS, tok, width),
         arr(CHIPS, tok, width),
-        arr(3, fo_rows, width),
-        arr(2, 3, CHIPS, shard, ff),
-        arr(3, shard, width),
-        arr(2, 3, WIDE, shard, 2 * two),
+        arr(5, fo_rows, width),
+        arr(2, 5, CHIPS, shard, ff),
+        arr(5, shard, width),
+        arr(2, 5, WIDE, shard, 2 * two),
         arr(2, CHIPS, shard, ff),
         arr(2, WIDE, shard, 2 * two),
         arr(WIDE, tok, two),
-        arr(WIDE, tok, two),
-    )
-    scratch = [
-        pltpu.VMEM((CHIPS * ff // CHIPS, width), BF),
-        pltpu.VMEM((CHIPS, NARROW, shard, ff), BF),
-        pltpu.VMEM((CHIPS, NARROW, shard, ff), BF),
-        pltpu.VMEM((CHIPS, tok, width), BF),
-        pltpu.VMEM((tok, width), F32),
-        pltpu.VMEM((tok, width), BF),
-        pltpu.VMEM((CHIPS, shard, ff), BF),
-        pltpu.SemaphoreType.DMA((112,)),
-        pltpu.SemaphoreType.DMA((112,)),
-        pltpu.SemaphoreType.DMA((48,)),
-    ]
+        arr(full, two),
+    )
+    out_shape = results + held + landings
     outs = pl.pallas_call(
-        backward_kernel,
+        layer_kernel,
         out_shape=out_shape,
-        in_specs=[ANY] * 19 + [VMEM] * 2,
+        in_specs=[ANY] * 12 + [VMEM] * 2,
         out_specs=(ANY,) * len(out_shape),
-        scratch_shapes=scratch,
+        scratch_shapes=[
+            pltpu.VMEM((ff, width), BF),
+            pltpu.VMEM((CHIPS, NARROW, shard, ff), BF),
+            pltpu.VMEM((CHIPS, NARROW, shard, ff), BF),
+            pltpu.VMEM((CHIPS, tok, width), BF),
+            pltpu.VMEM((tok, width), F32),
+            pltpu.VMEM((tok, width), BF),
+            pltpu.VMEM((CHIPS, shard, ff), BF),
+            pltpu.SemaphoreType.DMA((272,)),
+            pltpu.SemaphoreType.DMA((272,)),
+            pltpu.SemaphoreType.DMA((80,)),
+        ],
         compiler_params=pltpu.CompilerParams(
-            collective_id=1, has_side_effects=True, vmem_limit_bytes=63 * 2**20
+            collective_id=0, has_side_effects=True, vmem_limit_bytes=63 * 2**20
         ),
-        cost_estimate=pl.CostEstimate(flops=6 * 10**10, bytes_accessed=2 * 10**8, transcendentals=0),
-    )(tokens, *kept, cols, decay, rowdoc, passing)
-    return outs[:10]
+        cost_estimate=pl.CostEstimate(flops=8 * 10**10, bytes_accessed=3 * 10**8, transcendentals=0),
+    )(tokens, *weights, dy, cols, decay, rowdoc, passing)
+    return outs[: len(results)]
 
 
 def prepare(doc_starts, length):
@@ -1521,13 +1547,9 @@
 
 
 def local_box(tokens, doc_starts, wq, wk, wv, wg, wo, fv, fg, fo, cotangent):
-    tok, width = tokens.shape[1:]
-    tables = prepare(doc_starts, WIDE * tok)
-    kept = list(
-        forward(tokens[0], (wq, wk, wv, wg, wo, fv, fg, fo), cotangent[0], *tables)
-    )
-    kept[3] = kept[3].reshape(WIDE, tok, width)
-    outs = backward(tokens[0], kept, *tables)
+    tables = prepare(doc_starts, WIDE * tokens.shape[1])
+    weights = (wq, wk, wv, wg, wo, fv, fg, fo)
+    outs = layer(tokens[0], weights, cotangent[0], *tables)
     return (outs[0][None], outs[1][None]) + tuple(outs[2:])
 
 

time: 557 us -> 519 us (0.932)
  Pallas kernels: 534 us -> 499 us
    pallas_call x2 -> x1, Pallas kernels: 534 us -> 499 us  [layer(): pl.pallas_call(layer_kernel, out_shape=out_shape, in_specs=[ANY] * 12 + [...]
where the time goes in v5:
time: 519 us; the launch traced here: 516 us
  Pallas kernels  499 us (96%)
  local copies, waits for them, and re-layouts  14.1 us (3%)
    pallas_call x1, Pallas kernels, layer(): pl.pallas_call(layer_kernel, out_shape=out_shape, in_specs=[ANY] * 12 + [...  499 us
    unnamed x41, local copies, waits for them, and re-layouts  11.9 us

profile of v5, /device:TPU:0, one launch (start us, length us, event | category | flops | bytes accessed | tf_op | source)
XLA Modules:
  0.0 515.7 jit_solution(3988653970926263085)
XLA Ops:
  0.6 0.0 copy-start
  0.7 0.7 copy-done
  1.3 0.1 convert_reduce_fusion.2
  1.4 0.1 multiply_exponential_fusion.3
  1.6 0.1 multiply_exponential_fusion.2
  1.6 0.1 convert_reduce_fusion
  1.8 0.0 copy-start.11
  1.8 0.2 convert_reduce_fusion.1
  2.0 0.1 broadcast_multiply_fusion.2
  2.1 0.1 mul.144
  2.1 0.7 broadcast_in_dim.6.passing
  2.8 0.1 broadcast_bitcast_fusion.3
  2.9 0.1 broadcast_bitcast_fusion.2
  3.1 0.1 subtract_maximum_fusion
  3.2 0.9 multiply_exponential_fusion.decay_in
  4.1 0.4 copy.23
  4.5 1.0 pad.4.cols_in
  5.5 0.0 copy-done.11
  5.5 499.1 %shard_map.186 = (bf16[256,2048]{1,0:T(8,128)(2,1)}, f32[256,2048]{1,0:T(8,128)}, f32[64,2048]{1,0:T(8,128)}, f32[64,2048]{1,0:T(8,128)}, f32[64,2048]{1,0:T(8,1...) custom-call(bf16[256,2048]{1,0:T(8,128)(2,1)} %bitcast.30, ...), custom_call_target="tpu_custom_call" | custom-call | flops 80000000000 | bytes 300000000 | tf_op jit(solution)/shard_map/pallas_call | solution.py:1500
  504.6 0.0 copy-start.2
  504.6 0.0 copy-start.10
  504.6 2.5 copy.38
  507.1 0.0 copy-done.2
  507.1 0.0 copy-start.9
  507.1 0.0 copy-start.8
  507.1 0.0 copy-start.7
  507.1 1.3 copy.39
  508.4 0.0 copy-done.10
  508.4 0.0 copy-start.6
  508.4 0.0 copy-start.5
  508.4 0.8 copy.40
  509.2 0.0 copy-done.9
  509.2 0.8 copy.41
  510.0 0.0 copy-done.8
  510.0 0.0 copy-start.4
  510.0 0.8 copy.42
  510.8 0.0 copy-done.7
  510.8 0.8 copy.43
  511.6 0.0 copy-done.6
  511.6 0.0 copy-start.3
  511.6 0.8 copy.44
  512.4 0.0 copy-done.5
  512.4 1.1 copy.45
  513.5 0.0 copy-done.4
  513.5 1.1 copy.46
  514.6 0.0 copy-done.3
  514.6 1.1 copy.47
  515.7 0.0 copy-done.1
  (18 shorter events, 0.2 us)
Async XLA Ops:
  0.6 0.7 copy-start
  1.8 3.8 copy-start.11
  504.6 2.5 copy-start.2
  504.6 3.8 copy-start.10
  507.1 2.1 copy-start.9
  507.1 2.9 copy-start.8
  507.1 3.7 copy-start.7
  508.4 3.2 copy-start.6
  508.4 4.0 copy-start.5
  510.0 3.5 copy-start.4
  511.6 3.0 copy-start.3
  512.4 3.3 copy-start.1

commit v6 on v5

--- a/solution.py
+++ b/solution.py
@@ -364,10 +364,12 @@
             self.wait(self.links.far)
             self.copy(4).start()
 
-    def finish(self, then=lambda place: None):
+    def finish(self, then=lambda place: None, late=lambda: None):
         k = self.links
         then(0)
         for place, index in enumerate((k.pair, k.cross, k.far)):
+            if place == 2:
+                late()
             pl.when(k.mid == 0)(lambda index=index: self.wait(index))
             then(place + 1)
 
@@ -516,26 +518,15 @@
     def wait(self, slot):
         self.links.arrived(self.land(slot), self.base + slot)
 
-    def forward(self, add):
+    def pass_on(self, index, add):
         k = self.links
+        which, slot = ((k.far, 0), (k.cross, 1), (k.pair, 3))[index]
 
         @pl.when(k.mid == 1)
         def _():
-            self.wait(0)
-            add(self.part(k.far), self.land(0))
-            self.copy(0).start()
-            self.wait(1)
-            add(self.part(k.cross), self.land(1))
-            self.copy(1).start()
-
-    def forward_near(self, add):
-        k = self.links
-
-        @pl.when(k.mid == 1)
-        def _():
-            self.wait(3)
-            add(self.part(k.pair), self.land(3))
-            self.copy(2).start()
+            self.wait(slot)
+            add(self.part(which), self.land(slot))
+            self.copy(index).start()
 
     def finish(self, fetch, spots):
         k = self.links
@@ -559,9 +550,9 @@
 
 
 class PlaneSum:
-    def __init__(self, links, block, corner, near, half):
+    def __init__(self, links, block, corner, near, half, base=None):
         self.links, self.block, self.corner, self.near, self.half = links, block, corner, near, half
-        self.base = links.take(6)
+        self.base = links.take(6) if base is None else base
 
     def rows(self, h):
         return pl.ds(h * self.half, self.half)
@@ -614,7 +605,7 @@
     gate_in, mixed_in, x1_in, x1n_in,
     corner, near, twin_fo_land, twin_ff, twin_wo, twin_xn_land, land_fo, land_ff, land_wo, land_qk,
     turn_ff, turn_qk, a_land, g_land,
-    g_fo, g_fv, g_fg, stage, acc, tmp, tmp_ff,
+    g_fo, g_fv, g_fg, stage, acc, tmp, own_res, tmp_ff,
     send, recv, here,
 ):
     k = Links(send, recv, here)
@@ -657,10 +648,11 @@
         LineSum(k, lambda i, g=g: g.at[:, i], lambda s, m=m: land_ff.at[m, s])
         for m, g in enumerate((g_fv, g_fg))
     ]
-    def plane_sum(m, blocks):
-        return PlaneSum(k, lambda q: blocks.at[q], corner.at[m], near.at[m], half)
-
-    plane_mid, plane_res, plane_in = (plane_sum(m, stage) for m in (0, 1, 3))
+    def plane_sum(m, blocks, base=None):
+        return PlaneSum(k, lambda q: blocks.at[q], corner.at[m], near.at[m], half, base)
+
+    plane_mid, plane_in = (plane_sum(m, stage) for m in (0, 3))
+    base_res = k.take(6)
     twin_base = k.take(4 * 5)
 
     def twin(m, j, src, dst):
@@ -717,23 +709,44 @@
     )
 
     k.greet()
-    own_out = k.keep(wo, wo_in.at[w, n])
-    own_in = [
-        k.keep(weight.at[:, wide_cols(w)], to.at[w, n, :, pl.ds((m % 2) * two, two)])
-        for m, (weight, to) in enumerate(projections)
-    ]
-    own_ff = [
-        k.keep(fv.at[:, chip_cols(chip)], fv_in.at[chip, core, n]),
-        k.keep(fg.at[:, chip_cols(chip)], fg_in.at[chip, core, n]),
-        k.keep(fo, fo_in.at[core, n]),
-        k.keep(dy_arg, dy_in.at[chip]),
-    ]
-
     def before(
         x, xn, wqk, wvg, wout, slope, qkv, gates, sin, state, attn_s, attn, gate, mixed, x1, x1n,
         cols, decay,
     ):
-        k.keep(x_in, x).wait()
+        load_x = k.keep(x_in, x)
+        held = [
+            (k.keep(wo, mixed.at[pl.ds(0, 64)]), mixed.at[pl.ds(0, 64)], wo_in.at[w, n]),
+            *[
+                (
+                    k.keep(weight.at[:, wide_cols(w)], spot.at[w, n, :, lanes]),
+                    spot.at[w, n, :, lanes],
+                    to.at[w, n, :, lanes],
+                )
+                for weight, spot, to, lanes in (
+                    (wq, wqk, wqk_in, pl.ds(0, two)),
+                    (wk, wqk, wqk_in, pl.ds(two, two)),
+                    (wv, wvg, wvg_in, pl.ds(0, two)),
+                    (wg, wvg, wvg_in, pl.ds(two, two)),
+                )
+            ],
+            (k.keep(dy_arg, attn), attn, dy_in.at[chip]),
+            *[
+                (
+                    k.keep(weight.at[:, chip_cols(chip)], tmp_ff.at[m]),
+                    tmp_ff.at[m],
+                    to.at[chip, core, n],
+                )
+                for m, (weight, to) in enumerate(((fv, fv_in), (fg, fg_in)))
+            ],
+            (k.keep(fo, gate.at[pl.ds(0, fo_rows)]), gate.at[pl.ds(0, fo_rows)], fo_in.at[core, n]),
+        ]
+
+        def place(index):
+            load, spot, to = held[index]
+            load.wait()
+            return k.keep(spot, to)
+
+        load_x.wait()
 
         def norm_in(rows):
             v = x[rows, :].astype(F32)
@@ -741,25 +754,27 @@
 
         row_chunks(tok, norm_in)
         own_xn = k.keep(x1n, xn_in.at[w])
+        own_in = [place(i) for i in range(5)]
         load_cols, load_decay = k.keep(cols_in, cols), k.keep(decay_in, decay)
         k.met()
-        own_out.wait()
-        line_out.start()
         for spread in spreads:
             spread.start()
+        own_in[0].wait()
+        line_out.start()
         own_xn.wait()
-        plane_xn.start()
-        twin_xn.send(0)
-        for spread in spread_ff:
-            spread.start()
-        for copy in own_in:
+        for copy in own_in[1:]:
             copy.wait()
         spreads[0].finish()
         spreads[1].finish()
         line_qk.start()
+        plane_xn.start()
+        twin_xn.send(0)
         spreads[2].finish()
         spreads[3].finish()
         line_vg.start()
+        for spread in spread_ff:
+            spread.start()
+        own_ff = [place(i) for i in range(5, 9)]
         line_out.forward()
         plane_xn.forward()
         line_out.forward_far()
@@ -922,21 +937,32 @@
     )
 
     def ffn(x1n, dy, fvw, fgw, fow, mix, val, gat, side):
+        def shares(moved, src, dst, places):
+            copies = []
+            for i in places:
+                moved.wait(i)
+                copies.append(k.keep(src.at[:, :, near4[i]], dst.at[:, :, near4[i]]))
+            return copies
+
+        def fo_shares(places):
+            copies = []
+            for i in places:
+                twin_fo.wait(i)
+                copies.append(k.keep(fo_in.at[:, near4[i]], fow.at[:, near4[i]]))
+            return copies
+
         line_fv.finish(twin_fv.send)
+        load_fv = shares(twin_fv, fv_in, fvw, range(4))
         plane_x1n.finish_near()
         plane_x1n.finish_far()
         load_x1n = k.keep(x1n_in, x1n)
-        for i in range(4):
-            twin_fv.wait(i)
-        load_fv = k.keep(fv_in, fvw)
         line_fo.forward()
-        line_fg.finish(twin_fg.send)
+        load_fg = []
+        line_fg.finish(twin_fg.send, lambda: load_fg.extend(shares(twin_fg, fg_in, fgw, range(3))))
         line_fo.start_home()
-        for i in range(4):
-            twin_fg.wait(i)
-        load_fg = k.keep(fg_in, fgw)
+        load_fg += shares(twin_fg, fg_in, fgw, range(3, 4))
         plane_dy.forward()
-        for copy in (load_x1n, load_fv, load_fg):
+        for copy in (load_x1n, *load_fv, *load_fg):
             copy.wait()
 
         def up(j, carry):
@@ -949,11 +975,10 @@
 
         lax.fori_loop(0, CHIPS // 2, up, 0)
         line_fo.forward_far()
+        lax.fori_loop(CHIPS // 2, CHIPS, up, 0)
         plane_dy.finish_near()
         plane_dy.finish_far()
-        load_dy = k.keep(dy_in, dy)
-        lax.fori_loop(CHIPS // 2, CHIPS, up, 0)
-        load_dy.wait()
+        k.keep(dy_in, dy).wait()
 
         def fo_grad(j, carry):
             chunk = lax.rem(j + 2 * other, chunks)
@@ -970,16 +995,23 @@
         for i in range(NARROW):
             twin(0, i, fo_part(other, i), twin_fo_land.at[i]).start()
         lax.fori_loop(4, chunks, fo_grad, 0)
+        came = []
         for i in range(NARROW):
             copy = twin(0, i, fo_part(other, i), twin_fo_land.at[i])
             copy.wait_recv()
-            add_fo(fo_part(core, i), twin_fo_land.at[i])
+            spot = stage.at[i, pl.ds(0, fo_rows)]
+            came.append((copy, k.keep(twin_fo_land.at[i], spot), spot))
+        for i, (copy, load, spot) in enumerate(came):
+            load.wait()
+            own = fo_part(core, i)
+            own[...] = (own[...].astype(F32) + spot[...].astype(F32)).astype(BF)
             copy.wait_send()
         sum_fo.start()
-        line_fo.finish(twin_fo.send)
-        for i in range(4):
-            twin_fo.wait(i)
-        k.keep(fo_in, fow).wait()
+        load_fo = []
+        line_fo.finish(twin_fo.send, lambda: load_fo.extend(fo_shares(range(3))))
+        load_fo += fo_shares(range(3, 4))
+        for copy in load_fo:
+            copy.wait()
 
         def down(q, carry):
             d_mix = dot_rt(dy[q], fow[...].reshape(ff, width))
@@ -990,6 +1022,17 @@
             return carry
 
         lax.fori_loop(0, CHIPS, down, 0)
+
+        plane_res = plane_sum(1, dy, base_res)
+
+        def out_step(j, carry):
+            q = nth(j)
+            dy[q] = dot(mix[q], fow[...].reshape(ff, width)).astype(BF)
+            for step, push in enumerate((plane_res.send_far, plane_res.send_x, plane_res.send_y)):
+                pl.when(j == step)(push)
+            return carry
+
+        lax.fori_loop(0, CHIPS, out_step, 0)
 
         def back(j, carry):
             q = nth(j)
@@ -1046,17 +1089,14 @@
             if m == 0:
                 lax.fori_loop(0, CHIPS, back, 0)
                 plane_mid.combine(add_half)
-                sum_fo.forward(add_fo)
-
-        sum_fo.forward_near(add_fo)
+                plane_res.combine(add_half)
+                sum_fo.pass_on(0, add_fo)
+                sum_fo.pass_on(1, add_fo)
+
+        sum_fo.pass_on(2, add_fo)
+        own_res[...] = dy[chip]
         plane_mid.drain()
-
-        def out_step(j, carry):
-            q = nth(j)
-            stage[q] = dot(mix[q], fow[...].reshape(ff, width)).astype(BF)
-            return carry
-
-        lax.fori_loop(0, CHIPS, out_step, 0)
+        plane_res.drain()
 
     pl.run_scoped(
         ffn,
@@ -1071,9 +1111,8 @@
         pltpu.VMEM((2, *g_fv.shape[1:]), BF),
     )
 
-    def rest(d_x1, d_branch, mixed, da_src, dg_src, side, stage_wo, own_res, g_wo, g_qk, g_vg):
+    def rest(d_x1, d_branch, mixed, da_src, dg_src, side, stage_wo, g_wo, g_qk, g_vg):
         plane_out = plane_sum(2, stage_wo)
-        own_res[...] = stage[chip]
         sum_wo = LineSum(k, lambda i: g_wo.at[i], lambda s: land_wo.at[s])
         sum_qk = [
             LineSum(k, lambda i, g=g: g.at[:, i], lambda s, m=m: land_qk.at[m, s])
@@ -1131,9 +1170,6 @@
             row_chunks(tok, attn_back)
             spread_a.start()
             spread_g.start()
-            plane_res.send_far()
-            plane_res.send_x()
-            plane_res.send_y()
             own = [
                 k.keep(da_src.at[:, at(w * two, two)], a_land.at[w]),
                 k.keep(dg_src.at[:, at(w * two, two)], g_land.at[at(w * tok, tok)]),
@@ -1192,7 +1228,8 @@
             stage_wo,
             lambda owner: dot_lt(mixed[:, at(owner * tok, tok)], d_branch[...]),
         )
-        sum_ff[0].forward(add_ff)
+        sum_ff[0].pass_on(0, add_ff)
+        sum_ff[0].pass_on(1, add_ff)
 
         def attention(xn, d_qk, d_vg, state):
             state[...] = jnp.zeros_like(state)
@@ -1239,7 +1276,7 @@
                     return carry
 
                 lax.fori_loop(0, WIDE, step, 0)
-                sum_ff[0].forward_near(add_ff)
+                sum_ff[0].pass_on(2, add_ff)
                 spread_g.finish()
                 load_g = k.keep(g_land, d_vg.at[:, pl.ds(two, two)])
                 load_g.wait()
@@ -1265,10 +1302,9 @@
                 lax.fori_loop(0, WIDE, in_grad, 0)
                 sum_qk[m].start()
 
-            plane_res.combine(add_half)
             plane_out.combine(add_half)
-            sum_ff[1].forward(add_ff)
-            plane_res.drain()
+            sum_ff[1].pass_on(0, add_ff)
+            sum_ff[1].pass_on(1, add_ff)
             g_wo[...] = acc[...].astype(BF).reshape(g_wo.shape)
 
             def spread_in(wqk, wvg):
@@ -1300,7 +1336,9 @@
             add_qk = adder(tmp_qk)
             load_x, load_x1 = k.keep(x_in, x), k.keep(x1_in, x1)
             plane_in.combine(add_half)
-            sum_ff[1].forward_near(add_ff)
+            sum_ff[1].pass_on(2, add_ff)
+            sum_qk[0].pass_on(0, add_qk)
+            sum_qk[0].pass_on(1, add_qk)
             plane_out.finish()
             fetch(near.at[2], pair)
             for i in range(NARROW):
@@ -1325,7 +1363,7 @@
                 )
                 turn.start()
                 ff_turns.append((turn, k.keep(ff_src.at[m, chip], turn_ff.at[m, chip])))
-            sum_qk[0].forward(add_qk)
+            sum_qk[0].pass_on(2, add_qk)
             sum_fo.finish(fetch, three.at[:, pl.ds(0, fo_rows)])
             own = fo_part(core, n)
             for r in range(0, fo_rows, 16):
@@ -1333,7 +1371,7 @@
                 w_fo[rows, :] = total(own[rows, :], three[:, rows, :])
             stores = [k.keep(w_fo, gfo_o)]
 
-            plane_res.finish()
+            plane_sum(1, stage, base_res).finish()
             fetch(near.at[1], pair)
             load_x1.wait()
 
@@ -1344,8 +1382,8 @@
 
             row_chunks(tok, add_up)
             stores.append(k.keep(own_res, result_o))
-            sum_qk[1].forward(add_qk)
-            sum_qk[0].forward_near(add_qk)
+            sum_qk[1].pass_on(0, add_qk)
+            sum_qk[1].pass_on(1, add_qk)
             load_x.wait()
             plane_in.finish()
             fetch(near.at[3], pair)
@@ -1368,10 +1406,12 @@
                 for q in range(CHIPS):
                     ff_f32[m, :, q * ff : (q + 1) * ff] = ff_all[q].astype(F32)
                 stores.append(k.keep(ff_f32.at[m], (gfv_o, gfg_o)[m]))
-            sum_wo.forward(add_wo)
-            sum_qk[1].forward_near(add_qk)
             qk_turns = []
             for m, g_in in enumerate((g_qk, g_vg)):
+                if m == 1:
+                    sum_qk[1].pass_on(2, add_qk)
+                    sum_wo.pass_on(0, add_wo)
+                    sum_wo.pass_on(1, add_wo)
                 sum_qk[m].finish(fetch, three_qk)
                 for s in range(WIDE):
                     qk_src[m, s] = total(g_in[s, n], three_qk[:, s]).astype(BF)
@@ -1382,11 +1422,7 @@
                 )
                 turn.start()
                 qk_turns.append((turn, k.keep(qk_src.at[m, w], turn_qk.at[m, w])))
-                if m == 0:
-                    sum_wo.forward_near(add_wo)
-            sum_wo.finish(fetch, three.at[:, pl.ds(0, 64)])
-            w_f32[4] = total(g_wo[n], three[:, 0:64, :])
-            stores.append(k.keep(w_f32.at[4], go_o))
+            sum_wo.pass_on(2, add_wo)
             for m, (turn, copy) in enumerate(qk_turns):
                 turn.finish()
                 copy.wait()
@@ -1398,6 +1434,9 @@
                 outs = ((gq_o, gk_o), (gv_o, gg_o))[m]
                 stores.append(k.keep(w_f32.at[2 * m], outs[0]))
                 stores.append(k.keep(w_f32.at[2 * m + 1], outs[1]))
+            sum_wo.finish(fetch, three.at[:, pl.ds(0, 64)])
+            w_f32[4] = total(g_wo[n], three[:, 0:64, :])
+            stores.append(k.keep(w_f32.at[4], go_o))
             for copy in stores:
                 copy.wait()
             plane_in.drain()
@@ -1435,7 +1474,6 @@
         pltpu.VMEM((tok, width), BF),
         pltpu.VMEM((CHIPS, tok, width), BF),
         pltpu.VMEM((CHIPS, tok, width), BF),
-        pltpu.VMEM((tok, width), BF),
         pltpu.VMEM((NARROW, 64, width), BF),
         pltpu.VMEM((WIDE, NARROW, 64, 2 * two), BF),
         pltpu.VMEM((WIDE, NARROW, 64, 2 * two), BF),
@@ -1509,10 +1547,11 @@
             pltpu.VMEM((CHIPS, tok, width), BF),
             pltpu.VMEM((tok, width), F32),
             pltpu.VMEM((tok, width), BF),
+            pltpu.VMEM((tok, width), BF),
             pltpu.VMEM((CHIPS, shard, ff), BF),
             pltpu.SemaphoreType.DMA((272,)),
             pltpu.SemaphoreType.DMA((272,)),
-            pltpu.SemaphoreType.DMA((80,)),
+            pltpu.SemaphoreType.DMA((96,)),
         ],
         compiler_params=pltpu.CompilerParams(
             collective_id=0, has_side_effects=True, vmem_limit_bytes=63 * 2**20

time: 519 us -> 484 us (0.933)
  Pallas kernels: 499 us -> 464 us
    pallas_call x1, Pallas kernels: 499 us -> 464 us  [layer(): pl.pallas_call(layer_kernel, out_shape=out_shape, in_specs=[ANY] * 12 + [...]
where the time goes in v6:
time: 484 us; the launch traced here: 481 us
  Pallas kernels  464 us (96%)
  local copies, waits for them, and re-layouts  14.1 us (3%)
    pallas_call x1, Pallas kernels, layer(): pl.pallas_call(layer_kernel, out_shape=out_shape, in_specs=[ANY] * 12 + [...  464 us
    unnamed x41, local copies, waits for them, and re-layouts  11.9 us

profile of v6, /device:TPU:0, one launch (start us, length us, event | category | flops | bytes accessed | tf_op | source)
XLA Modules:
  0.0 480.9 jit_solution(40883634868877204)
XLA Ops:
  0.6 0.0 copy-start
  0.7 0.7 copy-done
  1.3 0.1 convert_reduce_fusion.2
  1.4 0.1 multiply_exponential_fusion.3
  1.6 0.1 multiply_exponential_fusion.2
  1.6 0.1 convert_reduce_fusion
  1.8 0.0 copy-start.11
  1.8 0.2 convert_reduce_fusion.1
  2.0 0.1 broadcast_multiply_fusion.2
  2.1 0.1 mul.144
  2.1 0.7 broadcast_in_dim.6.passing
  2.8 0.1 broadcast_bitcast_fusion.3
  2.9 0.1 broadcast_bitcast_fusion.2
  3.1 0.1 subtract_maximum_fusion
  3.2 0.9 multiply_exponential_fusion.decay_in
  4.1 0.4 copy.23
  4.5 1.0 pad.4.cols_in
  5.5 0.0 copy-done.11
  5.5 464.2 %shard_map.186 = (bf16[256,2048]{1,0:T(8,128)(2,1)}, f32[256,2048]{1,0:T(8,128)}, f32[64,2048]{1,0:T(8,128)}, f32[64,2048]{1,0:T(8,128)}, f32[64,2048]{1,0:T(8,1...) custom-call(bf16[256,2048]{1,0:T(8,128)(2,1)} %bitcast.30, ...), custom_call_target="tpu_custom_call" | custom-call | flops 80000000000 | bytes 300000000 | tf_op jit(solution)/shard_map/pallas_call | solution.py:1538
  469.8 0.0 copy-start.2
  469.8 0.0 copy-start.10
  469.8 2.5 copy.38
  472.2 0.0 copy-done.2
  472.2 0.0 copy-start.9
  472.2 0.0 copy-start.8
  472.2 0.0 copy-start.7
  472.3 1.3 copy.39
  473.6 0.0 copy-done.10
  473.6 0.0 copy-start.6
  473.6 0.8 copy.40
  474.4 0.0 copy-done.9
  474.4 0.8 copy.41
  475.2 0.0 copy-done.8
  475.2 0.0 copy-start.4
  475.2 0.8 copy.42
  476.0 0.0 copy-done.7
  476.0 0.8 copy.43
  476.8 0.0 copy-done.6
  476.8 0.0 copy-start.3
  476.8 0.8 copy.44
  477.6 0.0 copy-done.5
  477.6 0.0 copy-start.1
  477.6 1.1 copy.45
  478.7 0.0 copy-done.4
  478.7 1.1 copy.46
  479.8 0.0 copy-done.3
  479.8 1.1 copy.47
  480.9 0.0 copy-done.1
  (18 shorter events, 0.2 us)
Async XLA Ops:
  0.6 0.7 copy-start
  1.8 3.8 copy-start.11
  469.8 2.5 copy-start.2
  469.8 3.8 copy-start.10
  472.2 2.1 copy-start.9
  472.2 2.9 copy-start.8
  472.2 3.7 copy-start.7
  473.6 3.2 copy-start.6
  473.6 4.0 copy-start.5
  475.2 3.5 copy-start.4
  476.8 3.0 copy-start.3
  477.6 3.3 copy-start.1
